TPU v7x, 32 devices: a whole 2x2x4 slice. The times are simulated.
32 devices in a mesh: azim: 4 (over z), rad: 4 (over x, core), axial: 2 (over y).
Axes of the slice: x: 2, y: 2, z: 4, core: 2. Of those that a mesh axis runs over, the one named last changes fastest.
Arguments:
- residual: float32 [5, 128, 64, 256], P(None, 'azim', 'rad', 'axial'), may hold values from -12 to 12
- left_vec: float32 [5, 5], replicated, may hold values from -2.5 to 2.5
- dissip: float32 [5], replicated, may hold values from 0.2 to 0.5
- azim_coef: float32 [4, 5, 128], replicated, may hold values from 0 to 1, as said below
- radial_coef: float32 [2, 5, 64], replicated, may hold values from 0 to 3328
Outputs:
- update: float32 [5, 128, 64, 256], P(None, 'azim', 'rad', 'axial')
Inputs may be any that keep to these rules, and one draw needn't show every extreme that they name: `azim_coef`: at every position a and b are positive with a + b < 1, and so are c and e with c + e < 1.
All inputs are finite; a program needn't handle non-finite values.
Results may differ from a plain program's by a relative error of at most 0.0003.
Values sent between devices are 32-bit elements; how exact they have to be, the bound alone decides.
No kernel may reach another device: no remote copies, remote signals or barrier semaphores. Data moves between devices by JAX's collectives and lax.ppermute only.
A program may use at most 64 MiB of HBM per device.

v0:
```python
import jax
import jax.numpy as jnp
from jax import lax
from jax.sharding import PartitionSpec as P

exact_mode = lax.Precision.HIGHEST


def with_halo(cells, sides, width):
    for axis, dim in sides:
        count = lax.axis_size(axis)
        ends = count - 1
        head = lax.slice_in_dim(cells, 0, width, axis=dim)
        tail = lax.slice_in_dim(cells, cells.shape[dim] - width, cells.shape[dim], axis=dim)
        cells = jnp.concatenate(
            [
                lax.ppermute(tail, axis, [(i, (i + 1) % count) for i in range(ends)]),
                cells,
                lax.ppermute(head, axis, [((i + 1) % count, i) for i in range(ends)]),
            ],
            axis=dim,
        )
    return cells


def apply_map(linear_map, states):
    return jnp.einsum("fkm,fmrx->fkrx", linear_map, states, precision=exact_mode)


def compose(earlier, later):
    earlier_map, earlier_state = earlier
    later_map, later_state = later
    joined_map = jnp.einsum("fkm,fmn->fkn", later_map, earlier_map, precision=exact_mode)
    return (joined_map, apply_map(later_map, earlier_state) + later_state)


def state_step(running, element):
    return (compose(running, element), running)


def lower_inverse(first_blocks, second_blocks):
    group_len = first_blocks.shape[-1]
    identity = jnp.eye(group_len, dtype=jnp.float32)
    start = jnp.zeros(first_blocks.shape, jnp.float32)

    def row_step(carry, inputs):
        prev_one, prev_two = carry
        first_now, second_now, unit_row = inputs
        row = unit_row + first_now[..., None] * prev_one + second_now[..., None] * prev_two
        return ((row, prev_one), row)

    inputs = (jnp.moveaxis(first_blocks, -1, 0), jnp.moveaxis(second_blocks, -1, 0), identity)
    _, rows = lax.scan(row_step, (start, start), inputs)
    return jnp.moveaxis(rows, 0, -2)


def group_tables(first_coef, second_coef, ndevices, group_len):
    fields = first_coef.shape[0]
    first_blocks = jnp.transpose(first_coef.reshape(fields, ndevices, group_len), (1, 0, 2))
    second_blocks = jnp.transpose(second_coef.reshape(fields, ndevices, group_len), (1, 0, 2))
    inverses = lower_inverse(first_blocks, second_blocks)
    entry_col = (
        inverses[..., :, 0] * first_blocks[..., 0:1] + inverses[..., :, 1] * second_blocks[..., 1:2]
    )
    second_col = inverses[..., :, 0] * second_blocks[..., 0:1]
    coupling = jnp.stack([entry_col, second_col], axis=-1)
    group_maps = jnp.stack(
        [coupling[..., group_len - 1, :], coupling[..., group_len - 2, :]], axis=-2
    )
    return (inverses, coupling, group_maps)


def sweep(source, first_coef, second_coef, reverse):
    fields, group_len = (source.shape[0], source.shape[1])
    ndevices = lax.axis_size("azim")
    if reverse:
        source = jnp.flip(source, 1)
        first_coef = jnp.flip(first_coef, 1)
        second_coef = jnp.flip(second_coef, 1)
        own_index = ndevices - 1 - lax.axis_index("azim")
    else:
        own_index = lax.axis_index("azim")
    weights = jnp.sqrt(1.0 - (first_coef + second_coef) ** 2)
    own_weights = lax.dynamic_index_in_dim(
        weights.reshape(fields, ndevices, group_len), own_index, 1, keepdims=False
    )
    inverses, coupling, group_maps = group_tables(first_coef, second_coef, ndevices, group_len)
    own_inverse = lax.dynamic_index_in_dim(inverses, own_index, 0, keepdims=False)
    own_coupling = lax.dynamic_index_in_dim(coupling, own_index, 0, keepdims=False)
    own_map = lax.dynamic_index_in_dim(group_maps, own_index, 0, keepdims=False)
    local_part = jnp.einsum(
        "fij,fjrx->firx", own_inverse, source * own_weights[:, :, None, None], precision=exact_mode
    )
    own_state = jnp.stack([local_part[:, group_len - 1], local_part[:, group_len - 2]], axis=1)
    identity_map = jnp.broadcast_to(jnp.eye(2, dtype=jnp.float32), own_map.shape)
    gathered = lax.all_gather(own_state[None], "azim", axis=0, tiled=True)
    if reverse:
        gathered = jnp.flip(gathered, 0)
    totals, prefixes = lax.scan(
        state_step, (identity_map, jnp.zeros_like(own_state)), (group_maps, gathered)
    )
    total_map, total_state = totals
    enter_map = lax.dynamic_index_in_dim(prefixes[0], own_index, 0, keepdims=False)
    enter_state = lax.dynamic_index_in_dim(prefixes[1], own_index, 0, keepdims=False)
    loop_matrix = jnp.eye(2, dtype=jnp.float32)[None] - total_map
    determinant = (
        loop_matrix[:, 0, 0] * loop_matrix[:, 1, 1] - loop_matrix[:, 0, 1] * loop_matrix[:, 1, 0]
    )
    adjugate = jnp.stack(
        [
            jnp.stack([loop_matrix[:, 1, 1], -loop_matrix[:, 0, 1]], -1),
            jnp.stack([-loop_matrix[:, 1, 0], loop_matrix[:, 0, 0]], -1),
        ],
        -2,
    )
    start_state = apply_map(adjugate / determinant[:, None, None], total_state)
    entering = apply_map(enter_map, start_state) + enter_state
    result = local_part + jnp.einsum("fim,fmrx->firx", own_coupling, entering, precision=exact_mode)
    if reverse:
        result = jnp.flip(result, 1)
    return result


def band_inverse(below, middle, above):
    order = middle.shape[-1]
    unit = jnp.broadcast_to(jnp.eye(order, dtype=jnp.float32), middle.shape + (order,))
    return lax.linalg.tridiagonal_solve(below, middle, above, unit)


def local(residual, left_vec, dissip, azim_coef, radial_coef):
    characteristic = jnp.einsum("gf,farx->garx", left_vec, residual, precision=exact_mode)
    padded = with_halo(characteristic, (("axial", 3),), 1)
    source = characteristic + dissip[:, None, None, None] * (
        padded[..., 2:] + padded[..., :-2] - 2.0 * characteristic
    )
    lower_out = sweep(source, azim_coef[0], azim_coef[1], False)
    upper_out = sweep(lower_out, azim_coef[2], azim_coef[3], True)
    lower_rad = radial_coef[0]
    upper_rad = radial_coef[1]
    diagonal = 1.0 + lower_rad + upper_rad
    row_scale = diagonal**0.25
    below_diag = jnp.concatenate([jnp.zeros_like(lower_rad[:, :1]), -lower_rad[:, 1:]], axis=1)
    above_diag = jnp.concatenate([-upper_rad[:, :-1], jnp.zeros_like(upper_rad[:, :1])], axis=1)
    line_inverse = band_inverse(below_diag, diagonal, above_diag) * row_scale[:, None, :]
    return lax.all_to_all(
        jnp.einsum(
            "fij,fajx->faix",
            line_inverse,
            lax.all_to_all(upper_out, "rad", split_axis=1, concat_axis=2, tiled=True),
            precision=exact_mode,
        ),
        "rad",
        split_axis=2,
        concat_axis=1,
        tiled=True,
    )


def solution(mesh):
    placed = (P(None, "azim", "rad", "axial"), P(), P(), P(), P())
    return jax.shard_map(
        local,
        mesh=mesh,
        in_specs=placed,
        out_specs=P(None, "azim", "rad", "axial"),
        check_vma=False,
    )
```

profile of v0, /device:TPU:0, one launch (start us, length us, event | category | flops | bytes accessed | tf_op | source)
XLA Modules:
  0.0 353.0 jit_solution(4023763067698190563)
XLA Ops:
  1.3 3.3 fusion.11
  4.6 2.8 fusion.267
  7.3 2.9 copy.244
  10.2 5.6 %collective-permute-start.1 = (f32[5,32,16,1]{1,2,3,0:T(8,128)}, f32[5,32,16,1]{1,2,3,0:T(8,128)}, u32[]{:S(2)}, u32[]{:S(2)}) collective-permute-start(f32[5,32,16,1]{1,2,3,0:T(8,128)} %copy.244), channel_id=1, source_target_pairs={{0,1},{2,3},{4,5},{6,7},{8,9},{10,11},{12,13},{14,15},{16,17},{18,... | collective-permute-start | bytes 30728 | tf_op jit(solution)/shard_map/ppermute | solution.py:17
  15.8 2.9 copy.242
  23.1 84.3 %while.77 = (s32[]{:T(128)}, f32[4,5,32]{2,1,0:T(8,128)S(1)}, f32[4,5,32]{2,1,0:T(8,128)S(1)}, f32[32,4,5,32]{3,2,1,0:T(8,128)}, f32[32,32]{1,0:T(8,128)S(1)}, /...) while((s32[]{:T(128)}, f32[4,5,32]{2,1,0:T(8,128)S(1)}, ...), condition=%wide.region_3.4_spmd.clone, body=%wide.region_2.3_spmd.clone.sunk | while | flops 3203 | bytes 27995 | solution.py:53
  107.4 2.0 copy.248
  126.2 1.7 slice_bitcast_fusion.83
  133.7 65.3 %while.76 = (s32[]{:T(128)}, f32[4,5,32]{2,1,0:T(8,128)S(1)}, f32[4,5,32]{2,1,0:T(8,128)S(1)}, f32[32,4,5,32]{3,2,1,0:T(8,128)}, f32[32,32]{1,0:T(8,128)}, /*ind...) while((s32[]{:T(128)}, f32[4,5,32]{2,1,0:T(8,128)S(1)}, ...), condition=%wide.region_1.2_spmd.clone, body=%wide.region_0.1_spmd.clone.sunk | while | flops 3203 | bytes 27611 | solution.py:53
  199.0 2.0 copy.262
  208.3 1.8 fusion.130
  212.1 3.4 subtract_bitcast_fusion
  226.4 2.0 copy.237
  230.5 3.6 %copy.245 = f32[5,32,16,1]{3,0,2,1:T(8,128)} copy(f32[5,32,16,1]{1,2,3,0:T(8,128)} %collective-permute-done.1) | data formatting | bytes 20480 | tf_op jit(solution)/shard_map/ppermute | solution.py:17
  234.1 3.6 %copy.243 = f32[5,32,16,1]{3,0,2,1:T(8,128)} copy(f32[5,32,16,1]{1,2,3,0:T(8,128)} %collective-permute-done) | data formatting | bytes 20480 | tf_op jit(solution)/shard_map/ppermute | solution.py:19
  237.7 3.9 %fusion.10 = f32[5,32,16,128]{3,0,2,1:T(8,128)S(1)} fusion(f32[5,32,16,128]{3,0,2,1:T(8,128)S(1)} %fusion.11, f32[5,32,16,1]{3,0,2,1:T(8,128)} %copy.245, f32[5,32,16,1]{3,0,2,1:T(8,128)} %copy.243, f32[5,32]{0,1:T(8,128)S(1)} %bitcast.2008, f32[5]{0:T(128)} %param.15), kind=kLoop, calls=%fused_computation.35 | loop fusion | flops 2621440 | bytes 2642580 | tf_op jit(solution)/shard_map/mul | solution.py:92
  241.7 2.9 fusion.13
  244.7 14.5 %all-gather = f32[20,2,16,128]{3,2,1,0:T(8,128)S(1)} all-gather(f32[5,2,16,128]{3,2,1,0:T(8,128)S(1)} %copy.257), channel_id=2, replica_groups=mesh['azim'=4,'rad'=4,'axial'=2] {'azim'}, dimensions={0}, use_global_device_ids=true | all-gather | bytes 409600 | tf_op jit(solution)/shard_map/all_gather | solution.py:96
  260.2 6.6 %while.78 = (s32[]{:T(128)}, f32[5,2,2]{2,1,0:T(2,128)S(1)}, f32[5,2,16,128]{3,1,2,0:T(2,128)S(1)}, f32[4,5,2,2]{1,3,2,0:T(2,128)S(1)}, f32[4,5,2,16,128]{4,2,3,...) while((s32[]{:T(128)}, f32[5,2,2]{2,1,0:T(2,128)S(1)}, ...), condition=%wide.region_5.6_spmd.clone, body=%wide.region_4.5_spmd.clone.sunk | while | flops 553443 | bytes 742624 | solution.py:99
  269.0 2.3 convolution_add_fusion.3
  271.3 3.1 rev.20
  274.4 2.6 fusion.15
  277.2 15.0 %all-gather.1 = f32[20,2,16,128]{3,2,1,0:T(8,128)S(1)} all-gather(f32[5,2,16,128]{3,2,1,0:T(8,128)S(1)} %copy.271), channel_id=3, replica_groups=mesh['azim'=4,'rad'=4,'axial'=2] {'azim'}, dimensions={0}, use_global_device_ids=true | all-gather | bytes 409600 | tf_op jit(solution)/shard_map/all_gather | solution.py:96
  293.3 7.6 %while.79 = (s32[]{:T(128)}, f32[5,2,2]{2,1,0:T(2,128)S(1)}, f32[5,2,16,128]{3,1,2,0:T(2,128)S(1)}, f32[4,5,2,2]{1,3,2,0:T(2,128)S(1)}, f32[4,5,2,16,128]{4,2,3,...) while((s32[]{:T(128)}, f32[5,2,2]{2,1,0:T(2,128)S(1)}, ...), condition=%wide.region_7.8_spmd.clone, body=%wide.region_6.7_spmd.clone.sunk | while | flops 553443 | bytes 578784 | solution.py:99
  302.2 2.3 convolution_add_fusion.2
  304.5 2.2 rev.22
  306.7 1.8 copy.276
  308.9 3.8 %all-to-all-start = ((f32[5,32,16,128]{3,2,0,1:T(8,128)}), f32[5,32,16,128]{3,2,0,1:T(8,128)S(1)}, u32[]{:S(2)}, u32[]{:S(2)}) async-start(f32[5,32,16,128]{3,2,0,1:T(8,128)} %copy.276), calls=%async_computation | async-start | bytes 2621440 | tf_op jit(solution)/shard_map/all_to_all | solution.py:149
  315.6 2.1 subtract_divide_fusion.64
  317.8 2.6 multiply_subtract_fusion.20
  320.7 9.0 %all-to-all-done = f32[5,32,16,128]{3,2,0,1:T(8,128)S(1)} async-done(((f32[5,32,16,128]{3,2,0,1:T(8,128)}), f32[5,32,16,128]{3,2,0,1:T(8,128)S(1)}, u32[]{:S(2)}, u32[]{:S(2)}) %all-to-all-start) | async-done | bytes 1310752 | tf_op jit(solution)/shard_map/all_to_all | solution.py:149
  332.0 19.7 %all_to_all.36 = f32[5,8,64,128]{3,1,0,2:T(8,128)S(1)} all-to-all(f32[5,8,64,128]{3,1,0,2:T(8,128)S(1)} %copy.302), channel_id=1, replica_groups=mesh['azim'=4,'rad'=4,'axial'=2] {'rad'}, dimensions={2} | all-to-all | bytes 2621440 | tf_op jit(solution)/shard_map/all_to_all | solution.py:145
  (614 shorter events, 225.2 us)
Async XLA Ops:
  10.2 220.3 %collective-permute-start.1 = (f32[5,32,16,1]{1,2,3,0:T(8,128)}, f32[5,32,16,1]{1,2,3,0:T(8,128)}, u32[]{:S(2)}, u32[]{:S(2)}) collective-permute-start(f32[5,32,16,1]{1,2,3,0:T(8,128)} %copy.244), channel_id=1, source_target_pairs={{0,1},{2,3},{4,5},{6,7},{8,9},{10,11},{12,13},{14,15},{16,17},{18,... | collective-permute-start | bytes 30728 | tf_op jit(solution)/shard_map/ppermute | solution.py:17
  18.7 215.4 %collective-permute-start = (f32[5,32,16,1]{1,2,3,0:T(8,128)}, f32[5,32,16,1]{1,2,3,0:T(8,128)}, u32[]{:S(2)}, u32[]{:S(2)}) collective-permute-start(f32[5,32,16,1]{1,2,3,0:T(8,128)} %copy.242), channel_id=1, source_target_pairs={{1,0},{3,2},{5,4},{7,6},{9,8},{11,10},{13,12},{15,14},{17,16},{19,... | collective-permute-start | bytes 30728 | tf_op jit(solution)/shard_map/ppermute | solution.py:19
  113.1 20.6 %copy-start.6 = (f32[5,4,32]{2,1,0:T(4,128)}, f32[5,4,32]{2,1,0:T(4,128)S(1)}, u32[]{:S(2)}) copy-start(f32[5,4,32]{2,1,0:T(4,128)S(1)} %reshape.191661) | copy-start | bytes 7684
  113.2 19.0 %copy-start.4 = (f32[5,4,32]{2,1,0:T(4,128)}, f32[5,4,32]{2,1,0:T(4,128)S(1)}, u32[]{:S(2)}) copy-start(f32[5,4,32]{2,1,0:T(4,128)S(1)} %reshape.191662) | copy-start | bytes 7684
  132.9 77.6 %copy-start.30 = (f32[64]{0:T(128)S(1)}, f32[64]{0:T(128)}, u32[]{:S(2)}) copy-start(f32[64]{0:T(128)} %get-tuple-element.831) | copy-start | bytes 772
  199.0 17.9 %copy-start.25 = (f32[4,5,1,2]{1,0,3,2:T(4,128)S(1)}, f32[4,5,1,2]{1,0,3,2:T(4,128)}, u32[]{:S(2)}) copy-start(f32[4,5,1,2]{1,0,3,2:T(4,128)} %copy.256) | copy-start | bytes 484
  199.0 17.9 %copy-start.26 = (f32[4,5,1,2]{1,0,3,2:T(4,128)S(1)}, f32[4,5,1,2]{1,0,3,2:T(4,128)}, u32[]{:S(2)}) copy-start(f32[4,5,1,2]{1,0,3,2:T(4,128)} %copy.255) | copy-start | bytes 484
  208.3 17.2 %copy-start.1 = (f32[32,4,5,32]{3,2,1,0:T(8,128)S(1)}, f32[32,4,5,32]{3,2,1,0:T(8,128)}, u32[]{:S(2)}) copy-start(f32[32,4,5,32]{3,2,1,0:T(8,128)} %get-tuple-element.202) | copy-start | bytes 245764
  210.1 14.5 %copy-start.42 = (f32[5,1]{0,1:T(1,128)}, f32[5,1]{0,1:T(1,128)S(1)}, u32[]{:S(2)}) copy-start(f32[5,1]{0,1:T(1,128)S(1)} %get-tuple-element.543) | copy-start | bytes 64
  210.1 14.5 %copy-start.44 = (f32[5,1]{0,1:T(1,128)}, f32[5,1]{0,1:T(1,128)S(1)}, u32[]{:S(2)}) copy-start(f32[5,1]{0,1:T(1,128)S(1)} %get-tuple-element.545) | copy-start | bytes 64
  210.1 14.5 %copy-start.46 = (f32[5,1]{0,1:T(1,128)}, f32[5,1]{0,1:T(1,128)S(1)}, u32[]{:S(2)}) copy-start(f32[5,1]{0,1:T(1,128)S(1)} %get-tuple-element.547) | copy-start | bytes 64
  210.1 14.5 %copy-start.48 = (f32[5,1]{0,1:T(1,128)}, f32[5,1]{0,1:T(1,128)S(1)}, u32[]{:S(2)}) copy-start(f32[5,1]{0,1:T(1,128)S(1)} %get-tuple-element.549) | copy-start | bytes 64
  210.1 14.5 %copy-start.50 = (f32[5,1]{0,1:T(1,128)}, f32[5,1]{0,1:T(1,128)S(1)}, u32[]{:S(2)}) copy-start(f32[5,1]{0,1:T(1,128)S(1)} %get-tuple-element.551) | copy-start | bytes 64
  210.1 14.5 %copy-start.52 = (f32[5,1]{0,1:T(1,128)}, f32[5,1]{0,1:T(1,128)S(1)}, u32[]{:S(2)}) copy-start(f32[5,1]{0,1:T(1,128)S(1)} %get-tuple-element.553) | copy-start | bytes 64
  210.1 14.5 %copy-start.54 = (f32[5,1]{0,1:T(1,128)}, f32[5,1]{0,1:T(1,128)S(1)}, u32[]{:S(2)}) copy-start(f32[5,1]{0,1:T(1,128)S(1)} %get-tuple-element.557) | copy-start | bytes 64
  210.1 14.5 %copy-start.56 = (f32[5,1]{0,1:T(1,128)}, f32[5,1]{0,1:T(1,128)S(1)}, u32[]{:S(2)}) copy-start(f32[5,1]{0,1:T(1,128)S(1)} %get-tuple-element.558) | copy-start | bytes 64
  210.2 14.5 %copy-start.58 = (f32[5,1]{0,1:T(1,128)}, f32[5,1]{0,1:T(1,128)S(1)}, u32[]{:S(2)}) copy-start(f32[5,1]{0,1:T(1,128)S(1)} %get-tuple-element.560) | copy-start | bytes 64
  210.2 14.5 %copy-start.60 = (f32[5,1]{0,1:T(1,128)}, f32[5,1]{0,1:T(1,128)S(1)}, u32[]{:S(2)}) copy-start(f32[5,1]{0,1:T(1,128)S(1)} %get-tuple-element.562) | copy-start | bytes 64
  210.2 14.5 %copy-start.62 = (f32[5,1]{0,1:T(1,128)}, f32[5,1]{0,1:T(1,128)S(1)}, u32[]{:S(2)}) copy-start(f32[5,1]{0,1:T(1,128)S(1)} %get-tuple-element.564) | copy-start | bytes 64
  210.2 14.5 %copy-start.64 = (f32[5,1]{0,1:T(1,128)}, f32[5,1]{0,1:T(1,128)S(1)}, u32[]{:S(2)}) copy-start(f32[5,1]{0,1:T(1,128)S(1)} %get-tuple-element.566) | copy-start | bytes 64
  210.2 14.5 %copy-start.66 = (f32[5,1]{0,1:T(1,128)}, f32[5,1]{0,1:T(1,128)S(1)}, u32[]{:S(2)}) copy-start(f32[5,1]{0,1:T(1,128)S(1)} %get-tuple-element.568) | copy-start | bytes 64
  210.2 14.5 %copy-start.68 = (f32[5,1]{0,1:T(1,128)}, f32[5,1]{0,1:T(1,128)S(1)}, u32[]{:S(2)}) copy-start(f32[5,1]{0,1:T(1,128)S(1)} %get-tuple-element.570) | copy-start | bytes 64
  210.2 14.5 %copy-start.70 = (f32[5,1]{0,1:T(1,128)}, f32[5,1]{0,1:T(1,128)S(1)}, u32[]{:S(2)}) copy-start(f32[5,1]{0,1:T(1,128)S(1)} %get-tuple-element.572) | copy-start | bytes 64
  210.2 14.5 %copy-start.72 = (f32[5,1]{0,1:T(1,128)}, f32[5,1]{0,1:T(1,128)S(1)}, u32[]{:S(2)}) copy-start(f32[5,1]{0,1:T(1,128)S(1)} %get-tuple-element.574) | copy-start | bytes 64
  210.2 14.5 %copy-start.74 = (f32[5,1]{0,1:T(1,128)}, f32[5,1]{0,1:T(1,128)S(1)}, u32[]{:S(2)}) copy-start(f32[5,1]{0,1:T(1,128)S(1)} %get-tuple-element.576) | copy-start | bytes 64
  210.4 18.0 %copy-start.28 = (f32[5,1]{0,1:T(1,128)}, f32[5,1]{0,1:T(1,128)S(1)}, u32[]{:S(2)}) copy-start(f32[5,1]{0,1:T(1,128)S(1)} %get-tuple-element.617) | copy-start | bytes 64
  210.4 18.0 %copy-start.36 = (f32[5,1]{0,1:T(1,128)}, f32[5,1]{0,1:T(1,128)S(1)}, u32[]{:S(2)}) copy-start(f32[5,1]{0,1:T(1,128)S(1)} %get-tuple-element.537) | copy-start | bytes 64
  210.4 18.0 %copy-start.38 = (f32[5,1]{0,1:T(1,128)}, f32[5,1]{0,1:T(1,128)S(1)}, u32[]{:S(2)}) copy-start(f32[5,1]{0,1:T(1,128)S(1)} %get-tuple-element.539) | copy-start | bytes 64
  210.4 18.0 %copy-start.40 = (f32[5,1]{0,1:T(1,128)}, f32[5,1]{0,1:T(1,128)S(1)}, u32[]{:S(2)}) copy-start(f32[5,1]{0,1:T(1,128)S(1)} %get-tuple-element.541) | copy-start | bytes 64
  241.7 17.6 %copy-start.27 = (f32[2,2]{1,0:T(2,128)S(1)}, f32[2,2]{1,0:T(2,128)}, u32[]{:S(2)}) copy-start(f32[2,2]{1,0:T(2,128)} %compare_convert_fusion) | copy-start | bytes 52
  241.7 18.5 %copy-start.2 = (f32[5,2,16,128]{3,1,2,0:T(2,128)S(1)}, f32[5,2,16,128]{3,1,2,0:T(2,128)}, u32[]{:S(2)}) copy-start(f32[5,2,16,128]{3,1,2,0:T(2,128)} %custom-call.2) | copy-start | bytes 245764
  308.9 20.8 %all-to-all-start = ((f32[5,32,16,128]{3,2,0,1:T(8,128)}), f32[5,32,16,128]{3,2,0,1:T(8,128)S(1)}, u32[]{:S(2)}, u32[]{:S(2)}) async-start(f32[5,32,16,128]{3,2,0,1:T(8,128)} %copy.276), calls=%async_computation | async-start | bytes 2621440 | tf_op jit(solution)/shard_map/all_to_all | solution.py:149
  (66 other events, 540.6 us)
where the time goes:
time: 358 us; the launch traced here: 353 us
  local copies, waits for them, and re-layouts  151 us (42%)
  other arithmetic  105 us (29%)
  blocking collectives  49.2 us (14%)
  matrix products  25.3 us (7%)
  starting transfers between devices  10.7 us (3%)
  waiting for transfers between devices  9.01 us (3%)
    dynamic_update_slice x64, other arithmetic, lower_inverse(): _, rows = lax.scan(row_step, (start, start), inputs)  65.4 us
    mul x64, local copies, waits for them, and re-layouts, row_step(): second_now[..., None] * prev_two  43.2 us
    add x64, local copies, waits for them, and re-layouts, row_step(): unit_row + first_now[..., None] * prev_one  41 us
    all_gather x2, blocking collectives, sweep(): gathered = lax.all_gather(own_state[None], 'azim', axis=0, tiled=True)  29.5 us
    all_to_all x1, blocking collectives, local(): lax.all_to_all(jnp.einsum('fij,fajx->faix', line_inverse, lax.all_to_all(...  19.7 us
    broadcast_in_dim x10, other arithmetic, band_inverse(): return lax.linalg.tridiagonal_solve(below, middle, above, unit)  13.8 us
    dot_general x12, matrix products, apply_map(): jnp.einsum('fkm,fmrx->fkrx', linear_map, states, precision=exact_mode)  9.34 us
    all_to_all x1, waiting for transfers between devices, local(): lax.all_to_all(upper_out, 'rad', split_axis=1, concat_axis=2, tiled=True)  9 us
  transfers between devices with their start and end apart: 3, of which 1 were waited for; matrix products, arithmetic and copies ran while one was open for 63% of the time, Pallas kernels for 0%

commit v1 on v0

v1 whole, which is shorter than its diff:
```python
import functools

import jax
import jax.numpy as jnp
from jax import lax
from jax.experimental import pallas as pl
from jax.experimental.pallas import tpu as pltpu
from jax.sharding import PartitionSpec as P

f32 = jnp.float32
VMEM = pl.BlockSpec(memory_space=pltpu.VMEM)
SMEM = pl.BlockSpec(memory_space=pltpu.SMEM)
params = pltpu.CompilerParams(vmem_limit_bytes=32 * 1024 * 1024)


def call(body, outs, n_smem, n_vmem, scratch=(), cost=None):
    return pl.pallas_call(
        body,
        out_shape=[jax.ShapeDtypeStruct(shape, f32) for shape in outs],
        in_specs=[SMEM] * n_smem + [VMEM] * n_vmem,
        out_specs=[VMEM] * len(outs),
        scratch_shapes=[pltpu.VMEM(shape, f32) for shape in scratch],
        compiler_params=params,
        cost_estimate=cost,
    )


def lanes_of(shape):
    return lax.broadcasted_iota(jnp.int32, shape, len(shape) - 1)


def edge_kernel(res_ref, edge_ref):
    fields, cells, rows, width = res_ref.shape
    source = jnp.where(lax.axis_index("axial") == 0, width - 1, 0)
    lane = lanes_of((rows, width))

    def step(j, packed):
        return tuple(
            jnp.where(lane == j, pltpu.roll(res_ref[f, j], (j - source + width) % width, 1), packed[f])
            for f in range(fields)
        )

    edge_ref[...] = jnp.zeros(edge_ref.shape, f32)
    packed = lax.fori_loop(0, cells, step, tuple(edge_ref[f] for f in range(fields)), unroll=4)
    for f in range(fields):
        edge_ref[f] = packed[f]


def first_kernel(coef_ref, vec_ref, dis_ref, res_ref, halo_ref, src_ref, state_ref, z_ref):
    fields, cells, rows, width = res_ref.shape
    tile = (rows, width)
    lane = lanes_of(tile)
    target = jnp.where(lax.axis_index("axial") == 0, width - 1, 0)
    vec = [[vec_ref[g * fields + f] for f in range(fields)] for g in range(fields)]
    dis = [dis_ref[g] for g in range(fields)]

    def mix(values):
        return [sum(vec[g][f] * values[f] for f in range(fields)) for g in range(fields)]

    halo = [dis[g] * h for g, h in enumerate(mix([halo_ref[f] for f in range(fields)]))]

    def coef(kind, f, j):
        return coef_ref[(kind * fields + f) * cells + j]

    def down(j, carry):
        chars = mix([res_ref[f, j] for f in range(fields)])
        out = []
        for f in range(fields):
            one, two = carry[f]
            c = chars[f]
            beside = jnp.where(lane == 0, 0.0, pltpu.roll(c, 1, 1)) + jnp.where(
                lane == width - 1, 0.0, pltpu.roll(c, width - 1, 1)
            )
            src = (1.0 - 2.0 * dis[f]) * c + dis[f] * beside
            src = src + jnp.where(
                lane == target, pltpu.roll(halo[f], (target - j + width) % width, 1), 0.0
            )
            src_ref[f, j] = src
            z = coef(2, f, j) * src + coef(1, f, j) * two + coef(0, f, j) * one
            z_ref[f, j] = z
            out.append((z, one))
        return tuple(out)

    state_ref[...] = jnp.zeros(state_ref.shape, f32)
    start = tuple((state_ref[f, 0], state_ref[f, 1]) for f in range(fields))
    carry = lax.fori_loop(0, cells, down, start, unroll=2)
    for f in range(fields):
        state_ref[f, 0], state_ref[f, 1] = carry[f]

    def up(i, carry):
        j = cells - 1 - i
        out = []
        for f in range(fields):
            one, two = carry[f]
            v = coef(5, f, j) * z_ref[f, j] + coef(4, f, j) * two + coef(3, f, j) * one
            out.append((v, one))
        return tuple(out)

    start = tuple((state_ref[f, 2], state_ref[f, 3]) for f in range(fields))
    carry = lax.fori_loop(0, cells, up, start, unroll=4)
    for f in range(fields):
        state_ref[f, 2], state_ref[f, 3] = carry[f]


def second_kernel(coef_ref, enter_ref, rad_ref, *refs):
    states, (src_ref, line_ref, end_ref, z_ref) = refs[:-4], refs[-4:]
    fields, cells, rows, width = src_ref.shape
    tile = (rows, width)
    slots = 4 * len(states)

    def coef(kind, f, j):
        return coef_ref[(kind * fields + f) * cells + j]

    entry = []
    for f in range(fields):
        sums = []
        for m in range(4):
            total = jnp.zeros(tile, f32)
            for k in range(slots):
                total = total + enter_ref[(m * slots + k) * fields + f] * states[k // 4][f, k % 4]
            sums.append(total)
        entry.append(sums)

    def down(j, carry):
        out = []
        for f in range(fields):
            one, two = carry[f]
            z = coef(2, f, j) * src_ref[f, j] + coef(1, f, j) * two + coef(0, f, j) * one
            z_ref[f, j] = z
            out.append((z, one))
        return tuple(out)

    lax.fori_loop(0, cells, down, tuple((e[0], e[1]) for e in entry), unroll=4)

    def up(i, carry):
        j = cells - 1 - i
        out = []
        for f in range(fields):
            one, two = carry[f]
            v = coef(5, f, j) * z_ref[f, j] + coef(4, f, j) * two + coef(3, f, j) * one
            line_ref[pl.ds(f * rows * cells + j, rows, stride=cells)] = v
            out.append((v, one))
        return tuple(out)

    lax.fori_loop(0, cells, up, tuple((e[2], e[3]) for e in entry), unroll=4)

    for f in range(fields):
        ahead = jnp.zeros((cells, width), f32)
        held = []
        for i in range(rows):
            line = line_ref[pl.ds((f * rows + i) * cells, cells)]
            ahead = rad_ref[(0 * fields + f) * rows + i] * line + rad_ref[(fields + f) * rows + i] * ahead
            held.append(ahead)
        end_ref[f, 0] = ahead
        back = jnp.zeros((cells, width), f32)
        for i in reversed(range(rows)):
            back = rad_ref[(2 * fields + f) * rows + i] * held[i] + rad_ref[(3 * fields + f) * rows + i] * back
        end_ref[f, 1] = back


def third_kernel(enter_ref, rad_ref, *refs):
    ends, (line_ref, out_ref) = refs[:-2], refs[-2:]
    fields, _, cells, width = ends[0].shape
    rows = line_ref.shape[0] // (fields * cells)
    slots = 2 * len(ends)
    for f in range(fields):
        entry = []
        for m in range(2):
            total = jnp.zeros((cells, width), f32)
            for k in range(slots):
                total = total + enter_ref[(m * slots + k) * fields + f] * ends[k // 2][f, k % 2]
            entry.append(total)
        ahead, back = entry
        held = []
        for i in range(rows):
            line = line_ref[pl.ds((f * rows + i) * cells, cells)]
            ahead = rad_ref[(0 * fields + f) * rows + i] * line + rad_ref[(fields + f) * rows + i] * ahead
            held.append(ahead)
        for i in reversed(range(rows)):
            back = rad_ref[(2 * fields + f) * rows + i] * held[i] + rad_ref[(3 * fields + f) * rows + i] * back
            out_ref[pl.ds(f * rows * cells + i, cells, stride=rows)] = back


def azim_table_kernel(coef_ref, enter_ref):
    _, blocks, cells, fields = coef_ref.shape
    own = lax.axis_index("azim")
    unit = lax.broadcasted_iota(jnp.int32, (blocks, 8, fields), 1)

    def ones(k):
        return (unit == k).astype(f32)

    one, two = ones(0), ones(1)
    held = []
    for j in range(cells):
        z = coef_ref[0, :, j : j + 1] * one + coef_ref[1, :, j : j + 1] * two
        held.append(z)
        one, two = z, one
    lower = (one, two)
    one, two = ones(2), ones(3)
    for j in reversed(range(cells)):
        c, e = coef_ref[2, :, j : j + 1], coef_ref[3, :, j : j + 1]
        v = jnp.sqrt(1.0 - (c + e) * (c + e)) * held[j] + c * one + e * two
        one, two = v, one
    upper = (one, two)

    def entry(pair, p, m, k):
        return pair[m][p, k : k + 1]

    count = 4 * blocks
    height = -(-(count + 2) // 8) * 8
    row = lax.broadcasted_iota(jnp.int32, (height, fields), 0)

    def slot(p, k):
        return (row == 4 * (p ^ own) + k).astype(f32)

    def through(order, pair, first, source, start):
        state, entering = start, {}
        for p in order:
            entering[p] = state
            state = tuple(
                source(p, m) + entry(pair, p, m, first) * state[0] + entry(pair, p, m, first + 1) * state[1]
                for m in range(2)
            )
        return state, entering

    def closed(order, pair, first, source):
        start = tuple((row == count + k).astype(f32) for k in range(2))
        (total_one, total_two), _ = through(order, pair, first, source, start)
        a = 1.0 - total_one[count : count + 1]
        b = total_one[count + 1 : count + 2]
        c = total_two[count : count + 1]
        d = 1.0 - total_two[count + 1 : count + 2]
        scale = 1.0 / (a * d - b * c)
        live = row < count
        total_one, total_two = jnp.where(live, total_one, 0.0), jnp.where(live, total_two, 0.0)
        start = ((d * total_one + b * total_two) * scale, (c * total_one + a * total_two) * scale)
        return through(order, pair, first, source, start)[1]

    lower_in = closed(range(blocks), lower, 0, slot)

    def upper_source(p, m):
        z_one, z_two = lower_in[p]
        return slot(p, 2 + m) + entry(upper, p, m, 0) * z_one + entry(upper, p, m, 1) * z_two

    upper_in = closed(list(reversed(range(blocks))), upper, 2, upper_source)
    for m in range(4):
        picked = jnp.zeros((height, fields), f32)
        for p in range(blocks):
            value = lower_in[p][m] if m < 2 else upper_in[p][m - 2]
            picked = jnp.where(own == p, value, picked)
        enter_ref[m] = picked[:count]


def rad_table_kernel(coef_ref, own_ref, enter_ref, pivot_ref):
    _, cells, fields = coef_ref.shape
    rows = own_ref.shape[1]
    blocks = cells // rows
    own = lax.axis_index("rad")
    total = 1.0 + coef_ref[0, 0:1]
    for i in range(cells):
        pivot = coef_ref[1, i : i + 1] + total
        pivot_ref[1 + i : 2 + i] = pivot
        if i + 1 < cells:
            total = 1.0 + coef_ref[0, i + 1 : i + 2] * (total / pivot)
    pivot_ref[0:1] = jnp.ones((1, fields), f32)
    lower, upper = coef_ref[0], coef_ref[1]
    first = lax.broadcasted_iota(jnp.int32, (cells, fields), 0) == 0
    scale = jnp.sqrt(jnp.sqrt(1.0 + lower + upper))
    inverse = 1.0 / pivot_ref[1 : cells + 1]
    forward = jnp.where(first, 0.0, lower / pivot_ref[0:cells])
    backward = upper * inverse
    for kind, table in enumerate((scale, forward, inverse, backward)):
        picked = jnp.zeros((rows, fields), f32)
        for p in range(blocks):
            picked = jnp.where(own == p, table[p * rows : (p + 1) * rows], picked)
        own_ref[kind] = picked

    maps = []
    for p in range(blocks):
        lines = [slice(p * rows + i, p * rows + i + 1) for i in range(rows)]
        ahead, held = jnp.ones((1, fields), f32), []
        for line in lines:
            ahead = forward[line] * ahead
            held.append(ahead)
        back, gain = jnp.zeros((1, fields), f32), jnp.ones((1, fields), f32)
        for line, value in zip(reversed(lines), reversed(held)):
            back = inverse[line] * value + backward[line] * back
            gain = backward[line] * gain
        maps.append((ahead, back, gain))
    count = 2 * blocks
    height = -(-count // 8) * 8
    row = lax.broadcasted_iota(jnp.int32, (height, fields), 0)

    def slot(p, k):
        return (row == 2 * (p ^ own) + k).astype(f32)

    zero = jnp.zeros((height, fields), f32)
    ahead, ahead_in = zero, {}
    for p in range(blocks):
        ahead_in[p] = ahead
        ahead = slot(p, 0) + maps[p][0] * ahead
    back, back_in = zero, {}
    for p in reversed(range(blocks)):
        back_in[p] = back
        back = slot(p, 1) + maps[p][1] * ahead_in[p] + maps[p][2] * back
    for m, entering in enumerate((ahead_in, back_in)):
        picked = zero
        for p in range(blocks):
            picked = jnp.where(own == p, entering[p], picked)
        enter_ref[m] = picked[:count]


def from_partners(values, axis):
    count = lax.axis_size(axis)
    return [values] + [
        lax.ppermute(values, axis, [(i, i ^ s) for i in range(count)]) for s in range(1, count)
    ]


def local(residual, left_vec, dissip, azim_coef, radial_coef):
    fields, cells, rows, width = residual.shape
    azim_count, rad_count = lax.axis_size("azim"), lax.axis_size("rad")
    edge = call(edge_kernel, [(fields, rows, width)], 0, 1)(residual)[0]
    halo = lax.ppermute(edge, "axial", [(0, 1), (1, 0)])

    weights = jnp.sqrt(1.0 - (azim_coef[0::2] + azim_coef[1::2]) ** 2)
    kinds = jnp.concatenate([azim_coef[:2], weights[:1], azim_coef[2:], weights[1:]])
    own_azim = lax.dynamic_slice_in_dim(kinds, lax.axis_index("azim") * cells, cells, 2).reshape(-1)
    azim_blocks = azim_coef.reshape(4, fields, azim_count, cells).transpose(0, 2, 3, 1)
    azim_enter = call(azim_table_kernel, [(4, 4 * azim_count, fields)], 0, 1)(azim_blocks)[0].reshape(-1)
    all_rows = rad_count * rows
    own_rad, rad_enter = call(
        rad_table_kernel,
        [(4, rows, fields), (2, 2 * rad_count, fields)],
        0,
        1,
        [(all_rows + 8, fields)],
    )(radial_coef.transpose(0, 2, 1))
    own_rad, rad_enter = own_rad.transpose(0, 2, 1).reshape(-1), rad_enter.reshape(-1)

    whole = (fields, cells, rows, width)
    src, states = call(first_kernel, [whole, (fields, 4, rows, width)], 3, 2, [whole])(
        own_azim, left_vec.reshape(-1), dissip, residual, halo
    )
    gathered = from_partners(states, "azim")
    flat = (fields * cells * rows, width)
    lines, ends = call(second_kernel, [flat, (fields, 2, cells, width)], 3, 1 + azim_count, [whole])(
        own_azim, azim_enter, own_rad, *gathered, src
    )
    gathered = from_partners(ends, "rad")
    out = call(third_kernel, [flat], 2, 1 + rad_count)(rad_enter, own_rad, *gathered, lines)[0]
    return out.reshape(whole)


def solution(mesh):
    placed = (P(None, "azim", "rad", "axial"), P(), P(), P(), P())
    return jax.shard_map(
        local,
        mesh=mesh,
        in_specs=placed,
        out_specs=P(None, "azim", "rad", "axial"),
        check_vma=False,
    )
```

time: 358 us -> 43 us (0.12); the launches traced: 353 us -> 42.8 us
  local copies, waits for them, and re-layouts: 151 us -> 2.2 us
  other arithmetic: 105 us -> 0.1 us
  blocking collectives: 49.2 us -> 0 us
  matrix products: 25.3 us -> 0 us
  waiting for transfers between devices: 9.01 us -> 20 us
  Pallas kernels: 0 us -> 10.7 us
    dynamic_update_slice x72 -> x0, other arithmetic: 68.3 us -> none  [the longest x64 65.4 us: lower_inverse(): _, rows = lax.scan(row_step, (start, start), inputs)]
    mul x75 -> x0, local copies, waits for them, and re-layouts: 47.1 us -> none  [the longest x64 43.2 us: row_step(): second_now[..., None] * prev_two]
    add x64 -> x0, local copies, waits for them, and re-layouts: 41 us -> none  [row_step(): unit_row + first_now[..., None] * prev_one]
    all_gather x2 -> x0, blocking collectives: 29.5 us -> none  [sweep(): gathered = lax.all_gather(own_state[None], 'azim', axis=0, tiled=True)]
    dot_general x26 -> x0, matrix products: 25.3 us -> none  [the longest x12 9.34 us: apply_map(): jnp.einsum('fkm,fmrx->fkrx', linear_map, states, precision=exact_mode)]
    ppermute x2 -> x7, waiting for transfers between devices: 0.01 us -> 20 us  [the longest x6 18.4 us: from_partners(): lax.ppermute(values, axis, [(i, i ^ s) for i in range(count)])]
    all_to_all x1 -> x0, blocking collectives: 19.7 us -> none  [local(): lax.all_to_all(jnp.einsum('fij,fajx->faix', line_inverse, lax.all_to_all(...]
    slice x19 -> x4, local copies, waits for them, and re-layouts: 16.8 us -> 0.06 us  [the longest x2 0.05 us: local(): weights = jnp.sqrt(1.0 - (azim_coef[0::2] + azim_coef[1::2]) ** 2)]
  transfers between devices with their start and end apart: 3 -> 7, of which waited for: 1 -> 5; matrix products, arithmetic and copies ran while one was open for 63% -> 2% of each run, Pallas kernels for 0% -> 3%
where the time goes in v1:
time: 43 us; the launch traced here: 42.8 us
  waiting for transfers between devices  20 us (47%)
  Pallas kernels  10.7 us (25%)
  starting transfers between devices  9.77 us (23%)
  local copies, waits for them, and re-layouts  2.2 us (5%)
    ppermute x6, waiting for transfers between devices, from_partners(): lax.ppermute(values, axis, [(i, i ^ s) for i in range(count)])  18.4 us
    ppermute x6, starting transfers between devices, from_partners(): lax.ppermute(values, axis, [(i, i ^ s) for i in range(count)])  6.74 us
    pallas_call x1, Pallas kernels, local(): call(first_kernel, [whole, (fields, 4, rows, width)], 3, 2, [whole])  3.36 us
    ppermute x1, starting transfers between devices, local(): halo = lax.ppermute(edge, 'axial', [(0, 1), (1, 0)])  3.03 us
    pallas_call x1, Pallas kernels, local(): call(second_kernel, [flat, (fields, 2, cells, width)], 3, 1 + azim_count,...  3.02 us
    pallas_call x1, Pallas kernels, local(): call(third_kernel, [flat], 2, 1 + rad_count)  2.19 us
    ppermute x1, waiting for transfers between devices, local(): halo = lax.ppermute(edge, 'axial', [(0, 1), (1, 0)])  1.61 us
    unnamed x14, local copies, waits for them, and re-layouts  1.58 us
  transfers between devices with their start and end apart: 7, of which 5 were waited for; matrix products, arithmetic and copies ran while one was open for 2% of the time, Pallas kernels for 3%

profile of v1, /device:TPU:0, one launch (start us, length us, event | category | flops | bytes accessed | tf_op | source)
XLA Modules:
  0.0 42.8 jit_solution(6165031615744360511)
XLA Ops:
  0.0 1.3 %copy-done = f32[5,32,16,128]{3,2,1,0:T(8,128)S(1)} copy-done((f32[5,32,16,128]{3,2,1,0:T(8,128)S(1)}, f32[5,32,16,128]{3,2,1,0:T(8,128)}, u32[]{:S(2)}) %copy-start) | copy-done | bytes 1310744
  1.3 0.0 copy-start.4
  1.3 0.9 %shard_map.57 = f32[5,16,128]{2,1,0:T(8,128)S(1)} custom-call(f32[5,32,16,128]{3,2,1,0:T(8,128)S(1)} %copy-done), custom_call_target="tpu_custom_call" | custom-call | tf_op jit(solution)/shard_map/pallas_call | solution.py:323
  2.3 3.0 %collective-permute-start = (f32[5,16,128]{2,1,0:T(8,128)S(1)}, f32[5,16,128]{2,1,0:T(8,128)S(1)}, u32[]{:S(2)}, u32[]{:S(2)}) collective-permute-start(f32[5,16,128]{2,1,0:T(8,128)S(1)} %shard_map.57), channel_id=1, source_target_pairs={{0,1},{1,0},{2,3},{3,2},{4,5},{5,4},{6,7},{7,6},{8,9},{9,8},{10,11... | collective-permute-start | bytes 122888 | tf_op jit(solution)/shard_map/ppermute | solution.py:324
  5.3 0.0 copy-done.3
  5.4 0.1 dynamic-slice_maximum_fusion
  5.5 0.1 reshape.26.vec_ref
  5.6 0.1 reshape.23.coef_ref
  5.7 1.6 %collective-permute-done.halo_ref = f32[5,16,128]{2,1,0:T(8,128)S(1)} collective-permute-done((f32[5,16,128]{2,1,0:T(8,128)S(1)}, f32[5,16,128]{2,1,0:T(8,128)S(1)}, u32[]{:S(2)}, u32[]{:S(2)}) %collective-permute-start) | collective-permute-done | bytes 40992 | tf_op jit(solution)/shard_map/ppermute | solution.py:324
  7.3 3.4 %shard_map.58 = (f32[5,32,16,128]{3,2,1,0:T(8,128)S(1)}, f32[5,4,16,128]{3,2,1,0:T(8,128)S(1)}) custom-call(f32[960]{0:T(1024)S(1)} %reshape.23.coef_ref, f32[25]{0:T(128)S(1)} %reshape.26.vec_ref, f32[5]{0:T(128)S(1)} %copy-done.2, f32[5,32,16,128]{3,2,1,0:T(8,128)S(1)} %copy-done.1, f32[5,16,128]{2,1,0:T(8,128)S(1)} %collective-permute-done.halo_ref), custom_call_target="tpu_custom_call" | custom-call | tf_op jit(solution)/shard_map/pallas_call | solution.py:342
  10.6 4.2 %collective-permute-start.3 = (f32[5,4,16,128]{3,2,1,0:T(8,128)S(1)}, f32[5,4,16,128]{3,2,1,0:T(8,128)S(1)}, u32[]{:S(2)}, u32[]{:S(2)}) collective-permute-start(f32[5,4,16,128]{3,2,1,0:T(8,128)S(1)} %get-tuple-element.13.refs_0_), channel_id=1, source_target_pairs={{0,24},{8,16},{16,8},{24,0},{1,25},{9,17},{17,9},{25,1},{2,26},{10... | collective-permute-start | bytes 491528 | tf_op jit(solution)/shard_map/ppermute | solution.py:316
  14.8 0.0 collective-permute-start.2
  14.8 0.6 %collective-permute-start.1 = (f32[5,4,16,128]{3,2,1,0:T(8,128)S(1)}, f32[5,4,16,128]{3,2,1,0:T(8,128)S(1)}, u32[]{:S(2)}, u32[]{:S(2)}) collective-permute-start(f32[5,4,16,128]{3,2,1,0:T(8,128)S(1)} %get-tuple-element.13.refs_0_), channel_id=1, source_target_pairs={{0,8},{8,0},{16,24},{24,16},{1,9},{9,1},{17,25},{25,17},{2,10},{10... | collective-permute-start | bytes 491528 | tf_op jit(solution)/shard_map/ppermute | solution.py:316
  15.5 0.1 copy.11
  15.6 0.1 copy.8
  15.7 0.7 %shard_map.55 = (f32[4,16,5]{2,1,0:T(8,128)S(1)}, f32[2,8,5]{2,1,0:T(8,128)S(1)}) custom-call(f32[2,64,5]{2,1,0:T(8,128)S(1)} %bitcast.7), custom_call_target="tpu_custom_call" | custom-call | tf_op jit(solution)/shard_map/pallas_call | solution.py:332
  16.4 0.1 copy.9
  16.5 0.1 reshape.22.rad_ref
  16.6 0.5 %shard_map.56 = f32[4,16,5]{2,1,0:T(8,128)S(1)} custom-call(f32[4,4,32,5]{3,2,1,0:T(8,128)S(1)} %bitcast.6), custom_call_target="tpu_custom_call" | custom-call | tf_op jit(solution)/shard_map/pallas_call | solution.py:330
  17.1 0.1 reshape.25.enter_ref
  17.2 2.7 %collective-permute-done.3.refs_3_ = f32[5,4,16,128]{3,2,1,0:T(8,128)S(1)} collective-permute-done((f32[5,4,16,128]{3,2,1,0:T(8,128)S(1)}, f32[5,4,16,128]{3,2,1,0:T(8,128)S(1)}, u32[]{:S(2)}, u32[]{:S(2)}) %collective-permute-start.3) | collective-permute-done | bytes 163872 | tf_op jit(solution)/shard_map/ppermute | solution.py:316
  19.9 7.6 %collective-permute-done.2.refs_2_ = f32[5,4,16,128]{3,2,1,0:T(8,128)S(1)} collective-permute-done((f32[5,4,16,128]{3,2,1,0:T(8,128)S(1)}, f32[5,4,16,128]{3,2,1,0:T(8,128)S(1)}, u32[]{:S(2)}, u32[]{:S(2)}) %collective-permute-start.2) | collective-permute-done | bytes 163872 | tf_op jit(solution)/shard_map/ppermute | solution.py:316
  27.5 0.0 collective-permute-done.1.refs_1_
  27.6 3.0 %shard_map.59 = (f32[2560,128]{1,0:T(8,128)S(1)}, f32[5,2,32,128]{3,2,1,0:T(8,128)S(1)}) custom-call(f32[960]{0:T(1024)S(1)} %reshape.23.coef_ref, f32[320]{0:T(512)S(1)} %reshape.25.enter_ref, f32[320]{0:T(512)S(1)} %reshape.22.rad_ref, f32[5,4,16,128]{3,2,1,0:T(8,128)S(1)} %get-tuple-element.13.refs_0_, ...), custom_call_target="tpu_custom_call" | custom-call | tf_op jit(solution)/shard_map/pallas_call | solution.py:347
  30.6 0.3 collective-permute-start.6
  30.8 1.4 %collective-permute-start.5 = (f32[5,2,32,128]{3,2,1,0:T(8,128)S(1)}, f32[5,2,32,128]{3,2,1,0:T(8,128)S(1)}, u32[]{:S(2)}, u32[]{:S(2)}) collective-permute-start(f32[5,2,32,128]{3,2,1,0:T(8,128)S(1)} %get-tuple-element.15.refs_0_), channel_id=1, source_target_pairs={{0,4},{2,6},{4,0},{6,2},{1,5},{3,7},{5,1},{7,3},{8,12},{10,14},{12... | collective-permute-start | bytes 491528 | tf_op jit(solution)/shard_map/ppermute | solution.py:316
  32.2 0.3 collective-permute-start.4
  32.5 0.1 reshape.21.enter_ref
  32.6 4.5 %collective-permute-done.6.refs_3_ = f32[5,2,32,128]{3,2,1,0:T(8,128)S(1)} collective-permute-done((f32[5,2,32,128]{3,2,1,0:T(8,128)S(1)}, f32[5,2,32,128]{3,2,1,0:T(8,128)S(1)}, u32[]{:S(2)}, u32[]{:S(2)}) %collective-permute-start.6) | collective-permute-done | bytes 163872 | tf_op jit(solution)/shard_map/ppermute | solution.py:316
  37.1 3.6 %collective-permute-done.5.refs_2_ = f32[5,2,32,128]{3,2,1,0:T(8,128)S(1)} collective-permute-done((f32[5,2,32,128]{3,2,1,0:T(8,128)S(1)}, f32[5,2,32,128]{3,2,1,0:T(8,128)S(1)}, u32[]{:S(2)}, u32[]{:S(2)}) %collective-permute-start.5) | collective-permute-done | bytes 163872 | tf_op jit(solution)/shard_map/ppermute | solution.py:316
  40.7 0.0 collective-permute-done.4.refs_1_
  40.7 2.2 %shard_map.60 = f32[2560,128]{1,0:T(8,128)} custom-call(f32[80]{0:T(128)S(1)} %reshape.21.enter_ref, f32[320]{0:T(512)S(1)} %reshape.22.rad_ref, f32[5,2,32,128]{3,2,1,0:T(8,128)S(1)} %get-tuple-element.15.refs_0_, f32[5,2,32,128]{3,2,1,0:T(8,128)S(1)} %collective-permute-done.4.refs_1_, f32[5,2,32,128]{3,2,1,0:T(8,128)S(1)} %collective-permute-done.5.refs_2_, ...), custom_call_target="tpu_custom_call" | custom-call | tf_op jit(solution)/shard_map/pallas_call | solution.py:351
  (15 shorter events, 0.1 us)
Async XLA Ops:
  0.0 1.3 %copy-start = (f32[5,32,16,128]{3,2,1,0:T(8,128)S(1)}, f32[5,32,16,128]{3,2,1,0:T(8,128)}, u32[]{:S(2)}) copy-start(f32[5,32,16,128]{3,2,1,0:T(8,128)} %res_ref.3) | copy-start | bytes 3932164
  1.3 4.0 %copy-start.3 = (f32[4,5,128]{2,0,1:T(4,128)S(1)}, f32[4,5,128]{2,0,1:T(4,128)}, u32[]{:S(2)}) copy-start(f32[4,5,128]{2,0,1:T(4,128)} %param.8) | copy-start | bytes 30724
  1.3 4.2 %copy-start.5 = (f32[5,5]{1,0:T(8,128)S(1)}, f32[5,5]{1,0:T(8,128)}, u32[]{:S(2)}) copy-start(f32[5,5]{1,0:T(8,128)} %param.6) | copy-start | bytes 304
  1.3 6.0 %copy-start.1 = (f32[5,32,16,128]{3,2,1,0:T(8,128)S(1)}, f32[5,32,16,128]{3,2,1,0:T(8,128)}, u32[]{:S(2)}) copy-start(f32[5,32,16,128]{3,2,1,0:T(8,128)} %res_ref.3) | copy-start | bytes 3932164
  1.3 6.0 %copy-start.2 = (f32[5]{0:T(128)S(1)}, f32[5]{0:T(128)}, u32[]{:S(2)}) copy-start(f32[5]{0:T(128)} %dis_ref.1) | copy-start | bytes 64
  1.3 14.3 %copy-start.4 = (f32[2,5,64]{2,0,1:T(2,128)S(1)}, f32[2,5,64]{2,0,1:T(2,128)}, u32[]{:S(2)}) copy-start(f32[2,5,64]{2,0,1:T(2,128)} %param.9) | copy-start | bytes 7684
  2.3 5.0 %collective-permute-start = (f32[5,16,128]{2,1,0:T(8,128)S(1)}, f32[5,16,128]{2,1,0:T(8,128)S(1)}, u32[]{:S(2)}, u32[]{:S(2)}) collective-permute-start(f32[5,16,128]{2,1,0:T(8,128)S(1)} %shard_map.57), channel_id=1, source_target_pairs={{0,1},{1,0},{2,3},{3,2},{4,5},{5,4},{6,7},{7,6},{8,9},{9,8},{10,11... | collective-permute-start | bytes 122888 | tf_op jit(solution)/shard_map/ppermute | solution.py:324
  10.6 9.3 %collective-permute-start.3 = (f32[5,4,16,128]{3,2,1,0:T(8,128)S(1)}, f32[5,4,16,128]{3,2,1,0:T(8,128)S(1)}, u32[]{:S(2)}, u32[]{:S(2)}) collective-permute-start(f32[5,4,16,128]{3,2,1,0:T(8,128)S(1)} %get-tuple-element.13.refs_0_), channel_id=1, source_target_pairs={{0,24},{8,16},{16,8},{24,0},{1,25},{9,17},{17,9},{25,1},{2,26},{10... | collective-permute-start | bytes 491528 | tf_op jit(solution)/shard_map/ppermute | solution.py:316
  14.8 12.7 %collective-permute-start.2 = (f32[5,4,16,128]{3,2,1,0:T(8,128)S(1)}, f32[5,4,16,128]{3,2,1,0:T(8,128)S(1)}, u32[]{:S(2)}, u32[]{:S(2)}) collective-permute-start(f32[5,4,16,128]{3,2,1,0:T(8,128)S(1)} %get-tuple-element.13.refs_0_), channel_id=1, source_target_pairs={{0,16},{8,24},{16,0},{24,8},{1,17},{9,25},{17,1},{25,9},{2,18},{10... | collective-permute-start | bytes 491528 | tf_op jit(solution)/shard_map/ppermute | solution.py:316
  14.8 12.7 %collective-permute-start.1 = (f32[5,4,16,128]{3,2,1,0:T(8,128)S(1)}, f32[5,4,16,128]{3,2,1,0:T(8,128)S(1)}, u32[]{:S(2)}, u32[]{:S(2)}) collective-permute-start(f32[5,4,16,128]{3,2,1,0:T(8,128)S(1)} %get-tuple-element.13.refs_0_), channel_id=1, source_target_pairs={{0,8},{8,0},{16,24},{24,16},{1,9},{9,1},{17,25},{25,17},{2,10},{10... | collective-permute-start | bytes 491528 | tf_op jit(solution)/shard_map/ppermute | solution.py:316
  30.6 6.5 %collective-permute-start.6 = (f32[5,2,32,128]{3,2,1,0:T(8,128)S(1)}, f32[5,2,32,128]{3,2,1,0:T(8,128)S(1)}, u32[]{:S(2)}, u32[]{:S(2)}) collective-permute-start(f32[5,2,32,128]{3,2,1,0:T(8,128)S(1)} %get-tuple-element.15.refs_0_), channel_id=1, source_target_pairs={{0,6},{2,4},{4,2},{6,0},{1,7},{3,5},{5,3},{7,1},{8,14},{10,12},{12... | collective-permute-start | bytes 491528 | tf_op jit(solution)/shard_map/ppermute | solution.py:316
  30.8 9.8 %collective-permute-start.5 = (f32[5,2,32,128]{3,2,1,0:T(8,128)S(1)}, f32[5,2,32,128]{3,2,1,0:T(8,128)S(1)}, u32[]{:S(2)}, u32[]{:S(2)}) collective-permute-start(f32[5,2,32,128]{3,2,1,0:T(8,128)S(1)} %get-tuple-element.15.refs_0_), channel_id=1, source_target_pairs={{0,4},{2,6},{4,0},{6,2},{1,5},{3,7},{5,1},{7,3},{8,12},{10,14},{12... | collective-permute-start | bytes 491528 | tf_op jit(solution)/shard_map/ppermute | solution.py:316
  32.2 8.4 %collective-permute-start.4 = (f32[5,2,32,128]{3,2,1,0:T(8,128)S(1)}, f32[5,2,32,128]{3,2,1,0:T(8,128)S(1)}, u32[]{:S(2)}, u32[]{:S(2)}) collective-permute-start(f32[5,2,32,128]{3,2,1,0:T(8,128)S(1)} %get-tuple-element.15.refs_0_), channel_id=1, source_target_pairs={{0,2},{2,0},{4,6},{6,4},{1,3},{3,1},{5,7},{7,5},{8,10},{10,8},{12,... | collective-permute-start | bytes 491528 | tf_op jit(solution)/shard_map/ppermute | solution.py:316

commit v2 on v1

v2 whole, which is shorter than its diff:
```python
import jax
import jax.numpy as jnp
from jax import lax
from jax.experimental import pallas as pl
from jax.experimental.pallas import tpu as pltpu
from jax.sharding import PartitionSpec as P

f32 = jnp.float32
VMEM = pl.BlockSpec(memory_space=pltpu.VMEM)
SMEM = pl.BlockSpec(memory_space=pltpu.SMEM)
params = pltpu.CompilerParams(vmem_limit_bytes=32 * 1024 * 1024)


def call(body, outs, n_smem, n_vmem, scratch=()):
    return pl.pallas_call(
        body,
        out_shape=[jax.ShapeDtypeStruct(shape, f32) for shape in outs],
        in_specs=[SMEM] * n_smem + [VMEM] * n_vmem,
        out_specs=[VMEM] * len(outs),
        scratch_shapes=[pltpu.VMEM(shape, f32) for shape in scratch],
        compiler_params=params,
    )


def lanes_of(shape):
    return lax.broadcasted_iota(jnp.int32, shape, len(shape) - 1)


def low_high(count):
    split = 1 << ((count.bit_length() - 1) // 2)
    return list(range(split)), list(range(0, count, split))


def targets_of(count):
    low, high = low_high(count)
    return low + high[1:]


def far_lane(width):
    return jnp.where(lax.axis_index("axial") == 0, width - 1, 0)


def edge_kernel(res_ref, edge_ref):
    fields, cells, rows, width = res_ref.shape
    source = far_lane(width)
    lane = lanes_of((rows, width))

    def step(j, packed):
        return tuple(
            jnp.where(lane == j, pltpu.roll(res_ref[f, j], (j - source + width) % width, 1), packed[f])
            for f in range(fields)
        )

    edge_ref[...] = jnp.zeros(edge_ref.shape, f32)
    packed = lax.fori_loop(0, cells, step, tuple(edge_ref[f] for f in range(fields)), unroll=4)
    for f in range(fields):
        edge_ref[f] = packed[f]


def lower_sweep(coef_ref, cells, load, z_ref, start):
    fields = len(start)

    def step(j, carry):
        source = load(j)
        out = []
        for f in range(fields):
            one, two = carry[f]
            at = f * cells + j
            z = (
                coef_ref[2 * fields * cells + at] * source[f]
                + coef_ref[fields * cells + at] * two
                + coef_ref[at] * one
            )
            z_ref[f, j] = z
            out.append((z, one))
        return tuple(out)

    return lax.fori_loop(0, cells, step, start, unroll=4)


def upper_sweep(coef_ref, cells, z_ref, start, store=None):
    fields = len(start)

    def step(i, carry):
        j = cells - 1 - i
        out = []
        for f in range(fields):
            one, two = carry[f]
            at = f * cells + j
            v = (
                coef_ref[5 * fields * cells + at] * z_ref[f, j]
                + coef_ref[4 * fields * cells + at] * two
                + coef_ref[3 * fields * cells + at] * one
            )
            if store is not None:
                store(f, j, v)
            out.append((v, one))
        return tuple(out)

    return lax.fori_loop(0, cells, step, start, unroll=4)


def radial_sweeps(rad_ref, fields, rows, f, load, ahead, back, store=None):
    def coef(kind, i):
        return rad_ref[(kind * fields + f) * rows + i]

    held = []
    for i in range(rows):
        line = coef(0, i) * load(i)
        ahead = line if ahead is None else line + coef(1, i) * ahead
        held.append(ahead)
    for i in reversed(range(rows)):
        line = coef(2, i) * held[i]
        back = line if back is None else line + coef(3, i) * back
        if store is not None:
            store(i, back)
    return ahead, back


def mix(vec_ref, values):
    fields = len(values)
    return [sum(vec_ref[g * fields + f] * values[f] for f in range(fields)) for g in range(fields)]


def first_kernel(coef_ref, vec_ref, dis_ref, res_ref, src_ref, state_ref, z_ref):
    fields, cells, rows, width = res_ref.shape
    lane = lanes_of((rows, width))

    def load(j):
        out = []
        for f, c in enumerate(mix(vec_ref, [res_ref[f, j] for f in range(fields)])):
            beside = jnp.where(lane == 0, 0.0, pltpu.roll(c, 1, 1)) + jnp.where(
                lane == width - 1, 0.0, pltpu.roll(c, width - 1, 1)
            )
            src = (1.0 - 2.0 * dis_ref[f]) * c + dis_ref[f] * beside
            src_ref[f, j] = src
            out.append(src)
        return out

    state_ref[...] = jnp.zeros(state_ref.shape, f32)
    start = tuple((state_ref[f, 0], state_ref[f, 1]) for f in range(fields))
    carry = lower_sweep(coef_ref, cells, load, z_ref, start)
    for f in range(fields):
        state_ref[f, 0], state_ref[f, 1] = carry[f]
    start = tuple((state_ref[f, 2], state_ref[f, 3]) for f in range(fields))
    carry = upper_sweep(coef_ref, cells, z_ref, start)
    for f in range(fields):
        state_ref[f, 2], state_ref[f, 3] = carry[f]


def patch_kernel(vec_ref, dis_ref, rad_ref, halo_ref, state_ref, reply_ref, out_ref, part_ref, end_ref):
    fields, _, rows, width = state_ref.shape
    lane = lanes_of((rows, width))
    target = far_lane(width)
    for f, h in enumerate(mix(vec_ref, [halo_ref[f] for f in range(fields)])):
        h = dis_ref[f] * h
        part_ref[f] = h
        for m in range(4):
            extra = jnp.sum(h * reply_ref[f, m : m + 1], axis=1, keepdims=True)
            out_ref[pl.ds((f * 4 + m) * rows, rows)] = state_ref[f, m] + jnp.where(lane == target, extra, 0.0)
    for f in range(fields):
        ahead, back = radial_sweeps(
            rad_ref, fields, rows, f, lambda i: out_ref[pl.ds(f * 4 * rows + i, 4, stride=rows)], None, None
        )
        end_ref[f, 0:4] = ahead
        end_ref[f, 4:8] = back


def source_kernel(rad_ref, src_ref, part_ref, out_ref, end_ref):
    fields, cells, rows, width = src_ref.shape
    lane = lanes_of((rows, width))
    target = far_lane(width)

    def step(j, carry):
        for f in range(fields):
            moved = pltpu.roll(part_ref[f], (target - j + width) % width, 1)
            tile = src_ref[f, j] + jnp.where(lane == target, moved, 0.0)
            out_ref[pl.ds(pl.multiple_of((f * cells + j) * rows, rows), rows)] = tile
        return carry

    lax.fori_loop(0, cells, step, 0, unroll=2)
    for f in range(fields):
        end_ref[f, 0], end_ref[f, 1] = radial_sweeps(
            rad_ref, fields, rows, f, lambda i: out_ref[pl.ds(f * cells * rows + i, cells, stride=rows)], None, None
        )


def weighted(enter_ref, fields, f, width, target, m, pieces):
    total = None
    for column, value in pieces:
        term = enter_ref[((target[0] * target[1] + m) * width + column) * fields + f] * value
        total = term if total is None else total + term
    return total


def state_kernel(rad_enter_ref, rad_ref, *refs):
    ends, (state_ref, first_ref, second_ref, work_ref) = refs[:-4], refs[-4:]
    fields, _, half, width = first_ref.shape
    rows = 2 * half
    for f in range(fields):
        pieces = [(2 * s + k, ends[s][f, 4 * k : 4 * k + 4]) for s in range(len(ends)) for k in range(2)]
        ahead, back = (
            weighted(rad_enter_ref, fields, f, 2 * len(ends), (0, 2), m, pieces) for m in range(2)
        )

        def store(i, value):
            work_ref[pl.ds(f * 4 * rows + i, 4, stride=rows)] = value

        radial_sweeps(
            rad_ref, fields, rows, f, lambda i: state_ref[pl.ds(f * 4 * rows + i, 4, stride=rows)], ahead, back, store
        )
        for m in range(4):
            at = (f * 4 + m) * rows
            first_ref[f, m] = work_ref[pl.ds(at, half)]
            second_ref[f, m] = work_ref[pl.ds(at + half, half)]


def spread_kernel(count, size, near, far, enter_ref, *refs):
    arrays, sums = refs[: len(near)], refs[len(near) :]
    fields = sums[0].shape[0]
    for s, out_ref in zip(far, sums):
        target = targets_of(count).index(s)
        for f in range(fields):
            pieces = [(size * n + k, ref[f, k]) for n, ref in zip(near, arrays) for k in range(size)]
            for m in range(size):
                out_ref[f, m] = weighted(enter_ref, fields, f, size * count, (target, size), m, pieces)


def spread_both(count, near, far, enter_ref, *refs):
    ins, outs = refs[: len(near) + len(far)], refs[len(near) + len(far) :]
    spread_kernel(count, 4, near, far, enter_ref, *ins[: len(near)], *outs[: len(far)])
    spread_kernel(count, 4, far, near, enter_ref, *ins[len(near) :], *outs[len(far) :])


def radial_kernel(rad_ref, *refs):
    ends, (src_ref, out_ref) = refs[:-2], refs[-2:]
    fields, _, cells, width = ends[0].shape
    rows = src_ref.shape[0] // (fields * cells)
    for f in range(fields):
        ahead, back = (sum(ref[f, m] for ref in ends) for m in range(2))

        def store(i, value):
            out_ref[pl.ds(f * cells * rows + i, cells, stride=rows)] = value

        radial_sweeps(
            rad_ref,
            fields,
            rows,
            f,
            lambda i: src_ref[pl.ds(f * cells * rows + i, cells, stride=rows)],
            ahead,
            back,
            store,
        )


def last_kernel(coef_ref, *refs):
    parts, (src_ref, out_ref, z_ref) = refs[:-3], refs[-3:]
    count = len(parts) // 2
    fields, cells, rows, width = src_ref.shape
    entry = [
        [
            jnp.concatenate([sum(ref[f, m] for ref in parts[:count]), sum(ref[f, m] for ref in parts[count:])])
            for m in range(4)
        ]
        for f in range(fields)
    ]
    lower_sweep(
        coef_ref,
        cells,
        lambda j: [src_ref[f, j] for f in range(fields)],
        z_ref,
        tuple((e[0], e[1]) for e in entry),
    )

    def store(f, j, value):
        out_ref[f, j] = value

    upper_sweep(coef_ref, cells, z_ref, tuple((e[2], e[3]) for e in entry), store)


def azim_table_kernel(coef_ref, enter_ref, reply_ref):
    _, blocks, cells, fields = coef_ref.shape
    own = lax.axis_index("azim")

    def weight(a, b):
        return jnp.sqrt(1.0 - (a + b) * (a + b))

    unit = lax.broadcasted_iota(jnp.int32, (blocks, 8, fields), 1)

    def ones(k):
        return (unit == k).astype(f32)

    one, two = ones(0), ones(1)
    held = []
    for j in range(cells):
        z = coef_ref[0, :, j : j + 1] * one + coef_ref[1, :, j : j + 1] * two
        held.append(z)
        one, two = z, one
    lower = (one, two)
    one, two = ones(2), ones(3)
    for j in reversed(range(cells)):
        c, e = coef_ref[2, :, j : j + 1], coef_ref[3, :, j : j + 1]
        v = weight(c, e) * held[j] + c * one + e * two
        one, two = v, one
    upper = (one, two)

    cell = lax.broadcasted_iota(jnp.int32, (cells, fields), 0)
    one = two = jnp.zeros((cells, fields), f32)
    held = []
    for j in range(cells):
        a, b = coef_ref[0, own, j : j + 1], coef_ref[1, own, j : j + 1]
        z = jnp.where(cell == j, weight(a, b), 0.0) + a * one + b * two
        held.append(z)
        one, two = z, one
    reply_ref[0], reply_ref[1] = one, two
    one = two = jnp.zeros((cells, fields), f32)
    for j in reversed(range(cells)):
        c, e = coef_ref[2, own, j : j + 1], coef_ref[3, own, j : j + 1]
        v = weight(c, e) * held[j] + c * one + e * two
        one, two = v, one
    reply_ref[2], reply_ref[3] = one, two

    def entry(pair, p, m, k):
        return pair[m][p, k : k + 1]

    count = 4 * blocks
    height = -(-(count + 2) // 8) * 8
    row = lax.broadcasted_iota(jnp.int32, (height, fields), 0)

    def slot(p, k):
        return (row == 4 * (p ^ own) + k).astype(f32)

    def through(order, pair, first, source, start):
        state, entering = start, {}
        for p in order:
            entering[p] = state
            state = tuple(
                source(p, m) + entry(pair, p, m, first) * state[0] + entry(pair, p, m, first + 1) * state[1]
                for m in range(2)
            )
        return state, entering

    def closed(order, pair, first, source):
        start = tuple((row == count + k).astype(f32) for k in range(2))
        (total_one, total_two), _ = through(order, pair, first, source, start)
        a = 1.0 - total_one[count : count + 1]
        b = total_one[count + 1 : count + 2]
        c = total_two[count : count + 1]
        d = 1.0 - total_two[count + 1 : count + 2]
        scale = 1.0 / (a * d - b * c)
        live = row < count
        total_one, total_two = jnp.where(live, total_one, 0.0), jnp.where(live, total_two, 0.0)
        start = ((d * total_one + b * total_two) * scale, (c * total_one + a * total_two) * scale)
        return through(order, pair, first, source, start)[1]

    lower_in = closed(range(blocks), lower, 0, slot)

    def upper_source(p, m):
        z_one, z_two = lower_in[p]
        return slot(p, 2 + m) + entry(upper, p, m, 0) * z_one + entry(upper, p, m, 1) * z_two

    upper_in = closed(list(reversed(range(blocks))), upper, 2, upper_source)
    for i, step in enumerate(targets_of(blocks)):
        for m in range(4):
            picked = jnp.zeros((height, fields), f32)
            for p in range(blocks):
                value = lower_in[p][m] if m < 2 else upper_in[p][m - 2]
                picked = jnp.where(own == (p ^ step), value, picked)
            enter_ref[i, m] = picked[:count]


def rad_table_kernel(coef_ref, own_ref, enter_ref, pivot_ref):
    _, cells, fields = coef_ref.shape
    rows = own_ref.shape[1]
    blocks = cells // rows
    own = lax.axis_index("rad")
    total = 1.0 + coef_ref[0, 0:1]
    for i in range(cells):
        pivot = coef_ref[1, i : i + 1] + total
        pivot_ref[1 + i : 2 + i] = pivot
        if i + 1 < cells:
            total = 1.0 + coef_ref[0, i + 1 : i + 2] * (total / pivot)
    pivot_ref[0:1] = jnp.ones((1, fields), f32)
    lower, upper = coef_ref[0], coef_ref[1]
    first = lax.broadcasted_iota(jnp.int32, (cells, fields), 0) == 0
    scale = jnp.sqrt(jnp.sqrt(1.0 + lower + upper))
    inverse = 1.0 / pivot_ref[1 : cells + 1]
    forward = jnp.where(first, 0.0, lower / pivot_ref[0:cells])
    backward = upper * inverse
    for kind, table in enumerate((scale, forward, inverse, backward)):
        picked = jnp.zeros((rows, fields), f32)
        for p in range(blocks):
            picked = jnp.where(own == p, table[p * rows : (p + 1) * rows], picked)
        own_ref[kind] = picked

    maps = []
    for p in range(blocks):
        lines = [slice(p * rows + i, p * rows + i + 1) for i in range(rows)]
        ahead, held = jnp.ones((1, fields), f32), []
        for line in lines:
            ahead = forward[line] * ahead
            held.append(ahead)
        back, gain = jnp.zeros((1, fields), f32), jnp.ones((1, fields), f32)
        for line, value in zip(reversed(lines), reversed(held)):
            back = inverse[line] * value + backward[line] * back
            gain = backward[line] * gain
        maps.append((ahead, back, gain))
    count = 2 * blocks
    height = -(-count // 8) * 8
    row = lax.broadcasted_iota(jnp.int32, (height, fields), 0)

    def slot(p, k):
        return (row == 2 * (p ^ own) + k).astype(f32)

    zero = jnp.zeros((height, fields), f32)
    ahead, ahead_in = zero, {}
    for p in range(blocks):
        ahead_in[p] = ahead
        ahead = slot(p, 0) + maps[p][0] * ahead
    back, back_in = zero, {}
    for p in reversed(range(blocks)):
        back_in[p] = back
        back = slot(p, 1) + maps[p][1] * ahead_in[p] + maps[p][2] * back
    for i, step in enumerate(targets_of(blocks)):
        for m, entering in enumerate((ahead_in, back_in)):
            picked = zero
            for p in range(blocks):
                picked = jnp.where(own == (p ^ step), entering[p], picked)
            enter_ref[i, m] = picked[:count]


def from_partner(values, axis, step):
    if step == 0:
        return values
    return lax.ppermute(values, axis, [(i, i ^ step) for i in range(lax.axis_size(axis))])


def local(residual, left_vec, dissip, azim_coef, radial_coef):
    fields, cells, rows, width = residual.shape
    azim_count, rad_count = lax.axis_size("azim"), lax.axis_size("rad")
    whole, flat = (fields, cells, rows, width), (fields * cells * rows, width)
    edge = call(edge_kernel, [(fields, rows, width)], 0, 1)(residual)[0]
    halo = lax.ppermute(edge, "axial", [(0, 1), (1, 0)])

    weights = jnp.sqrt(1.0 - (azim_coef[0::2] + azim_coef[1::2]) ** 2)
    kinds = jnp.concatenate([azim_coef[:2], weights[:1], azim_coef[2:], weights[1:]])
    own_azim = lax.dynamic_slice_in_dim(kinds, lax.axis_index("azim") * cells, cells, 2).reshape(-1)
    azim_blocks = azim_coef.reshape(4, fields, azim_count, cells).transpose(0, 2, 3, 1)
    azim_enter, reply = call(
        azim_table_kernel,
        [(len(targets_of(azim_count)), 4, 4 * azim_count, fields), (4, cells, fields)],
        0,
        1,
    )(azim_blocks)
    reply = jnp.pad(reply.transpose(2, 0, 1), ((0, 0), (0, 0), (0, width - cells)))
    own_rad, rad_enter = call(
        rad_table_kernel,
        [(4, rows, fields), (len(targets_of(rad_count)), 2, 2 * rad_count, fields)],
        0,
        1,
        [(rad_count * rows + 8, fields)],
    )(radial_coef.transpose(0, 2, 1))
    azim_enter, rad_enter = azim_enter.reshape(-1), rad_enter.reshape(-1)
    own_rad = own_rad.transpose(0, 2, 1).reshape(-1)
    vec = left_vec.reshape(-1)

    four = (fields, 4, rows, width)
    src, states = call(first_kernel, [whole, four], 3, 1, [whole])(own_azim, vec, dissip, residual)
    states, part, small = call(
        patch_kernel, [(fields * 4 * rows, width), (fields, rows, width), (fields, 8, width)], 3, 3
    )(vec, dissip, own_rad, halo, states, reply)
    smalls = [from_partner(small, "rad", s) for s in range(rad_count)]
    src, ends = call(source_kernel, [flat, (fields, 2, cells, width)], 1, 2)(own_rad, src, part)
    half = (fields, 4, rows // 2, width)
    one, two = call(state_kernel, [half, half], 2, rad_count + 1, [(fields * 4 * rows, width)])(
        rad_enter, own_rad, *smalls, states
    )
    low, high = low_high(azim_count)
    ones = [from_partner(one, "azim", s) for s in low]
    twos = [from_partner(two, "azim", s) for s in high]

    near, far = low_high(rad_count)
    gathered = [from_partner(ends, "rad", s) for s in near]
    sums = call(
        lambda *refs: spread_kernel(rad_count, 2, near, far, *refs), [ends.shape] * len(far), 1, len(near)
    )(rad_enter, *gathered)
    entry = [from_partner(value, "rad", s) for s, value in zip(far, sums)]
    src = call(radial_kernel, [flat], 1, len(far) + 1)(own_rad, *entry, src)[0]

    sums = call(
        lambda *refs: spread_both(azim_count, low, high, *refs),
        [half] * (len(low) + len(high)),
        1,
        len(low) + len(high),
    )(azim_enter, *ones, *twos)
    ones = [from_partner(value, "azim", s) for s, value in zip(high, sums[: len(high)])]
    twos = [from_partner(value, "azim", s) for s, value in zip(low, sums[len(high) :])]
    ones = ones + [jnp.zeros_like(one)] * (max(len(low), len(high)) - len(high))
    twos = twos + [jnp.zeros_like(two)] * (max(len(low), len(high)) - len(low))
    return call(last_kernel, [whole], 1, len(ones) + len(twos) + 1, [whole])(
        own_azim, *ones, *twos, src.reshape(whole)
    )[0]


def solution(mesh):
    placed = (P(None, "azim", "rad", "axial"), P(), P(), P(), P())
    return jax.shard_map(
        local,
        mesh=mesh,
        in_specs=placed,
        out_specs=P(None, "azim", "rad", "axial"),
        check_vma=False,
    )
```

time: 43 us -> 38 us (0.88)
  waiting for transfers between devices: 20 us -> 7.98 us
  starting transfers between devices: 9.77 us -> 13.1 us
  Pallas kernels: 10.7 us -> 14 us
    ppermute x6 -> x9, waiting for transfers between devices: 18.4 us -> 7.98 us  [from_partner(): lax.ppermute(values, axis, [(i, i ^ step) for i in range(lax.axis_size(ax...]
    pallas_call x5 -> x10, Pallas kernels: 9.75 us -> 13.1 us  [the longest x1 2.56 us: local(): call(source_kernel, [flat, (fields, 2, cells, width)], 1, 2)]
    ppermute x6 -> x9, starting transfers between devices: 6.74 us -> 10.1 us  [from_partner(): lax.ppermute(values, axis, [(i, i ^ step) for i in range(lax.axis_size(ax...]
    ppermute x1, waiting for transfers between devices: 1.61 us -> 0.01 us  [local(): halo = lax.ppermute(edge, 'axial', [(0, 1), (1, 0)])]
  transfers between devices with their start and end apart: 7 -> 10, of which waited for: 5 -> 5; matrix products, arithmetic and copies ran while one was open for 2% -> 3% of each run, Pallas kernels for 3% -> 19%
where the time goes in v2:
time: 38 us; the launch traced here: 37.8 us
  Pallas kernels  14 us (37%)
  starting transfers between devices  13.1 us (34%)
  waiting for transfers between devices  7.98 us (21%)
  local copies, waits for them, and re-layouts  2.4 us (6%)
    ppermute x9, starting transfers between devices, from_partner(): lax.ppermute(values, axis, [(i, i ^ step) for i in range(lax.axis_size(ax...  10.1 us
    ppermute x9, waiting for transfers between devices, from_partner(): lax.ppermute(values, axis, [(i, i ^ step) for i in range(lax.axis_size(ax...  7.98 us
    ppermute x1, starting transfers between devices, local(): halo = lax.ppermute(edge, 'axial', [(0, 1), (1, 0)])  3.03 us
    pallas_call x1, Pallas kernels, local(): call(source_kernel, [flat, (fields, 2, cells, width)], 1, 2)  2.56 us
    pallas_call x1, Pallas kernels, local(): call(last_kernel, [whole], 1, len(ones) + len(twos) + 1, [whole])  2.41 us
    pallas_call x1, Pallas kernels, local(): call(first_kernel, [whole, four], 3, 1, [whole])  2.3 us
    unnamed x14, local copies, waits for them, and re-layouts  1.58 us
    pallas_call x1, Pallas kernels, local(): src = call(radial_kernel, [flat], 1, len(far) + 1)(own_rad, *entry, src)[0]  1.37 us
  transfers between devices with their start and end apart: 10, of which 5 were waited for; matrix products, arithmetic and copies ran while one was open for 3% of the time, Pallas kernels for 19%

profile of v2, /device:TPU:0, one launch (start us, length us, event | category | flops | bytes accessed | tf_op | source)
XLA Modules:
  0.0 37.8 jit_solution(2429183440274535910)
XLA Ops:
  0.0 1.3 %copy-done = f32[5,32,16,128]{3,2,1,0:T(8,128)S(1)} copy-done((f32[5,32,16,128]{3,2,1,0:T(8,128)S(1)}, f32[5,32,16,128]{3,2,1,0:T(8,128)}, u32[]{:S(2)}) %copy-start) | copy-done | bytes 1310744
  1.3 0.9 %shard_map.57 = f32[5,16,128]{2,1,0:T(8,128)S(1)} custom-call(f32[5,32,16,128]{3,2,1,0:T(8,128)S(1)} %copy-done), custom_call_target="tpu_custom_call" | custom-call | tf_op jit(solution)/shard_map/pallas_call | solution.py:443
  2.3 3.0 %collective-permute-start = (f32[5,16,128]{2,1,0:T(8,128)S(1)}, f32[5,16,128]{2,1,0:T(8,128)S(1)}, u32[]{:S(2)}, u32[]{:S(2)}) collective-permute-start(f32[5,16,128]{2,1,0:T(8,128)S(1)} %shard_map.57), channel_id=1, source_target_pairs={{0,1},{1,0},{2,3},{3,2},{4,5},{5,4},{6,7},{7,6},{8,9},{9,8},{10,11... | collective-permute-start | bytes 122888 | tf_op jit(solution)/shard_map/ppermute | solution.py:444
  5.4 0.1 dynamic-slice_maximum_fusion
  5.5 0.1 copy.10
  5.8 0.1 copy.11
  5.9 0.7 %shard_map.56 = (f32[4,16,5]{2,1,0:T(8,128)S(1)}, f32[3,2,8,5]{3,2,1,0:T(8,128)S(1)}) custom-call(f32[2,64,5]{2,1,0:T(8,128)S(1)} %bitcast.13), custom_call_target="tpu_custom_call" | custom-call | tf_op jit(solution)/shard_map/pallas_call | solution.py:457
  6.6 0.1 copy.12
  6.8 0.7 %shard_map.55 = (f32[3,4,16,5]{3,2,1,0:T(8,128)S(1)}, f32[4,32,5]{2,1,0:T(8,128)S(1)}) custom-call(f32[4,4,32,5]{3,2,1,0:T(8,128)S(1)} %bitcast.12), custom_call_target="tpu_custom_call" | custom-call | tf_op jit(solution)/shard_map/pallas_call | solution.py:450
  7.5 0.1 copy.13
  7.6 2.3 %shard_map.58 = (f32[5,32,16,128]{3,2,1,0:T(8,128)S(1)}, f32[5,4,16,128]{3,2,1,0:T(8,128)S(1)}) custom-call(f32[960]{0:T(1024)S(1)} %reshape.21.coef_ref, f32[25]{0:T(128)S(1)} %reshape.26.vec_ref, f32[5]{0:T(128)S(1)} %copy-done.2, f32[5,32,16,128]{3,2,1,0:T(8,128)S(1)} %copy-done.1), custom_call_target="tpu_custom_call" | custom-call | tf_op jit(solution)/shard_map/pallas_call | solution.py:469
  9.9 0.8 %shard_map.59 = (f32[320,128]{1,0:T(8,128)S(1)}, f32[5,16,128]{2,1,0:T(8,128)S(1)}, f32[5,8,128]{2,1,0:T(8,128)S(1)}) custom-call(f32[25]{0:T(128)S(1)} %reshape.26.vec_ref, f32[5]{0:T(128)S(1)} %copy-done.2, f32[320]{0:T(512)S(1)} %reshape.25.rad_ref, f32[5,16,128]{2,1,0:T(8,128)S(1)} %collective-permute-done.halo_ref, ...), custom_call_target="tpu_custom_call" | custom-call | tf_op jit(solution)/shard_map/pallas_call | solution.py:470
  10.8 2.6 %shard_map.62 = (f32[2560,128]{1,0:T(8,128)S(1)}, f32[5,2,32,128]{3,2,1,0:T(8,128)S(1)}) custom-call(f32[320]{0:T(512)S(1)} %reshape.25.rad_ref, f32[5,32,16,128]{3,2,1,0:T(8,128)S(1)} %get-tuple-element.37.src_ref, f32[5,16,128]{2,1,0:T(8,128)S(1)} %get-tuple-element.38.part_ref), custom_call_target="tpu_custom_call" | custom-call | tf_op jit(solution)/shard_map/pallas_call | solution.py:474
  13.4 0.5 %collective-permute-start.1 = (f32[5,8,128]{2,1,0:T(8,128)S(1)}, f32[5,8,128]{2,1,0:T(8,128)S(1)}, u32[]{:S(2)}, u32[]{:S(2)}) collective-permute-start(f32[5,8,128]{2,1,0:T(8,128)S(1)} %get-tuple-element.29.refs_0_), channel_id=1, source_target_pairs={{0,2},{2,0},{4,6},{6,4},{1,3},{3,1},{5,7},{7,5},{8,10},{10,8},{12,... | collective-permute-start | bytes 61448 | tf_op jit(solution)/shard_map/ppermute | solution.py:436
  13.9 1.5 %collective-permute-start.2 = (f32[5,8,128]{2,1,0:T(8,128)S(1)}, f32[5,8,128]{2,1,0:T(8,128)S(1)}, u32[]{:S(2)}, u32[]{:S(2)}) collective-permute-start(f32[5,8,128]{2,1,0:T(8,128)S(1)} %get-tuple-element.29.refs_0_), channel_id=1, source_target_pairs={{0,4},{2,6},{4,0},{6,2},{1,5},{3,7},{5,1},{7,3},{8,12},{10,14},{12... | collective-permute-start | bytes 61448 | tf_op jit(solution)/shard_map/ppermute | solution.py:436
  15.4 0.1 reshape.24.rad_enter_ref.refs_0_
  15.5 2.2 %collective-permute-done.2.refs_2_ = f32[5,8,128]{2,1,0:T(8,128)S(1)} collective-permute-done((f32[5,8,128]{2,1,0:T(8,128)S(1)}, f32[5,8,128]{2,1,0:T(8,128)S(1)}, u32[]{:S(2)}, u32[]{:S(2)}) %collective-permute-start.2) | collective-permute-done | bytes 20512 | tf_op jit(solution)/shard_map/ppermute | solution.py:436
  17.7 1.1 %collective-permute-done.3.refs_3_ = f32[5,8,128]{2,1,0:T(8,128)S(1)} collective-permute-done((f32[5,8,128]{2,1,0:T(8,128)S(1)}, f32[5,8,128]{2,1,0:T(8,128)S(1)}, u32[]{:S(2)}, u32[]{:S(2)}) %collective-permute-start.3) | collective-permute-done | bytes 20512 | tf_op jit(solution)/shard_map/ppermute | solution.py:436
  18.8 0.8 %shard_map.60 = (f32[5,4,8,128]{3,2,1,0:T(8,128)S(1)}, f32[5,4,8,128]{3,2,1,0:T(8,128)S(1)}) custom-call(f32[240]{0:T(256)S(1)} %reshape.24.rad_enter_ref.refs_0_, f32[320]{0:T(512)S(1)} %reshape.25.rad_ref, f32[5,8,128]{2,1,0:T(8,128)S(1)} %get-tuple-element.29.refs_0_, f32[5,8,128]{2,1,0:T(8,128)S(1)} %collective-permute-done.1.refs_1_, ...), custom_call_target="tpu_custom_call" | custom-call | tf_op jit(solution)/shard_map/pallas_call | solution.py:476
  19.6 1.6 %collective-permute-start.4 = (f32[5,4,8,128]{3,2,1,0:T(8,128)S(1)}, f32[5,4,8,128]{3,2,1,0:T(8,128)S(1)}, u32[]{:S(2)}, u32[]{:S(2)}) collective-permute-start(f32[5,4,8,128]{3,2,1,0:T(8,128)S(1)} %get-tuple-element.31.refs_1_), channel_id=1, source_target_pairs={{0,8},{8,0},{16,24},{24,16},{1,9},{9,1},{17,25},{25,17},{2,10},{10... | collective-permute-start | bytes 245768 | tf_op jit(solution)/shard_map/ppermute | solution.py:436
  21.2 2.6 %collective-permute-start.5 = (f32[5,4,8,128]{3,2,1,0:T(8,128)S(1)}, f32[5,4,8,128]{3,2,1,0:T(8,128)S(1)}, u32[]{:S(2)}, u32[]{:S(2)}) collective-permute-start(f32[5,4,8,128]{3,2,1,0:T(8,128)S(1)} %get-tuple-element.32.refs_3_), channel_id=1, source_target_pairs={{0,16},{8,24},{16,0},{24,8},{1,17},{9,25},{17,1},{25,9},{2,18},{10... | collective-permute-start | bytes 245768 | tf_op jit(solution)/shard_map/ppermute | solution.py:436
  23.8 0.6 %shard_map.63 = (f32[5,2,32,128]{3,2,1,0:T(8,128)S(1)}, f32[5,2,32,128]{3,2,1,0:T(8,128)S(1)}) custom-call(f32[240]{0:T(256)S(1)} %reshape.24.rad_enter_ref.refs_0_, f32[5,2,32,128]{3,2,1,0:T(8,128)S(1)} %get-tuple-element.39.refs_1_, f32[5,2,32,128]{3,2,1,0:T(8,128)S(1)} %collective-permute-done.8.refs_2_), custom_call_target="tpu_custom_call" | custom-call | tf_op jit(solution)/shard_map/pallas_call | solution.py:485
  24.5 0.6 %collective-permute-start.9 = (f32[5,2,32,128]{3,2,1,0:T(8,128)S(1)}, f32[5,2,32,128]{3,2,1,0:T(8,128)S(1)}, u32[]{:S(2)}, u32[]{:S(2)}) collective-permute-start(f32[5,2,32,128]{3,2,1,0:T(8,128)S(1)} %get-tuple-element.41), channel_id=1, source_target_pairs={{0,4},{2,6},{4,0},{6,2},{1,5},{3,7},{5,1},{7,3},{8,12},{10,14},{12... | collective-permute-start | bytes 491528 | tf_op jit(solution)/shard_map/ppermute | solution.py:436
  25.1 0.2 reshape.23.refs_0_
  25.3 2.8 %collective-permute-done.5.refs_4_ = f32[5,4,8,128]{3,2,1,0:T(8,128)S(1)} collective-permute-done((f32[5,4,8,128]{3,2,1,0:T(8,128)S(1)}, f32[5,4,8,128]{3,2,1,0:T(8,128)S(1)}, u32[]{:S(2)}, u32[]{:S(2)}) %collective-permute-start.5) | collective-permute-done | bytes 81952 | tf_op jit(solution)/shard_map/ppermute | solution.py:436
  28.1 0.8 %shard_map.61 = (f32[5,4,8,128]{3,2,1,0:T(8,128)S(1)}, f32[5,4,8,128]{3,2,1,0:T(8,128)S(1)}, f32[5,4,8,128]{3,2,1,0:T(8,128)S(1)}, f32[5,4,8,128]{3,2,1,0:T(8,128)S(1)}) custom-call(f32[960]{0:T(1024)S(1)} %reshape.23.refs_0_, f32[5,4,8,128]{3,2,1,0:T(8,128)S(1)} %get-tuple-element.31.refs_1_, f32[5,4,8,128]{3,2,1,0:T(8,128)S(1)} %collective-permute-done.4.refs_2_, ...), custom_call_target="tpu_custom_call" | custom-call | tf_op jit(solution)/shard_map/pallas_call | solution.py:491
  29.0 1.1 %collective-permute-start.6 = (f32[5,4,8,128]{3,2,1,0:T(8,128)S(1)}, f32[5,4,8,128]{3,2,1,0:T(8,128)S(1)}, u32[]{:S(2)}, u32[]{:S(2)}) collective-permute-start(f32[5,4,8,128]{3,2,1,0:T(8,128)S(1)} %get-tuple-element.34), channel_id=1, source_target_pairs={{0,16},{8,24},{16,0},{24,8},{1,17},{9,25},{17,1},{25,9},{2,18},{10... | collective-permute-start | bytes 245768 | tf_op jit(solution)/shard_map/ppermute | solution.py:436
  30.1 2.1 %collective-permute-start.7 = (f32[5,4,8,128]{3,2,1,0:T(8,128)S(1)}, f32[5,4,8,128]{3,2,1,0:T(8,128)S(1)}, u32[]{:S(2)}, u32[]{:S(2)}) collective-permute-start(f32[5,4,8,128]{3,2,1,0:T(8,128)S(1)} %get-tuple-element.36), channel_id=1, source_target_pairs={{0,8},{8,0},{16,24},{24,16},{1,9},{9,1},{17,25},{25,17},{2,10},{10... | collective-permute-start | bytes 245768 | tf_op jit(solution)/shard_map/ppermute | solution.py:436
  32.1 1.4 %shard_map.64 = f32[2560,128]{1,0:T(8,128)S(1)} custom-call(f32[320]{0:T(512)S(1)} %reshape.25.rad_ref, f32[5,2,32,128]{3,2,1,0:T(8,128)S(1)} %get-tuple-element.40.refs_0_, f32[5,2,32,128]{3,2,1,0:T(8,128)S(1)} %collective-permute-done.9.refs_1_, f32[2560,128]{1,0:T(8,128)S(1)} %get-tuple-element.42.refs_2_), custom_call_target="tpu_custom_call" | custom-call | tf_op jit(solution)/shard_map/pallas_call | solution.py:489
  33.5 1.7 %collective-permute-done.6.refs_1_ = f32[5,4,8,128]{3,2,1,0:T(8,128)S(1)} collective-permute-done((f32[5,4,8,128]{3,2,1,0:T(8,128)S(1)}, f32[5,4,8,128]{3,2,1,0:T(8,128)S(1)}, u32[]{:S(2)}, u32[]{:S(2)}) %collective-permute-start.6) | collective-permute-done | bytes 81952 | tf_op jit(solution)/shard_map/ppermute | solution.py:436
  35.2 0.2 collective-permute-done.7.refs_3_
  35.4 2.4 %shard_map.65 = f32[5,32,16,128]{3,2,1,0:T(8,128)} custom-call(f32[960]{0:T(1024)S(1)} %reshape.21.coef_ref, f32[5,4,8,128]{3,2,1,0:T(8,128)S(1)} %get-tuple-element.33.refs_0_, f32[5,4,8,128]{3,2,1,0:T(8,128)S(1)} %collective-permute-done.6.refs_1_, f32[5,4,8,128]{3,2,1,0:T(8,128)S(1)} %get-tuple-element.35.refs_2_, ...), custom_call_target="tpu_custom_call" | custom-call | tf_op jit(solution)/shard_map/pallas_call | solution.py:501
  (28 shorter events, 0.4 us)
Async XLA Ops:
  0.0 1.3 %copy-start = (f32[5,32,16,128]{3,2,1,0:T(8,128)S(1)}, f32[5,32,16,128]{3,2,1,0:T(8,128)}, u32[]{:S(2)}) copy-start(f32[5,32,16,128]{3,2,1,0:T(8,128)} %res_ref.3) | copy-start | bytes 3932164
  1.3 4.0 %copy-start.3 = (f32[4,5,128]{2,0,1:T(4,128)S(1)}, f32[4,5,128]{2,0,1:T(4,128)}, u32[]{:S(2)}) copy-start(f32[4,5,128]{2,0,1:T(4,128)} %param.8) | copy-start | bytes 30724
  1.3 4.4 %copy-start.5 = (f32[5,5]{1,0:T(8,128)S(1)}, f32[5,5]{1,0:T(8,128)}, u32[]{:S(2)}) copy-start(f32[5,5]{1,0:T(8,128)} %param.6) | copy-start | bytes 304
  1.3 4.5 %copy-start.4 = (f32[2,5,64]{2,0,1:T(2,128)S(1)}, f32[2,5,64]{2,0,1:T(2,128)}, u32[]{:S(2)}) copy-start(f32[2,5,64]{2,0,1:T(2,128)} %param.9) | copy-start | bytes 7684
  1.3 6.3 %copy-start.1 = (f32[5,32,16,128]{3,2,1,0:T(8,128)S(1)}, f32[5,32,16,128]{3,2,1,0:T(8,128)}, u32[]{:S(2)}) copy-start(f32[5,32,16,128]{3,2,1,0:T(8,128)} %res_ref.3) | copy-start | bytes 3932164
  1.3 6.3 %copy-start.2 = (f32[5]{0:T(128)S(1)}, f32[5]{0:T(128)}, u32[]{:S(2)}) copy-start(f32[5]{0:T(128)} %dis_ref.3) | copy-start | bytes 64
  2.3 7.7 %collective-permute-start = (f32[5,16,128]{2,1,0:T(8,128)S(1)}, f32[5,16,128]{2,1,0:T(8,128)S(1)}, u32[]{:S(2)}, u32[]{:S(2)}) collective-permute-start(f32[5,16,128]{2,1,0:T(8,128)S(1)} %shard_map.57), channel_id=1, source_target_pairs={{0,1},{1,0},{2,3},{3,2},{4,5},{5,4},{6,7},{7,6},{8,9},{9,8},{10,11... | collective-permute-start | bytes 122888 | tf_op jit(solution)/shard_map/ppermute | solution.py:444
  13.3 10.5 %collective-permute-start.8 = (f32[5,2,32,128]{3,2,1,0:T(8,128)S(1)}, f32[5,2,32,128]{3,2,1,0:T(8,128)S(1)}, u32[]{:S(2)}, u32[]{:S(2)}) collective-permute-start(f32[5,2,32,128]{3,2,1,0:T(8,128)S(1)} %get-tuple-element.39.refs_1_), channel_id=1, source_target_pairs={{0,2},{2,0},{4,6},{6,4},{1,3},{3,1},{5,7},{7,5},{8,10},{10,8},{12,... | collective-permute-start | bytes 491528 | tf_op jit(solution)/shard_map/ppermute | solution.py:436
  13.4 2.1 %collective-permute-start.1 = (f32[5,8,128]{2,1,0:T(8,128)S(1)}, f32[5,8,128]{2,1,0:T(8,128)S(1)}, u32[]{:S(2)}, u32[]{:S(2)}) collective-permute-start(f32[5,8,128]{2,1,0:T(8,128)S(1)} %get-tuple-element.29.refs_0_), channel_id=1, source_target_pairs={{0,2},{2,0},{4,6},{6,4},{1,3},{3,1},{5,7},{7,5},{8,10},{10,8},{12,... | collective-permute-start | bytes 61448 | tf_op jit(solution)/shard_map/ppermute | solution.py:436
  13.9 3.8 %collective-permute-start.2 = (f32[5,8,128]{2,1,0:T(8,128)S(1)}, f32[5,8,128]{2,1,0:T(8,128)S(1)}, u32[]{:S(2)}, u32[]{:S(2)}) collective-permute-start(f32[5,8,128]{2,1,0:T(8,128)S(1)} %get-tuple-element.29.refs_0_), channel_id=1, source_target_pairs={{0,4},{2,6},{4,0},{6,2},{1,5},{3,7},{5,1},{7,3},{8,12},{10,14},{12... | collective-permute-start | bytes 61448 | tf_op jit(solution)/shard_map/ppermute | solution.py:436
  15.4 3.4 %collective-permute-start.3 = (f32[5,8,128]{2,1,0:T(8,128)S(1)}, f32[5,8,128]{2,1,0:T(8,128)S(1)}, u32[]{:S(2)}, u32[]{:S(2)}) collective-permute-start(f32[5,8,128]{2,1,0:T(8,128)S(1)} %get-tuple-element.29.refs_0_), channel_id=1, source_target_pairs={{0,6},{2,4},{4,2},{6,0},{1,7},{3,5},{5,3},{7,1},{8,14},{10,12},{12... | collective-permute-start | bytes 61448 | tf_op jit(solution)/shard_map/ppermute | solution.py:436
  19.6 5.7 %collective-permute-start.4 = (f32[5,4,8,128]{3,2,1,0:T(8,128)S(1)}, f32[5,4,8,128]{3,2,1,0:T(8,128)S(1)}, u32[]{:S(2)}, u32[]{:S(2)}) collective-permute-start(f32[5,4,8,128]{3,2,1,0:T(8,128)S(1)} %get-tuple-element.31.refs_1_), channel_id=1, source_target_pairs={{0,8},{8,0},{16,24},{24,16},{1,9},{9,1},{17,25},{25,17},{2,10},{10... | collective-permute-start | bytes 245768 | tf_op jit(solution)/shard_map/ppermute | solution.py:436
  21.2 6.9 %collective-permute-start.5 = (f32[5,4,8,128]{3,2,1,0:T(8,128)S(1)}, f32[5,4,8,128]{3,2,1,0:T(8,128)S(1)}, u32[]{:S(2)}, u32[]{:S(2)}) collective-permute-start(f32[5,4,8,128]{3,2,1,0:T(8,128)S(1)} %get-tuple-element.32.refs_3_), channel_id=1, source_target_pairs={{0,16},{8,24},{16,0},{24,8},{1,17},{9,25},{17,1},{25,9},{2,18},{10... | collective-permute-start | bytes 245768 | tf_op jit(solution)/shard_map/ppermute | solution.py:436
  24.5 7.7 %collective-permute-start.9 = (f32[5,2,32,128]{3,2,1,0:T(8,128)S(1)}, f32[5,2,32,128]{3,2,1,0:T(8,128)S(1)}, u32[]{:S(2)}, u32[]{:S(2)}) collective-permute-start(f32[5,2,32,128]{3,2,1,0:T(8,128)S(1)} %get-tuple-element.41), channel_id=1, source_target_pairs={{0,4},{2,6},{4,0},{6,2},{1,5},{3,7},{5,1},{7,3},{8,12},{10,14},{12... | collective-permute-start | bytes 491528 | tf_op jit(solution)/shard_map/ppermute | solution.py:436
  29.0 6.3 %collective-permute-start.6 = (f32[5,4,8,128]{3,2,1,0:T(8,128)S(1)}, f32[5,4,8,128]{3,2,1,0:T(8,128)S(1)}, u32[]{:S(2)}, u32[]{:S(2)}) collective-permute-start(f32[5,4,8,128]{3,2,1,0:T(8,128)S(1)} %get-tuple-element.34), channel_id=1, source_target_pairs={{0,16},{8,24},{16,0},{24,8},{1,17},{9,25},{17,1},{25,9},{2,18},{10... | collective-permute-start | bytes 245768 | tf_op jit(solution)/shard_map/ppermute | solution.py:436
  30.1 5.3 %collective-permute-start.7 = (f32[5,4,8,128]{3,2,1,0:T(8,128)S(1)}, f32[5,4,8,128]{3,2,1,0:T(8,128)S(1)}, u32[]{:S(2)}, u32[]{:S(2)}) collective-permute-start(f32[5,4,8,128]{3,2,1,0:T(8,128)S(1)} %get-tuple-element.36), channel_id=1, source_target_pairs={{0,8},{8,0},{16,24},{24,16},{1,9},{9,1},{17,25},{25,17},{2,10},{10... | collective-permute-start | bytes 245768 | tf_op jit(solution)/shard_map/ppermute | solution.py:436

commit v3 on v2

--- a/solution.py
+++ b/solution.py
@@ -11,7 +11,7 @@
 params = pltpu.CompilerParams(vmem_limit_bytes=32 * 1024 * 1024)
 
 
-def call(body, outs, n_smem, n_vmem, scratch=()):
+def call(body, outs, n_smem, n_vmem, scratch=(), cost=0):
     return pl.pallas_call(
         body,
         out_shape=[jax.ShapeDtypeStruct(shape, f32) for shape in outs],
@@ -19,6 +19,7 @@
         out_specs=[VMEM] * len(outs),
         scratch_shapes=[pltpu.VMEM(shape, f32) for shape in scratch],
         compiler_params=params,
+        cost_estimate=pl.CostEstimate(flops=cost, bytes_accessed=0, transcendentals=0),
     )
 
 
@@ -44,15 +45,11 @@
     fields, cells, rows, width = res_ref.shape
     source = far_lane(width)
     lane = lanes_of((rows, width))
-
-    def step(j, packed):
-        return tuple(
-            jnp.where(lane == j, pltpu.roll(res_ref[f, j], (j - source + width) % width, 1), packed[f])
-            for f in range(fields)
-        )
-
-    edge_ref[...] = jnp.zeros(edge_ref.shape, f32)
-    packed = lax.fori_loop(0, cells, step, tuple(edge_ref[f] for f in range(fields)), unroll=4)
+    packed = [jnp.zeros((rows, width), f32)] * fields
+    for j in range(cells):
+        for f in range(fields):
+            moved = pltpu.roll(res_ref[f, j], (j - source + width) % width, 1)
+            packed[f] = jnp.where(lane == j, moved, packed[f])
     for f in range(fields):
         edge_ref[f] = packed[f]
 
@@ -78,11 +75,12 @@
     return lax.fori_loop(0, cells, step, start, unroll=4)
 
 
-def upper_sweep(coef_ref, cells, z_ref, start, store=None):
+def upper_sweep(coef_ref, cells, z_ref, start, store=None, first=0, count=None):
     fields = len(start)
+    count = cells if count is None else count
 
     def step(i, carry):
-        j = cells - 1 - i
+        j = first + count - 1 - i
         out = []
         for f in range(fields):
             one, two = carry[f]
@@ -97,7 +95,7 @@
             out.append((v, one))
         return tuple(out)
 
-    return lax.fori_loop(0, cells, step, start, unroll=4)
+    return lax.fori_loop(0, count, step, start, unroll=4)
 
 
 def radial_sweeps(rad_ref, fields, rows, f, load, ahead, back, store=None):
@@ -148,7 +146,9 @@
         state_ref[f, 2], state_ref[f, 3] = carry[f]
 
 
-def patch_kernel(vec_ref, dis_ref, rad_ref, halo_ref, state_ref, reply_ref, out_ref, part_ref, end_ref):
+def patch_kernel(
+    vec_ref, dis_ref, rad_ref, halo_ref, state_ref, reply_ref, first_ref, second_ref, part_ref, end_ref, work_ref
+):
     fields, _, rows, width = state_ref.shape
     lane = lanes_of((rows, width))
     target = far_lane(width)
@@ -157,10 +157,13 @@
         part_ref[f] = h
         for m in range(4):
             extra = jnp.sum(h * reply_ref[f, m : m + 1], axis=1, keepdims=True)
-            out_ref[pl.ds((f * 4 + m) * rows, rows)] = state_ref[f, m] + jnp.where(lane == target, extra, 0.0)
+            tile = state_ref[f, m] + jnp.where(lane == target, extra, 0.0)
+            first_ref[f, m] = tile[: rows // 2]
+            second_ref[f, m] = tile[rows // 2 :]
+            work_ref[pl.ds((f * 4 + m) * rows, rows)] = tile
     for f in range(fields):
         ahead, back = radial_sweeps(
-            rad_ref, fields, rows, f, lambda i: out_ref[pl.ds(f * 4 * rows + i, 4, stride=rows)], None, None
+            rad_ref, fields, rows, f, lambda i: work_ref[pl.ds(f * 4 * rows + i, 4, stride=rows)], None, None
         )
         end_ref[f, 0:4] = ahead
         end_ref[f, 4:8] = back
@@ -178,7 +181,7 @@
             out_ref[pl.ds(pl.multiple_of((f * cells + j) * rows, rows), rows)] = tile
         return carry
 
-    lax.fori_loop(0, cells, step, 0, unroll=2)
+    lax.fori_loop(0, cells, step, 0, unroll=8)
     for f in range(fields):
         end_ref[f, 0], end_ref[f, 1] = radial_sweeps(
             rad_ref, fields, rows, f, lambda i: out_ref[pl.ds(f * cells * rows + i, cells, stride=rows)], None, None
@@ -191,28 +194,6 @@
         term = enter_ref[((target[0] * target[1] + m) * width + column) * fields + f] * value
         total = term if total is None else total + term
     return total
-
-
-def state_kernel(rad_enter_ref, rad_ref, *refs):
-    ends, (state_ref, first_ref, second_ref, work_ref) = refs[:-4], refs[-4:]
-    fields, _, half, width = first_ref.shape
-    rows = 2 * half
-    for f in range(fields):
-        pieces = [(2 * s + k, ends[s][f, 4 * k : 4 * k + 4]) for s in range(len(ends)) for k in range(2)]
-        ahead, back = (
-            weighted(rad_enter_ref, fields, f, 2 * len(ends), (0, 2), m, pieces) for m in range(2)
-        )
-
-        def store(i, value):
-            work_ref[pl.ds(f * 4 * rows + i, 4, stride=rows)] = value
-
-        radial_sweeps(
-            rad_ref, fields, rows, f, lambda i: state_ref[pl.ds(f * 4 * rows + i, 4, stride=rows)], ahead, back, store
-        )
-        for m in range(4):
-            at = (f * 4 + m) * rows
-            first_ref[f, m] = work_ref[pl.ds(at, half)]
-            second_ref[f, m] = work_ref[pl.ds(at + half, half)]
 
 
 def spread_kernel(count, size, near, far, enter_ref, *refs):
@@ -226,10 +207,20 @@
                 out_ref[f, m] = weighted(enter_ref, fields, f, size * count, (target, size), m, pieces)
 
 
-def spread_both(count, near, far, enter_ref, *refs):
-    ins, outs = refs[: len(near) + len(far)], refs[len(near) + len(far) :]
-    spread_kernel(count, 4, near, far, enter_ref, *ins[: len(near)], *outs[: len(far)])
-    spread_kernel(count, 4, far, near, enter_ref, *ins[len(near) :], *outs[len(far) :])
+def send_kernel(count, near, far, rads, enter_ref, rad_enter_ref, *refs):
+    firsts, refs = refs[: len(near)], refs[len(near) :]
+    seconds, refs = refs[: len(far)], refs[len(far) :]
+    ends, outs = refs[:rads], refs[rads:]
+    fields = ends[0].shape[0]
+    spread_kernel(count, 4, near, far, enter_ref, *firsts, *outs[: len(far)])
+    spread_kernel(count, 4, far, near, enter_ref, *seconds, *outs[len(far) : -1])
+    for f in range(fields):
+        pieces = [(2 * s + k, ends[s][f, 4 * k : 4 * k + 4]) for s in range(rads) for k in range(2)]
+        for m in range(2):
+            own = weighted(rad_enter_ref, fields, f, 2 * rads, (0, 2), m, pieces)
+            for out_ref in outs[:-1]:
+                out_ref[f, 4, 4 * m : 4 * m + 4] = own
+            outs[-1][f, 4 * m : 4 * m + 4] = own
 
 
 def radial_kernel(rad_ref, *refs):
@@ -254,17 +245,49 @@
         )
 
 
-def last_kernel(coef_ref, *refs):
-    parts, (src_ref, out_ref, z_ref) = refs[:-3], refs[-3:]
-    count = len(parts) // 2
+def last_kernel(firsts, seconds, steps, coef_ref, enter_ref, rad_ref, *refs):
+    parts, (src_ref, out_ref, z_ref, work_ref, held_ref, sems) = refs[:-6], refs[-6:]
     fields, cells, rows, width = src_ref.shape
-    entry = [
-        [
-            jnp.concatenate([sum(ref[f, m] for ref in parts[:count]), sum(ref[f, m] for ref in parts[count:])])
-            for m in range(4)
+    half = rows // 2
+    at = {s: i for i, s in reversed(list(enumerate(steps)))}
+    entry = []
+    for f in range(fields):
+        for m in range(4):
+            base = (f * 4 + m) * rows
+            work_ref[pl.ds(base, half)] = sum(ref[f, m] for ref in parts[:firsts])
+            work_ref[pl.ds(base + half, half)] = sum(ref[f, m] for ref in parts[firsts : firsts + seconds])
+
+        def row(s, k):
+            ref = parts[at[s]]
+            if at[s] < firsts + seconds:
+                return ref[f, 4, k : k + 1]
+            return ref[f, k : k + 1]
+
+        sides = [
+            jnp.concatenate(
+                [
+                    weighted(
+                        enter_ref,
+                        fields,
+                        f,
+                        4 * len(at),
+                        (0, 4),
+                        m,
+                        [(4 * s + k, row(s, 4 * side + k)) for s in range(len(at)) for k in range(4)],
+                    )
+                    for m in range(4)
+                ]
+            )
+            for side in range(2)
         ]
-        for f in range(fields)
-    ]
+
+        def store(i, value):
+            work_ref[pl.ds(f * 4 * rows + i, 4, stride=rows)] = value
+
+        radial_sweeps(
+            rad_ref, fields, rows, f, lambda i: work_ref[pl.ds(f * 4 * rows + i, 4, stride=rows)], *sides, store
+        )
+        entry.append([work_ref[pl.ds((f * 4 + m) * rows, rows)] for m in range(4)])
     lower_sweep(
         coef_ref,
         cells,
@@ -274,37 +297,31 @@
     )
 
     def store(f, j, value):
-        out_ref[f, j] = value
-
-    upper_sweep(coef_ref, cells, z_ref, tuple((e[2], e[3]) for e in entry), store)
-
-
-def azim_table_kernel(coef_ref, enter_ref, reply_ref):
+        held_ref[f, j] = value
+
+    chunks = sems.shape[0]
+    size = cells // chunks
+    carry = tuple((e[2], e[3]) for e in entry)
+    copies = []
+    for c in reversed(range(chunks)):
+        carry = upper_sweep(coef_ref, cells, z_ref, carry, store, c * size, size)
+        copies.append(
+            pltpu.make_async_copy(
+                held_ref.at[:, pl.ds(c * size, size)], out_ref.at[:, pl.ds(c * size, size)], sems.at[c]
+            )
+        )
+        copies[-1].start()
+    for copy in copies:
+        copy.wait()
+
+
+def weight(a, b):
+    return jnp.sqrt(1.0 - (a + b) * (a + b))
+
+
+def reply_kernel(coef_ref, reply_ref):
     _, blocks, cells, fields = coef_ref.shape
     own = lax.axis_index("azim")
-
-    def weight(a, b):
-        return jnp.sqrt(1.0 - (a + b) * (a + b))
-
-    unit = lax.broadcasted_iota(jnp.int32, (blocks, 8, fields), 1)
-
-    def ones(k):
-        return (unit == k).astype(f32)
-
-    one, two = ones(0), ones(1)
-    held = []
-    for j in range(cells):
-        z = coef_ref[0, :, j : j + 1] * one + coef_ref[1, :, j : j + 1] * two
-        held.append(z)
-        one, two = z, one
-    lower = (one, two)
-    one, two = ones(2), ones(3)
-    for j in reversed(range(cells)):
-        c, e = coef_ref[2, :, j : j + 1], coef_ref[3, :, j : j + 1]
-        v = weight(c, e) * held[j] + c * one + e * two
-        one, two = v, one
-    upper = (one, two)
-
     cell = lax.broadcasted_iota(jnp.int32, (cells, fields), 0)
     one = two = jnp.zeros((cells, fields), f32)
     held = []
@@ -320,6 +337,29 @@
         v = weight(c, e) * held[j] + c * one + e * two
         one, two = v, one
     reply_ref[2], reply_ref[3] = one, two
+
+
+def azim_table_kernel(coef_ref, enter_ref):
+    _, blocks, cells, fields = coef_ref.shape
+    own = lax.axis_index("azim")
+    unit = lax.broadcasted_iota(jnp.int32, (blocks, 8, fields), 1)
+
+    def ones(k):
+        return (unit == k).astype(f32)
+
+    one, two = ones(0), ones(1)
+    held = []
+    for j in range(cells):
+        z = coef_ref[0, :, j : j + 1] * one + coef_ref[1, :, j : j + 1] * two
+        held.append(z)
+        one, two = z, one
+    lower = (one, two)
+    one, two = ones(2), ones(3)
+    for j in reversed(range(cells)):
+        c, e = coef_ref[2, :, j : j + 1], coef_ref[3, :, j : j + 1]
+        v = weight(c, e) * held[j] + c * one + e * two
+        one, two = v, one
+    upper = (one, two)
 
     def entry(pair, p, m, k):
         return pair[m][p, k : k + 1]
@@ -440,20 +480,20 @@
     fields, cells, rows, width = residual.shape
     azim_count, rad_count = lax.axis_size("azim"), lax.axis_size("rad")
     whole, flat = (fields, cells, rows, width), (fields * cells * rows, width)
-    edge = call(edge_kernel, [(fields, rows, width)], 0, 1)(residual)[0]
-    halo = lax.ppermute(edge, "axial", [(0, 1), (1, 0)])
-
+    vec = left_vec.reshape(-1)
+    azim_blocks = azim_coef.reshape(4, fields, azim_count, cells).transpose(0, 2, 3, 1)
+    reply = call(reply_kernel, [(4, cells, fields)], 0, 1)(azim_blocks)[0]
+    reply = jnp.pad(reply.transpose(2, 0, 1), ((0, 0), (0, 0), (0, width - cells)))
     weights = jnp.sqrt(1.0 - (azim_coef[0::2] + azim_coef[1::2]) ** 2)
     kinds = jnp.concatenate([azim_coef[:2], weights[:1], azim_coef[2:], weights[1:]])
     own_azim = lax.dynamic_slice_in_dim(kinds, lax.axis_index("azim") * cells, cells, 2).reshape(-1)
-    azim_blocks = azim_coef.reshape(4, fields, azim_count, cells).transpose(0, 2, 3, 1)
-    azim_enter, reply = call(
-        azim_table_kernel,
-        [(len(targets_of(azim_count)), 4, 4 * azim_count, fields), (4, cells, fields)],
-        0,
-        1,
-    )(azim_blocks)
-    reply = jnp.pad(reply.transpose(2, 0, 1), ((0, 0), (0, 0), (0, width - cells)))
+
+    edge = call(edge_kernel, [(fields, rows, width)], 0, 1)(residual)[0]
+    halo = from_partner(edge, "axial", 1)
+
+    azim_enter = call(
+        azim_table_kernel, [(len(targets_of(azim_count)), 4, 4 * azim_count, fields)], 0, 1
+    )(azim_blocks)[0]
     own_rad, rad_enter = call(
         rad_table_kernel,
         [(4, rows, fields), (len(targets_of(rad_count)), 2, 2 * rad_count, fields)],
@@ -463,44 +503,59 @@
     )(radial_coef.transpose(0, 2, 1))
     azim_enter, rad_enter = azim_enter.reshape(-1), rad_enter.reshape(-1)
     own_rad = own_rad.transpose(0, 2, 1).reshape(-1)
-    vec = left_vec.reshape(-1)
-
-    four = (fields, 4, rows, width)
-    src, states = call(first_kernel, [whole, four], 3, 1, [whole])(own_azim, vec, dissip, residual)
-    states, part, small = call(
-        patch_kernel, [(fields * 4 * rows, width), (fields, rows, width), (fields, 8, width)], 3, 3
+
+    src, states = call(first_kernel, [whole, (fields, 4, rows, width)], 3, 1, [whole])(
+        own_azim, vec, dissip, residual
+    )
+    half = (fields, 4, rows // 2, width)
+    small = (fields, 8, width)
+    one, two, part, end = call(
+        patch_kernel, [half, half, (fields, rows, width), small], 3, 3, [(fields * 4 * rows, width)]
     )(vec, dissip, own_rad, halo, states, reply)
-    smalls = [from_partner(small, "rad", s) for s in range(rad_count)]
-    src, ends = call(source_kernel, [flat, (fields, 2, cells, width)], 1, 2)(own_rad, src, part)
-    half = (fields, 4, rows // 2, width)
-    one, two = call(state_kernel, [half, half], 2, rad_count + 1, [(fields * 4 * rows, width)])(
-        rad_enter, own_rad, *smalls, states
-    )
     low, high = low_high(azim_count)
     ones = [from_partner(one, "azim", s) for s in low]
     twos = [from_partner(two, "azim", s) for s in high]
 
+    smalls = [from_partner(end, "rad", s) for s in range(rad_count)]
+    src, ends = call(source_kernel, [flat, (fields, 2, cells, width)], 1, 2)(own_rad, src, part)
+
+    message = (fields, 5, rows // 2, width)
+    *sums, lone = call(
+        lambda *refs: send_kernel(azim_count, low, high, rad_count, *refs),
+        [message] * (len(low) + len(high)) + [small],
+        2,
+        len(low) + len(high) + rad_count,
+        cost=10**11,
+    )(azim_enter, rad_enter, *ones, *twos, *smalls)
     near, far = low_high(rad_count)
     gathered = [from_partner(ends, "rad", s) for s in near]
-    sums = call(
-        lambda *refs: spread_kernel(rad_count, 2, near, far, *refs), [ends.shape] * len(far), 1, len(near)
-    )(rad_enter, *gathered)
-    entry = [from_partner(value, "rad", s) for s, value in zip(far, sums)]
+    entry = call(
+        lambda enter_ref, after_ref, *refs: spread_kernel(rad_count, 2, near, far, enter_ref, *refs),
+        [ends.shape] * len(far),
+        1,
+        len(near) + 1,
+    )(rad_enter, lone, *gathered)
+    entry = [from_partner(value, "rad", s) for s, value in zip(far, entry)]
     src = call(radial_kernel, [flat], 1, len(far) + 1)(own_rad, *entry, src)[0]
 
-    sums = call(
-        lambda *refs: spread_both(azim_count, low, high, *refs),
-        [half] * (len(low) + len(high)),
-        1,
-        len(low) + len(high),
-    )(azim_enter, *ones, *twos)
-    ones = [from_partner(value, "azim", s) for s, value in zip(high, sums[: len(high)])]
-    twos = [from_partner(value, "azim", s) for s, value in zip(low, sums[len(high) :])]
-    ones = ones + [jnp.zeros_like(one)] * (max(len(low), len(high)) - len(high))
-    twos = twos + [jnp.zeros_like(two)] * (max(len(low), len(high)) - len(low))
-    return call(last_kernel, [whole], 1, len(ones) + len(twos) + 1, [whole])(
-        own_azim, *ones, *twos, src.reshape(whole)
-    )[0]
+    rest = [s for s in range(azim_count) if s not in low + high]
+    parts = [from_partner(value, "azim", s) for s, value in zip(high + low, sums)]
+    parts += [from_partner(lone, "azim", s) for s in rest]
+
+    chunks = 4
+    return pl.pallas_call(
+        lambda *refs: last_kernel(len(high), len(low), high + low + rest, *refs),
+        out_shape=jax.ShapeDtypeStruct(whole, f32),
+        in_specs=[SMEM] * 3 + [VMEM] * (len(parts) + 1),
+        out_specs=pl.BlockSpec(memory_space=pl.ANY),
+        scratch_shapes=[
+            pltpu.VMEM(whole, f32),
+            pltpu.VMEM((fields * 4 * rows, width), f32),
+            pltpu.VMEM(whole, f32),
+            pltpu.SemaphoreType.DMA((chunks,)),
+        ],
+        compiler_params=params,
+    )(own_azim, azim_enter, own_rad, *parts, src.reshape(whole))
 
 
 def solution(mesh):

time: 38 us -> 33.1 us (0.87)
  waiting for transfers between devices: 7.98 us -> 2.73 us
  starting transfers between devices: 13.1 us -> 15.3 us
  Pallas kernels: 14 us -> 12.3 us
    ppermute x9 -> x11, waiting for transfers between devices: 7.98 us -> 2.73 us  [from_partner(): lax.ppermute(values, axis, [(i, i ^ step) for i in range(lax.axis_size(ax...]
    ppermute x9 -> x11, starting transfers between devices: 10.1 us -> 15.3 us  [from_partner(): lax.ppermute(values, axis, [(i, i ^ step) for i in range(lax.axis_size(ax...]
    ppermute x1 -> x0, starting transfers between devices: 3.03 us -> none  [local(): halo = lax.ppermute(edge, 'axial', [(0, 1), (1, 0)])]
    pallas_call x1, Pallas kernels: 2.56 us -> 1.71 us  [local(): call(source_kernel, [flat, (fields, 2, cells, width)], 1, 2)]
    pallas_call x1, Pallas kernels: 0.91 us -> 0.42 us  [local(): edge = call(edge_kernel, [(fields, rows, width)], 0, 1)(residual)[0]]
  transfers between devices with their start and end apart: 10 -> 11, of which waited for: 5 -> 3; matrix products, arithmetic and copies ran while one was open for 3% -> 4% of each run, Pallas kernels for 19% -> 23%
where the time goes in v3:
time: 33.1 us; the launch traced here: 33 us
  starting transfers between devices  15.3 us (46%)
  Pallas kernels  12.3 us (37%)
  waiting for transfers between devices  2.73 us (8%)
  local copies, waits for them, and re-layouts  2.41 us (7%)
    ppermute x11, starting transfers between devices, from_partner(): lax.ppermute(values, axis, [(i, i ^ step) for i in range(lax.axis_size(ax...  15.3 us
    ppermute x11, waiting for transfers between devices, from_partner(): lax.ppermute(values, axis, [(i, i ^ step) for i in range(lax.axis_size(ax...  2.73 us
    pallas_call x1, Pallas kernels, local(): pl.pallas_call(lambda *refs: last_kernel(len(high), len(low), high + low...  2.66 us
    pallas_call x1, Pallas kernels, local(): call(first_kernel, [whole, (fields, 4, rows, width)], 3, 1, [whole])  2.3 us
    pallas_call x1, Pallas kernels, local(): call(source_kernel, [flat, (fields, 2, cells, width)], 1, 2)  1.71 us
    unnamed x14, local copies, waits for them, and re-layouts  1.59 us
    pallas_call x1, Pallas kernels, local(): src = call(radial_kernel, [flat], 1, len(far) + 1)(own_rad, *entry, src)[0]  1.38 us
    pallas_call x1, Pallas kernels, local(): call(lambda *refs: send_kernel(azim_count, low, high, rad_count, *refs),...  0.9 us
  transfers between devices with their start and end apart: 11, of which 3 were waited for; matrix products, arithmetic and copies ran while one was open for 4% of the time, Pallas kernels for 23%

profile of v3, /device:TPU:0, one launch (start us, length us, event | category | flops | bytes accessed | tf_op | source)
XLA Modules:
  0.0 33.0 jit_solution(12015246473832569708)
XLA Ops:
  0.0 1.3 %copy-done = f32[5,32,16,128]{3,2,1,0:T(8,128)S(1)} copy-done((f32[5,32,16,128]{3,2,1,0:T(8,128)S(1)}, f32[5,32,16,128]{3,2,1,0:T(8,128)}, u32[]{:S(2)}) %copy-start) | copy-done | bytes 1310744
  1.3 0.4 %shard_map.57 = f32[5,16,128]{2,1,0:T(8,128)S(1)} custom-call(f32[5,32,16,128]{3,2,1,0:T(8,128)S(1)} %copy-done), custom_call_target="tpu_custom_call" | custom-call | tf_op jit(solution)/shard_map/pallas_call | solution.py:491
  1.8 3.0 %collective-permute-start = (f32[5,16,128]{2,1,0:T(8,128)S(1)}, f32[5,16,128]{2,1,0:T(8,128)S(1)}, u32[]{:S(2)}, u32[]{:S(2)}) collective-permute-start(f32[5,16,128]{2,1,0:T(8,128)S(1)} %shard_map.57), channel_id=1, source_target_pairs={{0,1},{1,0},{2,3},{3,2},{4,5},{5,4},{6,7},{7,6},{8,9},{9,8},{10,11... | collective-permute-start | bytes 122888 | tf_op jit(solution)/shard_map/ppermute | solution.py:476
  5.0 0.1 copy.10
  5.3 0.1 copy.11
  5.4 0.7 %shard_map.56 = (f32[4,16,5]{2,1,0:T(8,128)S(1)}, f32[3,2,8,5]{3,2,1,0:T(8,128)S(1)}) custom-call(f32[2,64,5]{2,1,0:T(8,128)S(1)} %bitcast.14), custom_call_target="tpu_custom_call" | custom-call | tf_op jit(solution)/shard_map/pallas_call | solution.py:497
  6.1 0.1 copy.12
  6.3 0.3 shard_map.59
  6.6 0.1 copy.13
  6.7 2.3 %shard_map.58 = (f32[5,32,16,128]{3,2,1,0:T(8,128)S(1)}, f32[5,4,16,128]{3,2,1,0:T(8,128)S(1)}) custom-call(f32[960]{0:T(1024)S(1)} %reshape.21.coef_ref.refs_0_, f32[25]{0:T(128)S(1)} %reshape.26.vec_ref, f32[5]{0:T(128)S(1)} %copy-done.2, f32[5,32,16,128]{3,2,1,0:T(8,128)S(1)} %copy-done.1), custom_call_target="tpu_custom_call" | custom-call | tf_op jit(solution)/shard_map/pallas_call | solution.py:507
  9.0 0.8 %shard_map.60 = (f32[5,4,8,128]{3,2,1,0:T(8,128)S(1)}, f32[5,4,8,128]{3,2,1,0:T(8,128)S(1)}, f32[5,16,128]{2,1,0:T(8,128)S(1)}, f32[5,8,128]{2,1,0:T(8,128)S(1)}) custom-call(f32[25]{0:T(128)S(1)} %reshape.26.vec_ref, f32[5]{0:T(128)S(1)} %copy-done.2, f32[320]{0:T(512)S(1)} %reshape.24.rad_ref.refs_2_, f32[5,16,128]{2,1,0:T(8,128)S(1)} %collective-permute-done.halo_ref, ...), custom_call_target="tpu_custom_call" | custom-call | tf_op jit(solution)/shard_map/pallas_call | solution.py:512
  9.9 1.6 %collective-permute-start.1 = (f32[5,4,8,128]{3,2,1,0:T(8,128)S(1)}, f32[5,4,8,128]{3,2,1,0:T(8,128)S(1)}, u32[]{:S(2)}, u32[]{:S(2)}) collective-permute-start(f32[5,4,8,128]{3,2,1,0:T(8,128)S(1)} %get-tuple-element.25.refs_2_), channel_id=1, source_target_pairs={{0,8},{8,0},{16,24},{24,16},{1,9},{9,1},{17,25},{25,17},{2,10},{10... | collective-permute-start | bytes 245768 | tf_op jit(solution)/shard_map/ppermute | solution.py:476
  11.5 2.6 %collective-permute-start.2 = (f32[5,4,8,128]{3,2,1,0:T(8,128)S(1)}, f32[5,4,8,128]{3,2,1,0:T(8,128)S(1)}, u32[]{:S(2)}, u32[]{:S(2)}) collective-permute-start(f32[5,4,8,128]{3,2,1,0:T(8,128)S(1)} %get-tuple-element.26.refs_4_), channel_id=1, source_target_pairs={{0,16},{8,24},{16,0},{24,8},{1,17},{9,25},{17,1},{25,9},{2,18},{10... | collective-permute-start | bytes 245768 | tf_op jit(solution)/shard_map/ppermute | solution.py:476
  14.1 0.1 collective-permute-start.5
  14.2 1.4 %collective-permute-start.4 = (f32[5,8,128]{2,1,0:T(8,128)S(1)}, f32[5,8,128]{2,1,0:T(8,128)S(1)}, u32[]{:S(2)}, u32[]{:S(2)}) collective-permute-start(f32[5,8,128]{2,1,0:T(8,128)S(1)} %get-tuple-element.27.refs_6_), channel_id=1, source_target_pairs={{0,4},{2,6},{4,0},{6,2},{1,5},{3,7},{5,1},{7,3},{8,12},{10,14},{12... | collective-permute-start | bytes 61448 | tf_op jit(solution)/shard_map/ppermute | solution.py:476
  15.6 0.3 %collective-permute-start.3 = (f32[5,8,128]{2,1,0:T(8,128)S(1)}, f32[5,8,128]{2,1,0:T(8,128)S(1)}, u32[]{:S(2)}, u32[]{:S(2)}) collective-permute-start(f32[5,8,128]{2,1,0:T(8,128)S(1)} %get-tuple-element.27.refs_6_), channel_id=1, source_target_pairs={{0,2},{2,0},{4,6},{6,4},{1,3},{3,1},{5,7},{7,5},{8,10},{10,8},{12,... | collective-permute-start | bytes 61448 | tf_op jit(solution)/shard_map/ppermute | solution.py:476
  16.0 0.5 %shard_map.55 = f32[3,4,16,5]{3,2,1,0:T(8,128)S(1)} custom-call(f32[4,4,32,5]{3,2,1,0:T(8,128)S(1)} %bitcast.13), custom_call_target="tpu_custom_call" | custom-call | tf_op jit(solution)/shard_map/pallas_call | solution.py:494
  16.4 0.1 reshape.25.refs_1_.enter_ref
  16.5 0.2 reshape.23.refs_0_.refs_1_
  16.8 1.7 %shard_map.62 = (f32[2560,128]{1,0:T(8,128)S(1)}, f32[5,2,32,128]{3,2,1,0:T(8,128)S(1)}) custom-call(f32[320]{0:T(512)S(1)} %reshape.24.rad_ref.refs_2_, f32[5,32,16,128]{3,2,1,0:T(8,128)S(1)} %get-tuple-element.33.src_ref, f32[5,16,128]{2,1,0:T(8,128)S(1)} %get-tuple-element.34.part_ref), custom_call_target="tpu_custom_call" | custom-call | tf_op jit(solution)/shard_map/pallas_call | solution.py:520
  18.5 0.2 collective-permute-start.9
  18.7 0.9 %shard_map.61 = (f32[5,5,8,128]{3,2,1,0:T(8,128)S(1)}, f32[5,5,8,128]{3,2,1,0:T(8,128)S(1)}, f32[5,5,8,128]{3,2,1,0:T(8,128)S(1)}, f32[5,5,8,128]{3,2,1,0:T(8,128)S(1)}, f32[5,8,128]{2,1,0:T(8,128)S(1)}) custom-call(f32[960]{0:T(1024)S(1)} %reshape.23.refs_0_.refs_1_, f32[240]{0:T(256)S(1)} %reshape.25.refs_1_.enter_ref, ...), custom_call_target="tpu_custom_call" | custom-call | flops 99999997952 | tf_op jit(solution)/shard_map/pallas_call | solution.py:523
  19.6 0.3 collective-permute-done.9.refs_1_
  19.9 0.6 %shard_map.63 = (f32[5,2,32,128]{3,2,1,0:T(8,128)S(1)}, f32[5,2,32,128]{3,2,1,0:T(8,128)S(1)}) custom-call(f32[240]{0:T(256)S(1)} %reshape.25.refs_1_.enter_ref, f32[5,8,128]{2,1,0:T(8,128)S(1)} %get-tuple-element.32.after_ref, f32[5,2,32,128]{3,2,1,0:T(8,128)S(1)} %get-tuple-element.35.refs_0_, f32[5,2,32,128]{3,2,1,0:T(8,128)S(1)} %collective-permute-done.9.refs_1_), custom_call_target="tpu_custom_call" | custom-call | tf_op jit(solution)/shard_map/pallas_call | solution.py:532
  20.6 1.6 %collective-permute-start.10 = (f32[5,2,32,128]{3,2,1,0:T(8,128)S(1)}, f32[5,2,32,128]{3,2,1,0:T(8,128)S(1)}, u32[]{:S(2)}, u32[]{:S(2)}) collective-permute-start(f32[5,2,32,128]{3,2,1,0:T(8,128)S(1)} %get-tuple-element.37), channel_id=1, source_target_pairs={{0,4},{2,6},{4,0},{6,2},{1,5},{3,7},{5,1},{7,3},{8,12},{10,14},{12... | collective-permute-start | bytes 491528 | tf_op jit(solution)/shard_map/ppermute | solution.py:476
  22.1 0.5 %collective-permute-start.6 = (f32[5,5,8,128]{3,2,1,0:T(8,128)S(1)}, f32[5,5,8,128]{3,2,1,0:T(8,128)S(1)}, u32[]{:S(2)}, u32[]{:S(2)}) collective-permute-start(f32[5,5,8,128]{3,2,1,0:T(8,128)S(1)} %get-tuple-element.29), channel_id=1, source_target_pairs={{0,16},{8,24},{16,0},{24,8},{1,17},{9,25},{17,1},{25,9},{2,18},{10... | collective-permute-start | bytes 307208 | tf_op jit(solution)/shard_map/ppermute | solution.py:476
  22.6 0.6 %collective-permute-start.7 = (f32[5,5,8,128]{3,2,1,0:T(8,128)S(1)}, f32[5,5,8,128]{3,2,1,0:T(8,128)S(1)}, u32[]{:S(2)}, u32[]{:S(2)}) collective-permute-start(f32[5,5,8,128]{3,2,1,0:T(8,128)S(1)} %get-tuple-element.31), channel_id=1, source_target_pairs={{0,8},{8,0},{16,24},{24,16},{1,9},{9,1},{17,25},{25,17},{2,10},{10... | collective-permute-start | bytes 307208 | tf_op jit(solution)/shard_map/ppermute | solution.py:476
  23.2 3.3 %collective-permute-start.8 = (f32[5,8,128]{2,1,0:T(8,128)S(1)}, f32[5,8,128]{2,1,0:T(8,128)S(1)}, u32[]{:S(2)}, u32[]{:S(2)}) collective-permute-start(f32[5,8,128]{2,1,0:T(8,128)S(1)} %get-tuple-element.32.after_ref), channel_id=1, source_target_pairs={{0,24},{8,16},{16,8},{24,0},{1,25},{9,17},{17,9},{25,1},{2,26},{10... | collective-permute-start | bytes 61448 | tf_op jit(solution)/shard_map/ppermute | solution.py:476
  26.5 0.4 %collective-permute-done.10.refs_1_ = f32[5,2,32,128]{3,2,1,0:T(8,128)S(1)} collective-permute-done((f32[5,2,32,128]{3,2,1,0:T(8,128)S(1)}, f32[5,2,32,128]{3,2,1,0:T(8,128)S(1)}, u32[]{:S(2)}, u32[]{:S(2)}) %collective-permute-start.10) | collective-permute-done | bytes 163872 | tf_op jit(solution)/shard_map/ppermute | solution.py:476
  26.9 1.4 %shard_map.64 = f32[2560,128]{1,0:T(8,128)S(1)} custom-call(f32[320]{0:T(512)S(1)} %reshape.24.rad_ref.refs_2_, f32[5,2,32,128]{3,2,1,0:T(8,128)S(1)} %get-tuple-element.36.refs_0_, f32[5,2,32,128]{3,2,1,0:T(8,128)S(1)} %collective-permute-done.10.refs_1_, f32[2560,128]{1,0:T(8,128)S(1)} %get-tuple-element.38.refs_2_), custom_call_target="tpu_custom_call" | custom-call | tf_op jit(solution)/shard_map/pallas_call | solution.py:539
  28.3 2.0 %collective-permute-done.8.refs_7_ = f32[5,8,128]{2,1,0:T(8,128)S(1)} collective-permute-done((f32[5,8,128]{2,1,0:T(8,128)S(1)}, f32[5,8,128]{2,1,0:T(8,128)S(1)}, u32[]{:S(2)}, u32[]{:S(2)}) %collective-permute-start.8) | collective-permute-done | bytes 20512 | tf_op jit(solution)/shard_map/ppermute | solution.py:476
  30.3 2.7 %shard_map.65 = f32[5,32,16,128]{3,2,1,0:T(8,128)} custom-call(f32[960]{0:T(1024)S(1)} %reshape.21.coef_ref.refs_0_, f32[960]{0:T(1024)S(1)} %reshape.23.refs_0_.refs_1_, f32[320]{0:T(512)S(1)} %reshape.24.rad_ref.refs_2_, f32[5,5,8,128]{3,2,1,0:T(8,128)S(1)} %get-tuple-element.28.refs_3_, f32[5,5,8,128]{3,2,1,0:T(8,128)S(1)} %collective-permute-done.6.refs_4_, ...), custom_call_target="tpu_custom_call" | custom-call | tf_op jit(solution)/shard_map/pallas_call | solution.py:546
  (30 shorter events, 0.5 us)
Async XLA Ops:
  0.0 1.3 %copy-start = (f32[5,32,16,128]{3,2,1,0:T(8,128)S(1)}, f32[5,32,16,128]{3,2,1,0:T(8,128)}, u32[]{:S(2)}) copy-start(f32[5,32,16,128]{3,2,1,0:T(8,128)} %res_ref.3) | copy-start | bytes 3932164
  1.3 3.5 %copy-start.3 = (f32[4,5,128]{2,0,1:T(4,128)S(1)}, f32[4,5,128]{2,0,1:T(4,128)}, u32[]{:S(2)}) copy-start(f32[4,5,128]{2,0,1:T(4,128)} %param.8) | copy-start | bytes 30724
  1.3 3.8 %copy-start.5 = (f32[5,5]{1,0:T(8,128)S(1)}, f32[5,5]{1,0:T(8,128)}, u32[]{:S(2)}) copy-start(f32[5,5]{1,0:T(8,128)} %param.6) | copy-start | bytes 304
  1.3 4.0 %copy-start.4 = (f32[2,5,64]{2,0,1:T(2,128)S(1)}, f32[2,5,64]{2,0,1:T(2,128)}, u32[]{:S(2)}) copy-start(f32[2,5,64]{2,0,1:T(2,128)} %param.9) | copy-start | bytes 7684
  1.3 5.4 %copy-start.1 = (f32[5,32,16,128]{3,2,1,0:T(8,128)S(1)}, f32[5,32,16,128]{3,2,1,0:T(8,128)}, u32[]{:S(2)}) copy-start(f32[5,32,16,128]{3,2,1,0:T(8,128)} %res_ref.3) | copy-start | bytes 3932164
  1.3 5.4 %copy-start.2 = (f32[5]{0:T(128)S(1)}, f32[5]{0:T(128)}, u32[]{:S(2)}) copy-start(f32[5]{0:T(128)} %dis_ref.3) | copy-start | bytes 64
  1.8 7.3 %collective-permute-start = (f32[5,16,128]{2,1,0:T(8,128)S(1)}, f32[5,16,128]{2,1,0:T(8,128)S(1)}, u32[]{:S(2)}, u32[]{:S(2)}) collective-permute-start(f32[5,16,128]{2,1,0:T(8,128)S(1)} %shard_map.57), channel_id=1, source_target_pairs={{0,1},{1,0},{2,3},{3,2},{4,5},{5,4},{6,7},{7,6},{8,9},{9,8},{10,11... | collective-permute-start | bytes 122888 | tf_op jit(solution)/shard_map/ppermute | solution.py:476
  9.9 8.8 %collective-permute-start.1 = (f32[5,4,8,128]{3,2,1,0:T(8,128)S(1)}, f32[5,4,8,128]{3,2,1,0:T(8,128)S(1)}, u32[]{:S(2)}, u32[]{:S(2)}) collective-permute-start(f32[5,4,8,128]{3,2,1,0:T(8,128)S(1)} %get-tuple-element.25.refs_2_), channel_id=1, source_target_pairs={{0,8},{8,0},{16,24},{24,16},{1,9},{9,1},{17,25},{25,17},{2,10},{10... | collective-permute-start | bytes 245768 | tf_op jit(solution)/shard_map/ppermute | solution.py:476
  11.5 7.2 %collective-permute-start.2 = (f32[5,4,8,128]{3,2,1,0:T(8,128)S(1)}, f32[5,4,8,128]{3,2,1,0:T(8,128)S(1)}, u32[]{:S(2)}, u32[]{:S(2)}) collective-permute-start(f32[5,4,8,128]{3,2,1,0:T(8,128)S(1)} %get-tuple-element.26.refs_4_), channel_id=1, source_target_pairs={{0,16},{8,24},{16,0},{24,8},{1,17},{9,25},{17,1},{25,9},{2,18},{10... | collective-permute-start | bytes 245768 | tf_op jit(solution)/shard_map/ppermute | solution.py:476
  14.1 4.4 %collective-permute-start.5 = (f32[5,8,128]{2,1,0:T(8,128)S(1)}, f32[5,8,128]{2,1,0:T(8,128)S(1)}, u32[]{:S(2)}, u32[]{:S(2)}) collective-permute-start(f32[5,8,128]{2,1,0:T(8,128)S(1)} %get-tuple-element.27.refs_6_), channel_id=1, source_target_pairs={{0,6},{2,4},{4,2},{6,0},{1,7},{3,5},{5,3},{7,1},{8,14},{10,12},{12... | collective-permute-start | bytes 61448 | tf_op jit(solution)/shard_map/ppermute | solution.py:476
  14.2 4.5 %collective-permute-start.4 = (f32[5,8,128]{2,1,0:T(8,128)S(1)}, f32[5,8,128]{2,1,0:T(8,128)S(1)}, u32[]{:S(2)}, u32[]{:S(2)}) collective-permute-start(f32[5,8,128]{2,1,0:T(8,128)S(1)} %get-tuple-element.27.refs_6_), channel_id=1, source_target_pairs={{0,4},{2,6},{4,0},{6,2},{1,5},{3,7},{5,1},{7,3},{8,12},{10,14},{12... | collective-permute-start | bytes 61448 | tf_op jit(solution)/shard_map/ppermute | solution.py:476
  15.6 3.1 %collective-permute-start.3 = (f32[5,8,128]{2,1,0:T(8,128)S(1)}, f32[5,8,128]{2,1,0:T(8,128)S(1)}, u32[]{:S(2)}, u32[]{:S(2)}) collective-permute-start(f32[5,8,128]{2,1,0:T(8,128)S(1)} %get-tuple-element.27.refs_6_), channel_id=1, source_target_pairs={{0,2},{2,0},{4,6},{6,4},{1,3},{3,1},{5,7},{7,5},{8,10},{10,8},{12,... | collective-permute-start | bytes 61448 | tf_op jit(solution)/shard_map/ppermute | solution.py:476
  18.5 1.5 %collective-permute-start.9 = (f32[5,2,32,128]{3,2,1,0:T(8,128)S(1)}, f32[5,2,32,128]{3,2,1,0:T(8,128)S(1)}, u32[]{:S(2)}, u32[]{:S(2)}) collective-permute-start(f32[5,2,32,128]{3,2,1,0:T(8,128)S(1)} %get-tuple-element.35.refs_0_), channel_id=1, source_target_pairs={{0,2},{2,0},{4,6},{6,4},{1,3},{3,1},{5,7},{7,5},{8,10},{10,8},{12,... | collective-permute-start | bytes 491528 | tf_op jit(solution)/shard_map/ppermute | solution.py:476
  20.6 6.3 %collective-permute-start.10 = (f32[5,2,32,128]{3,2,1,0:T(8,128)S(1)}, f32[5,2,32,128]{3,2,1,0:T(8,128)S(1)}, u32[]{:S(2)}, u32[]{:S(2)}) collective-permute-start(f32[5,2,32,128]{3,2,1,0:T(8,128)S(1)} %get-tuple-element.37), channel_id=1, source_target_pairs={{0,4},{2,6},{4,0},{6,2},{1,5},{3,7},{5,1},{7,3},{8,12},{10,14},{12... | collective-permute-start | bytes 491528 | tf_op jit(solution)/shard_map/ppermute | solution.py:476
  22.1 8.2 %collective-permute-start.6 = (f32[5,5,8,128]{3,2,1,0:T(8,128)S(1)}, f32[5,5,8,128]{3,2,1,0:T(8,128)S(1)}, u32[]{:S(2)}, u32[]{:S(2)}) collective-permute-start(f32[5,5,8,128]{3,2,1,0:T(8,128)S(1)} %get-tuple-element.29), channel_id=1, source_target_pairs={{0,16},{8,24},{16,0},{24,8},{1,17},{9,25},{17,1},{25,9},{2,18},{10... | collective-permute-start | bytes 307208 | tf_op jit(solution)/shard_map/ppermute | solution.py:476
  22.6 7.7 %collective-permute-start.7 = (f32[5,5,8,128]{3,2,1,0:T(8,128)S(1)}, f32[5,5,8,128]{3,2,1,0:T(8,128)S(1)}, u32[]{:S(2)}, u32[]{:S(2)}) collective-permute-start(f32[5,5,8,128]{3,2,1,0:T(8,128)S(1)} %get-tuple-element.31), channel_id=1, source_target_pairs={{0,8},{8,0},{16,24},{24,16},{1,9},{9,1},{17,25},{25,17},{2,10},{10... | collective-permute-start | bytes 307208 | tf_op jit(solution)/shard_map/ppermute | solution.py:476
  23.2 7.1 %collective-permute-start.8 = (f32[5,8,128]{2,1,0:T(8,128)S(1)}, f32[5,8,128]{2,1,0:T(8,128)S(1)}, u32[]{:S(2)}, u32[]{:S(2)}) collective-permute-start(f32[5,8,128]{2,1,0:T(8,128)S(1)} %get-tuple-element.32.after_ref), channel_id=1, source_target_pairs={{0,24},{8,16},{16,8},{24,0},{1,25},{9,17},{17,9},{25,1},{2,26},{10... | collective-permute-start | bytes 61448 | tf_op jit(solution)/shard_map/ppermute | solution.py:476

commit v4 on v3

v4 whole, which is shorter than its diff:
```python
import jax
import jax.numpy as jnp
from jax import lax
from jax.experimental import pallas as pl
from jax.experimental.pallas import tpu as pltpu
from jax.sharding import PartitionSpec as P

f32 = jnp.float32
VMEM = pl.BlockSpec(memory_space=pltpu.VMEM)
params = pltpu.CompilerParams(vmem_limit_bytes=32 * 1024 * 1024)


def call(body, outs, *operands, scratch=(), cost=0):
    return pl.pallas_call(
        body,
        out_shape=[jax.ShapeDtypeStruct(shape, f32) for shape in outs],
        in_specs=[VMEM] * len(operands),
        out_specs=[VMEM] * len(outs),
        scratch_shapes=[pltpu.VMEM(shape, f32) for shape in scratch],
        compiler_params=params,
        cost_estimate=pl.CostEstimate(flops=cost, bytes_accessed=0, transcendentals=0),
    )(*operands)


def over_lanes(column, width):
    return jnp.broadcast_to(column, (column.shape[0], width))


def lanes_of(shape):
    return lax.broadcasted_iota(jnp.int32, shape, len(shape) - 1)


def low_high(count):
    split = 1 << ((count.bit_length() - 1) // 2)
    return list(range(split)), list(range(0, count, split))


def targets_of(count):
    low, high = low_high(count)
    return low + high[1:]


def far_lane(width):
    return jnp.where(lax.axis_index("axial") == 0, width - 1, 0)


def edge_kernel(res_ref, edge_ref):
    fields, cells, rows, width = res_ref.shape
    source = far_lane(width)
    lane = lanes_of((rows, width))
    packed = [jnp.zeros((rows, width), f32)] * fields
    for j in range(cells):
        for f in range(fields):
            moved = pltpu.roll(res_ref[f, j], (j - source + width) % width, 1)
            packed[f] = jnp.where(lane == j, moved, packed[f])
    for f in range(fields):
        edge_ref[f] = packed[f]


def lower_sweep(coef_ref, cells, load, z_ref, start):
    fields = len(start)

    def step(j, carry):
        source = load(j)
        out = []
        for f in range(fields):
            one, two = carry[f]
            a, b, w = (coef_ref[kind, j, f : f + 1] for kind in range(3))
            z = w * source[f] + b * two + a * one
            z_ref[f, j] = z
            out.append((z, one))
        return tuple(out)

    return lax.fori_loop(0, cells, step, start, unroll=8)


def upper_sweep(coef_ref, cells, z_ref, start, store=None, first=0, count=None):
    fields = len(start)
    count = cells if count is None else count

    def step(i, carry):
        j = first + count - 1 - i
        out = []
        for f in range(fields):
            one, two = carry[f]
            c, e, w = (coef_ref[kind, j, f : f + 1] for kind in range(3, 6))
            v = w * z_ref[f, j] + e * two + c * one
            if store is not None:
                store(f, j, v)
            out.append((v, one))
        return tuple(out)

    return lax.fori_loop(0, count, step, start, unroll=8)


def radial_sweeps(rad_ref, f, load, ahead, back, store):
    rows = rad_ref.shape[2]

    def coef(kind, i):
        return rad_ref[f, kind, i : i + 1]

    held = []
    for i in range(rows):
        ahead = coef(0, i) * load(i) + coef(1, i) * ahead
        held.append(ahead)
    for i in reversed(range(rows)):
        back = coef(2, i) * held[i] + coef(3, i) * back
        store(i, back)


def radial_ends(rad_ref, f, load):
    last = first = None
    for i in range(rad_ref.shape[2]):
        line = load(i)
        to_last = rad_ref[f, 4, i : i + 1] * line
        to_first = rad_ref[f, 5, i : i + 1] * line
        last = to_last if last is None else last + to_last
        first = to_first if first is None else first + to_first
    return last, first


def mix(mix_ref, values):
    fields = len(values)
    return [sum(mix_ref[f, g : g + 1] * values[f] for f in range(fields)) for g in range(fields)]


def first_kernel(coef_ref, mix_ref, res_ref, src_ref, state_ref, z_ref):
    fields, cells, rows, width = res_ref.shape
    lane = lanes_of((rows, width))

    def load(j):
        out = []
        for f, c in enumerate(mix(mix_ref, [res_ref[f, j] for f in range(fields)])):
            beside = jnp.where(lane == 0, 0.0, pltpu.roll(c, 1, 1)) + jnp.where(
                lane == width - 1, 0.0, pltpu.roll(c, width - 1, 1)
            )
            src = mix_ref[fields + 1, f : f + 1] * c + mix_ref[fields, f : f + 1] * beside
            src_ref[f, j] = src
            out.append(src)
        return out

    state_ref[...] = jnp.zeros(state_ref.shape, f32)
    start = tuple((state_ref[f, 0], state_ref[f, 1]) for f in range(fields))
    carry = lower_sweep(coef_ref, cells, load, z_ref, start)
    for f in range(fields):
        state_ref[f, 0], state_ref[f, 1] = carry[f]
    start = tuple((state_ref[f, 2], state_ref[f, 3]) for f in range(fields))
    carry = upper_sweep(coef_ref, cells, z_ref, start)
    for f in range(fields):
        state_ref[f, 2], state_ref[f, 3] = carry[f]


def patch_kernel(
    mix_ref, rad_ref, halo_ref, state_ref, reply_ref, first_ref, second_ref, part_ref, end_ref, work_ref
):
    fields, _, rows, width = state_ref.shape
    lane = lanes_of((rows, width))
    target = far_lane(width)
    for f, h in enumerate(mix(mix_ref, [halo_ref[f] for f in range(fields)])):
        h = mix_ref[fields, f : f + 1] * h
        part_ref[f] = h
        for m in range(4):
            extra = jnp.sum(h * reply_ref[m, f : f + 1], axis=1, keepdims=True)
            tile = state_ref[f, m] + jnp.where(lane == target, extra, 0.0)
            first_ref[f, m] = tile[: rows // 2]
            second_ref[f, m] = tile[rows // 2 :]
            work_ref[pl.ds((f * 4 + m) * rows, rows)] = tile
    for f in range(fields):
        end_ref[f, 0:4], end_ref[f, 4:8] = radial_ends(
            rad_ref, f, lambda i: work_ref[pl.ds(f * 4 * rows + i, 4, stride=rows)]
        )


def source_kernel(rad_ref, src_ref, part_ref, end_ref, turn_ref):
    fields, _, cells, width = end_ref.shape
    rows = part_ref.shape[1]
    lane = lanes_of((cells, width))
    target = far_lane(width)
    turn_ref[...] = jnp.zeros(turn_ref.shape, f32)
    for f in range(fields):
        ends = radial_ends(rad_ref, f, lambda i: part_ref[f, i : i + 1])
        turn_ref[2 * f : 2 * f + 1], turn_ref[2 * f + 1 : 2 * f + 2] = ends
    turned = jnp.transpose(turn_ref[...])[:cells]
    for f in range(fields):
        ends = radial_ends(
            rad_ref, f, lambda i: src_ref[pl.ds(f * cells * rows + i, cells, stride=rows)]
        )
        for k in range(2):
            moved = pltpu.roll(turned, (target - (2 * f + k) + width) % width, 1)
            end_ref[f, k] = ends[k] + jnp.where(lane == target, moved, 0.0)


def weighted(enter_ref, f, target, m, pieces):
    total = None
    for column, value in pieces:
        term = enter_ref[f, target, m, column : column + 1] * value
        total = term if total is None else total + term
    return total


def spread_kernel(count, size, near, far, enter_ref, *refs):
    arrays, sums = refs[: len(near)], refs[len(near) :]
    fields = sums[0].shape[0]
    for s, out_ref in zip(far, sums):
        target = targets_of(count).index(s)
        for f in range(fields):
            pieces = [(size * n + k, ref[f, k]) for n, ref in zip(near, arrays) for k in range(size)]
            for m in range(size):
                out_ref[f, m] = weighted(enter_ref, f, target, m, pieces)


def send_kernel(count, near, far, rads, enter_ref, rad_enter_ref, *refs):
    firsts, refs = refs[: len(near)], refs[len(near) :]
    seconds, refs = refs[: len(far)], refs[len(far) :]
    ends, outs = refs[:rads], refs[rads:]
    fields = ends[0].shape[0]
    spread_kernel(count, 4, near, far, enter_ref, *firsts, *outs[: len(far)])
    spread_kernel(count, 4, far, near, enter_ref, *seconds, *outs[len(far) : -1])
    for f in range(fields):
        pieces = [(2 * s + k, ends[s][f, 4 * k : 4 * k + 4]) for s in range(rads) for k in range(2)]
        for m in range(2):
            own = weighted(rad_enter_ref, f, 0, m, pieces)
            for out_ref in outs[:-1]:
                out_ref[f, 4, 4 * m : 4 * m + 4] = own
            outs[-1][f, 4 * m : 4 * m + 4] = own


def radial_kernel(rad_ref, *refs):
    ends, (src_ref, part_ref, out_ref, all_ref) = refs[:-4], refs[-4:]
    fields, _, cells, width = ends[0].shape
    rows = part_ref.shape[1]
    lane = lanes_of((rows, width))
    target = far_lane(width)
    for f in range(fields):
        for j in range(cells):
            at = pl.ds((f * cells + j) * rows, rows)
            moved = pltpu.roll(part_ref[f], (target - j + width) % width, 1)
            all_ref[at] = src_ref[at] + jnp.where(lane == target, moved, 0.0)
    for f in range(fields):
        for first in range(0, cells, 16):

            def at(i):
                return pl.ds((f * cells + first) * rows + i, 16, stride=rows)

            def store(i, value):
                out_ref[at(i)] = value

            ahead, back = (sum(ref[f, m, first : first + 16] for ref in ends) for m in range(2))
            radial_sweeps(rad_ref, f, lambda i: all_ref[at(i)], ahead, back, store)


def last_kernel(firsts, seconds, steps, coef_ref, enter_ref, rad_ref, *refs):
    parts, (src_ref, out_ref, z_ref, work_ref, held_ref, sems) = refs[:-6], refs[-6:]
    fields, cells, rows, width = src_ref.shape
    half = rows // 2
    at = {s: i for i, s in reversed(list(enumerate(steps)))}
    upper_rows = lax.broadcasted_iota(jnp.int32, (8, width), 0) < 4
    entry = []
    for f in range(fields):
        for m in range(4):
            base = (f * 4 + m) * rows
            work_ref[pl.ds(base, half)] = sum(ref[f, m] for ref in parts[:firsts])
            work_ref[pl.ds(base + half, half)] = sum(ref[f, m] for ref in parts[firsts : firsts + seconds])

        def row(s, k):
            ref = parts[at[s]]
            if at[s] < firsts + seconds:
                return ref[f, 4, k : k + 1]
            return ref[f, k : k + 1]

        sides = None
        for s in range(len(at)):
            for k in range(4):
                value = jnp.where(upper_rows, row(s, k), row(s, 4 + k))
                term = enter_ref[f, 4 * s + k] * value
                sides = term if sides is None else sides + term

        def store(i, value):
            work_ref[pl.ds(f * 4 * rows + i, 4, stride=rows)] = value

        radial_sweeps(
            rad_ref,
            f,
            lambda i: work_ref[pl.ds(f * 4 * rows + i, 4, stride=rows)],
            sides[0:4],
            sides[4:8],
            store,
        )
        entry.append([work_ref[pl.ds((f * 4 + m) * rows, rows)] for m in range(4)])
    lower_sweep(
        coef_ref,
        cells,
        lambda j: [src_ref[f, j] for f in range(fields)],
        z_ref,
        tuple((e[0], e[1]) for e in entry),
    )

    def store(f, j, value):
        held_ref[f, j] = value

    chunks = sems.shape[0]
    size = cells // chunks
    carry = tuple((e[2], e[3]) for e in entry)
    copies = []
    for c in reversed(range(chunks)):
        carry = upper_sweep(coef_ref, cells, z_ref, carry, store, c * size, size)
        copies.append(
            pltpu.make_async_copy(
                held_ref.at[:, pl.ds(c * size, size)], out_ref.at[:, pl.ds(c * size, size)], sems.at[c]
            )
        )
        copies[-1].start()
    for copy in copies:
        copy.wait()


def weight(a, b):
    return jnp.sqrt(1.0 - (a + b) * (a + b))


def own_table_kernel(coef_ref, vec_ref, dis_ref, tab_ref, reply_ref, mix_ref):
    _, cells, fields, width = tab_ref.shape
    total = coef_ref.shape[2]
    start = lax.axis_index("azim") * cells
    a, b, c, e = (pltpu.roll(coef_ref[kind], (total - start) % total, 1)[:, :width] for kind in range(4))
    for kind, table in enumerate((a, b, weight(a, b), c, e, weight(c, e))):
        for j in range(cells):
            tab_ref[kind, j] = over_lanes(table[:, j : j + 1], width)
    lane = lanes_of((fields, width))
    one = two = jnp.zeros((fields, width), f32)
    held = []
    for j in range(cells):
        z = jnp.where(lane == j, tab_ref[2, j], 0.0) + tab_ref[0, j] * one + tab_ref[1, j] * two
        held.append(z)
        one, two = z, one
    reply_ref[0], reply_ref[1] = one, two
    one = two = jnp.zeros((fields, width), f32)
    for j in reversed(range(cells)):
        v = tab_ref[5, j] * held[j] + tab_ref[3, j] * one + tab_ref[4, j] * two
        one, two = v, one
    reply_ref[2], reply_ref[3] = one, two
    for f in range(fields):
        mix_ref[f] = over_lanes(vec_ref[:, f : f + 1], width)
    square = (fields, fields)
    diagonal = lanes_of(square) == lax.broadcasted_iota(jnp.int32, square, 0)
    dis = jnp.sum(jnp.where(diagonal, dis_ref[...], 0.0), axis=1, keepdims=True)
    mix_ref[fields] = over_lanes(dis, width)
    mix_ref[fields + 1] = over_lanes(1.0 - 2.0 * dis, width)


def azim_table_kernel(coef_ref, enter_ref, lone_ref):
    _, blocks, cells, fields = coef_ref.shape
    width = enter_ref.shape[-1]
    own = lax.axis_index("azim")
    unit = lax.broadcasted_iota(jnp.int32, (blocks, 8, fields), 1)

    def ones(k):
        return (unit == k).astype(f32)

    one, two = ones(0), ones(1)
    held = []
    for j in range(cells):
        z = coef_ref[0, :, j : j + 1] * one + coef_ref[1, :, j : j + 1] * two
        held.append(z)
        one, two = z, one
    lower = (one, two)
    one, two = ones(2), ones(3)
    for j in reversed(range(cells)):
        c, e = coef_ref[2, :, j : j + 1], coef_ref[3, :, j : j + 1]
        v = weight(c, e) * held[j] + c * one + e * two
        one, two = v, one
    upper = (one, two)

    def entry(pair, p, m, k):
        return pair[m][p, k : k + 1]

    count = 4 * blocks
    height = -(-(count + 2) // 8) * 8
    row = lax.broadcasted_iota(jnp.int32, (height, fields), 0)

    def slot(p, k):
        return (row == 4 * (p ^ own) + k).astype(f32)

    def through(order, pair, first, source, start):
        state, entering = start, {}
        for p in order:
            entering[p] = state
            state = tuple(
                source(p, m) + entry(pair, p, m, first) * state[0] + entry(pair, p, m, first + 1) * state[1]
                for m in range(2)
            )
        return state, entering

    def closed(order, pair, first, source):
        start = tuple((row == count + k).astype(f32) for k in range(2))
        (total_one, total_two), _ = through(order, pair, first, source, start)
        a = 1.0 - total_one[count : count + 1]
        b = total_one[count + 1 : count + 2]
        c = total_two[count : count + 1]
        d = 1.0 - total_two[count + 1 : count + 2]
        scale = 1.0 / (a * d - b * c)
        live = row < count
        total_one, total_two = jnp.where(live, total_one, 0.0), jnp.where(live, total_two, 0.0)
        start = ((d * total_one + b * total_two) * scale, (c * total_one + a * total_two) * scale)
        return through(order, pair, first, source, start)[1]

    lower_in = closed(range(blocks), lower, 0, slot)

    def upper_source(p, m):
        z_one, z_two = lower_in[p]
        return slot(p, 2 + m) + entry(upper, p, m, 0) * z_one + entry(upper, p, m, 1) * z_two

    upper_in = closed(list(reversed(range(blocks))), upper, 2, upper_source)
    for i, step in enumerate(targets_of(blocks)):
        for m in range(4):
            picked = jnp.zeros((height, fields), f32)
            for p in range(blocks):
                value = lower_in[p][m] if m < 2 else upper_in[p][m - 2]
                picked = jnp.where(own == (p ^ step), value, picked)
            for f in range(fields):
                value = over_lanes(picked[:count, f : f + 1], width)
                enter_ref[f, i, m] = value
                if i == 0:
                    for again in range(2):
                        lone_ref[pl.ds(f * count * 8 + 4 * again + m, count, stride=8)] = value


def rad_table_kernel(coef_ref, own_ref, enter_ref, work_ref):
    _, rows, blocks, fields = coef_ref.shape
    width = enter_ref.shape[-1]
    own = lax.axis_index("rad")
    lower, upper = coef_ref[0], coef_ref[1]
    scale = jnp.sqrt(jnp.sqrt(1.0 + lower + upper))
    one = jnp.ones((blocks, fields), f32)
    forward, inverse, backward, outer, sums = [], [], [], [], []
    for i in range(rows):
        if i == 0:
            factor = lower[0]
            reach, total = factor, one
        else:
            factor = lower[i] * inverse[-1]
            reach, total = factor * reach, 1.0 + factor * total
        forward.append(factor)
        inverse.append(1.0 / (upper[i] + reach + total))
        backward.append(upper[i] * inverse[-1])
        outer.append(inverse[-1] * reach)
        sums.append(inverse[-1] * total)
    to_last, to_first = [None] * rows, [None] * rows
    last = inverse[-1]
    for i in reversed(range(rows)):
        to_last[i] = scale[i] * last
        last = last * forward[i]
    gain = one
    gathered = []
    for i in range(rows):
        gathered.append(gain * inverse[i])
        gain = gain * backward[i]
    first = jnp.zeros((blocks, fields), f32)
    for i in reversed(range(rows)):
        first = gathered[i] + (forward[i + 1] * first if i + 1 < rows else 0.0)
        to_first[i] = scale[i] * first
    last_before, last_after, last_sum = outer[-1], backward[-1], sums[-1]
    first_before = first_sum = 0.0
    for i in reversed(range(rows)):
        first_before = outer[i] + backward[i] * first_before
        first_sum = sums[i] + backward[i] * first_sum
    first_after = gain

    tables = ([scale[i] for i in range(rows)], forward, inverse, backward, to_last, to_first)
    step = work_ref.shape[0] // (6 * rows)
    for kind, table in enumerate(tables):
        for i in range(rows):
            work_ref[pl.ds((kind * rows + i) * step, blocks)] = table[i]
    for kind in range(6):
        picked = work_ref[pl.ds(kind * rows * step + own, rows, stride=step)]
        for f in range(fields):
            own_ref[f, kind] = over_lanes(picked[:, f : f + 1], width)

    count = 2 * blocks
    height = -(-count // 8) * 8
    row = lax.broadcasted_iota(jnp.int32, (height, fields), 0)

    def slot(p, k):
        return (row == 2 * (p ^ own) + k).astype(f32)

    def of(table, p):
        return table[p : p + 1]

    known, share, spare = {}, {}, {}
    known[0], share[0] = slot(0, 0), of(last_after, 0)
    spare[0] = of(last_sum, 0) + of(last_before, 0)
    pivots, ready = {}, {}
    for p in range(1, blocks):
        before, after, total = of(first_before, p), of(first_after, p), of(first_sum, p)
        pivots[p] = 1.0 / (after + total + before * spare[p - 1])
        ready[p] = (slot(p, 1) + before * known[p - 1]) * pivots[p]
        known[p] = slot(p, 0) + of(last_before, p) * (known[p - 1] + share[p - 1] * ready[p])
        share[p] = of(last_after, p) + of(last_before, p) * share[p - 1] * after * pivots[p]
        spare[p] = of(last_sum, p) + of(last_before, p) * pivots[p] * (
            (after + before) * spare[p - 1] + total
        )
    zero = jnp.zeros((height, fields), f32)
    above, below = {blocks - 1: zero}, {0: zero}
    for p in reversed(range(1, blocks)):
        value = ready[p] + of(first_after, p) * pivots[p] * above[p]
        above[p - 1] = value
        below[p] = known[p - 1] + share[p - 1] * value
    for i, step in enumerate(targets_of(blocks)):
        for m, entering in enumerate((below, above)):
            picked = zero
            for p in range(blocks):
                picked = jnp.where(own == (p ^ step), entering[p], picked)
            for f in range(fields):
                enter_ref[f, i, m] = over_lanes(picked[:count, f : f + 1], width)


def from_partner(values, axis, step):
    if step == 0:
        return values
    return lax.ppermute(values, axis, [(i, i ^ step) for i in range(lax.axis_size(axis))])


def local(residual, left_vec, dissip, azim_coef, radial_coef):
    fields, cells, rows, width = residual.shape
    azim_count, rad_count = lax.axis_size("azim"), lax.axis_size("rad")
    whole, flat = (fields, cells, rows, width), (fields * cells * rows, width)
    edge = call(edge_kernel, [(fields, rows, width)], residual)[0]
    halo = from_partner(edge, "axial", 1)

    own_azim, reply, mixing = call(
        own_table_kernel,
        [(6, cells, fields, width), (4, fields, width), (fields + 2, fields, width)],
        azim_coef,
        left_vec,
        dissip.reshape(1, fields),
    )
    azim_blocks = azim_coef.reshape(4, fields, azim_count, cells).transpose(0, 2, 3, 1)
    azim_enter, lone_enter = call(
        azim_table_kernel,
        [
            (fields, len(targets_of(azim_count)), 4, 4 * azim_count, width),
            (fields * 4 * azim_count * 8, width),
        ],
        azim_blocks,
    )
    lone_enter = lone_enter.reshape(fields, 4 * azim_count, 8, width)
    rad_blocks = radial_coef.reshape(2, fields, rad_count, rows).transpose(0, 3, 2, 1)
    own_rad, rad_enter = call(
        rad_table_kernel,
        [(fields, 6, rows, width), (fields, len(targets_of(rad_count)), 2, 2 * rad_count, width)],
        rad_blocks,
        scratch=[(6 * rows * -(-rad_count // 8) * 8, fields)],
    )

    src, states = call(
        first_kernel, [whole, (fields, 4, rows, width)], own_azim, mixing, residual, scratch=[whole]
    )
    half, small = (fields, 4, rows // 2, width), (fields, 8, width)
    one, two, part, end = call(
        patch_kernel,
        [half, half, (fields, rows, width), small],
        mixing,
        own_rad,
        halo,
        states,
        reply,
        scratch=[(fields * 4 * rows, width)],
    )
    low, high = low_high(azim_count)
    ones = [from_partner(one, "azim", s) for s in low]
    twos = [from_partner(two, "azim", s) for s in high]
    smalls = [from_partner(end, "rad", s) for s in range(rad_count)]
    src = src.reshape(flat)
    ends = call(source_kernel, [(fields, 2, cells, width)], own_rad, src, part, scratch=[(width, width)])[0]

    message = (fields, 5, rows // 2, width)
    *sums, lone = call(
        lambda *refs: send_kernel(azim_count, low, high, rad_count, *refs),
        [message] * (len(low) + len(high)) + [small],
        azim_enter,
        rad_enter,
        *ones,
        *twos,
        *smalls,
        cost=10**11,
    )
    near, far = low_high(rad_count)
    gathered = [from_partner(ends, "rad", s) for s in near]
    entry = call(
        lambda enter_ref, after_ref, *refs: spread_kernel(rad_count, 2, near, far, enter_ref, *refs),
        [ends.shape] * len(far),
        rad_enter,
        lone,
        *gathered,
    )
    entry = [from_partner(value, "rad", s) for s, value in zip(far, entry)]
    src = call(radial_kernel, [flat], own_rad, *entry, src, part, scratch=[flat])[0]

    rest = [s for s in range(azim_count) if s not in low + high]
    parts = [from_partner(value, "azim", s) for s, value in zip(high + low, sums)]
    parts += [from_partner(lone, "azim", s) for s in rest]

    chunks = 4
    return pl.pallas_call(
        lambda *refs: last_kernel(len(high), len(low), high + low + rest, *refs),
        out_shape=jax.ShapeDtypeStruct(whole, f32),
        in_specs=[VMEM] * (len(parts) + 4),
        out_specs=pl.BlockSpec(memory_space=pl.ANY),
        scratch_shapes=[
            pltpu.VMEM(whole, f32),
            pltpu.VMEM((fields * 4 * rows, width), f32),
            pltpu.VMEM(whole, f32),
            pltpu.SemaphoreType.DMA((chunks,)),
        ],
        compiler_params=params,
    )(own_azim, lone_enter, own_rad, *parts, src.reshape(whole))


def solution(mesh):
    placed = (P(None, "azim", "rad", "axial"), P(), P(), P(), P())
    return jax.shard_map(
        local,
        mesh=mesh,
        in_specs=placed,
        out_specs=P(None, "azim", "rad", "axial"),
        check_vma=False,
    )
```

time: 33.1 us -> 28.2 us (0.85)
  Pallas kernels: 12.3 us -> 7.31 us
  waiting for transfers between devices: 2.73 us -> 3.77 us
  local copies, waits for them, and re-layouts: 2.41 us -> 1.71 us
    pallas_call x10, Pallas kernels: 9.61 us -> 5.59 us  [call(): pl.pallas_call(body, out_shape=[jax.ShapeDtypeStruct(shape, f32) for shap...]
    ppermute x11, waiting for transfers between devices: 2.73 us -> 3.77 us  [from_partner(): lax.ppermute(values, axis, [(i, i ^ step) for i in range(lax.axis_size(ax...]
    pallas_call x1, Pallas kernels: 2.66 us -> 1.73 us  [local(): pl.pallas_call(lambda *refs: last_kernel(len(high), len(low), high + low...]
    reshape x5 -> x2, local copies, waits for them, and re-layouts: 0.56 us -> 0.22 us  [local(): radial_coef.reshape(2, fields, rad_count, rows).transpose(0, 3, 2, 1)]
    unnamed x14 -> x18, local copies, waits for them, and re-layouts: 1.59 us -> 1.49 us
  transfers between devices with their start and end apart: 11 -> 11, of which waited for: 3 -> 5; matrix products, arithmetic and copies ran while one was open for 4% -> 1% of each run, Pallas kernels for 23% -> 17%
where the time goes in v4:
time: 28.2 us; the launch traced here: 28.1 us
  starting transfers between devices  15.2 us (54%)
  Pallas kernels  7.31 us (26%)
  waiting for transfers between devices  3.77 us (13%)
  local copies, waits for them, and re-layouts  1.71 us (6%)
    ppermute x11, starting transfers between devices, from_partner(): lax.ppermute(values, axis, [(i, i ^ step) for i in range(lax.axis_size(ax...  15.2 us
    pallas_call x10, Pallas kernels, call(): pl.pallas_call(body, out_shape=[jax.ShapeDtypeStruct(shape, f32) for shap...  5.59 us
    ppermute x11, waiting for transfers between devices, from_partner(): lax.ppermute(values, axis, [(i, i ^ step) for i in range(lax.axis_size(ax...  3.77 us
    pallas_call x1, Pallas kernels, local(): pl.pallas_call(lambda *refs: last_kernel(len(high), len(low), high + low...  1.73 us
    unnamed x18, local copies, waits for them, and re-layouts  1.49 us
  transfers between devices with their start and end apart: 11, of which 5 were waited for; matrix products, arithmetic and copies ran while one was open for 1% of the time, Pallas kernels for 17%

profile of v4, /device:TPU:0, one launch (start us, length us, event | category | flops | bytes accessed | tf_op | source)
XLA Modules:
  0.0 28.1 jit_solution(2711130121827989295)
XLA Ops:
  0.0 1.3 %copy-done = f32[5,32,16,128]{3,2,1,0:T(8,128)S(1)} copy-done((f32[5,32,16,128]{3,2,1,0:T(8,128)S(1)}, f32[5,32,16,128]{3,2,1,0:T(8,128)}, u32[]{:S(2)}) %copy-start) | copy-done | bytes 1310744
  1.3 0.4 %shard_map.58 = f32[5,16,128]{2,1,0:T(8,128)S(1)} custom-call(f32[5,32,16,128]{3,2,1,0:T(8,128)S(1)} %copy-done), custom_call_target="tpu_custom_call" | custom-call | tf_op jit(solution)/shard_map/pallas_call | solution.py:14
  1.8 3.0 %collective-permute-start = (f32[5,16,128]{2,1,0:T(8,128)S(1)}, f32[5,16,128]{2,1,0:T(8,128)S(1)}, u32[]{:S(2)}, u32[]{:S(2)}) collective-permute-start(f32[5,16,128]{2,1,0:T(8,128)S(1)} %shard_map.58), channel_id=1, source_target_pairs={{0,1},{1,0},{2,3},{3,2},{4,5},{5,4},{6,7},{7,6},{8,9},{9,8},{10,11... | collective-permute-start | bytes 122888 | tf_op jit(solution)/shard_map/ppermute | solution.py:520
  4.8 0.1 reshape.21
  4.9 0.1 copy.10
  5.0 0.4 %shard_map.57 = (f32[5,6,16,128]{3,2,1,0:T(8,128)S(1)}, f32[5,3,2,8,128]{4,3,2,1,0:T(8,128)S(1)}) custom-call(f32[2,16,4,5]{3,2,1,0:T(4,128)S(1)} %bitcast.15), custom_call_target="tpu_custom_call" | custom-call | tf_op jit(solution)/shard_map/pallas_call | solution.py:14
  5.4 0.5 %shard_map.55 = (f32[6,32,5,128]{3,2,1,0:T(8,128)S(1)}, f32[4,5,128]{2,1,0:T(8,128)S(1)}, f32[7,5,128]{2,1,0:T(8,128)S(1)}) custom-call(f32[4,5,128]{2,1,0:T(8,128)S(1)} %copy.8.coef_ref, f32[5,5]{1,0:T(8,128)S(1)} %copy-done.4, f32[1,5]{1,0:T(1,128)S(1)} %bitcast.16), custom_call_target="tpu_custom_call" | custom-call | tf_op jit(solution)/shard_map/pallas_call | solution.py:14
  6.0 0.0 copy-start.2
  6.0 1.4 %shard_map.59 = (f32[5,32,16,128]{3,2,1,0:T(8,128)S(1)}, f32[5,4,16,128]{3,2,1,0:T(8,128)S(1)}) custom-call(f32[6,32,5,128]{3,2,1,0:T(8,128)S(1)} %get-tuple-element.25.coef_ref.refs_0_, f32[7,5,128]{2,1,0:T(8,128)S(1)} %get-tuple-element.30.mix_ref, f32[5,32,16,128]{3,2,1,0:T(8,128)S(1)} %copy-done.1), custom_call_target="tpu_custom_call" | custom-call | tf_op jit(solution)/shard_map/pallas_call | solution.py:14
  7.4 0.2 shard_map.60
  7.6 1.6 %collective-permute-start.1 = (f32[5,4,8,128]{3,2,1,0:T(8,128)S(1)}, f32[5,4,8,128]{3,2,1,0:T(8,128)S(1)}, u32[]{:S(2)}, u32[]{:S(2)}) collective-permute-start(f32[5,4,8,128]{3,2,1,0:T(8,128)S(1)} %get-tuple-element.33.refs_2_), channel_id=1, source_target_pairs={{0,8},{8,0},{16,24},{24,16},{1,9},{9,1},{17,25},{25,17},{2,10},{10... | collective-permute-start | bytes 245768 | tf_op jit(solution)/shard_map/ppermute | solution.py:520
  9.2 2.6 %collective-permute-start.2 = (f32[5,4,8,128]{3,2,1,0:T(8,128)S(1)}, f32[5,4,8,128]{3,2,1,0:T(8,128)S(1)}, u32[]{:S(2)}, u32[]{:S(2)}) collective-permute-start(f32[5,4,8,128]{3,2,1,0:T(8,128)S(1)} %get-tuple-element.34.refs_4_), channel_id=1, source_target_pairs={{0,16},{8,24},{16,0},{24,8},{1,17},{9,25},{17,1},{25,9},{2,18},{10... | collective-permute-start | bytes 245768 | tf_op jit(solution)/shard_map/ppermute | solution.py:520
  11.8 0.1 collective-permute-start.5
  11.9 1.4 %collective-permute-start.4 = (f32[5,8,128]{2,1,0:T(8,128)S(1)}, f32[5,8,128]{2,1,0:T(8,128)S(1)}, u32[]{:S(2)}, u32[]{:S(2)}) collective-permute-start(f32[5,8,128]{2,1,0:T(8,128)S(1)} %get-tuple-element.35.refs_6_), channel_id=1, source_target_pairs={{0,4},{2,6},{4,0},{6,2},{1,5},{3,7},{5,1},{7,3},{8,12},{10,14},{12... | collective-permute-start | bytes 61448 | tf_op jit(solution)/shard_map/ppermute | solution.py:520
  13.3 0.3 %collective-permute-start.3 = (f32[5,8,128]{2,1,0:T(8,128)S(1)}, f32[5,8,128]{2,1,0:T(8,128)S(1)}, u32[]{:S(2)}, u32[]{:S(2)}) collective-permute-start(f32[5,8,128]{2,1,0:T(8,128)S(1)} %get-tuple-element.35.refs_6_), channel_id=1, source_target_pairs={{0,2},{2,0},{4,6},{6,4},{1,3},{3,1},{5,7},{7,5},{8,10},{10,8},{12,... | collective-permute-start | bytes 61448 | tf_op jit(solution)/shard_map/ppermute | solution.py:520
  13.7 0.1 copy.9
  13.8 0.6 %shard_map.56 = (f32[5,3,4,16,128]{4,3,2,1,0:T(8,128)S(1)}, f32[640,128]{1,0:T(8,128)S(1)}) custom-call(f32[4,4,32,5]{3,2,1,0:T(8,128)S(1)} %bitcast.13), custom_call_target="tpu_custom_call" | custom-call | tf_op jit(solution)/shard_map/pallas_call | solution.py:14
  14.4 0.6 %shard_map.62.refs_0_ = f32[5,2,32,128]{3,2,1,0:T(8,128)S(1)} custom-call(f32[5,6,16,128]{3,2,1,0:T(8,128)S(1)} %get-tuple-element.27.rad_ref.refs_2_, f32[2560,128]{1,0:T(8,128)S(1)} %bitcast.11, f32[5,16,128]{2,1,0:T(8,128)S(1)} %get-tuple-element.42.part_ref.refs_3_), custom_call_target="tpu_custom_call" | custom-call | tf_op jit(solution)/shard_map/pallas_call | solution.py:14
  15.1 0.1 collective-permute-done.5.refs_9_
  15.2 0.2 collective-permute-start.9
  15.3 0.3 %collective-permute-done.4.refs_8_ = f32[5,8,128]{2,1,0:T(8,128)S(1)} collective-permute-done((f32[5,8,128]{2,1,0:T(8,128)S(1)}, f32[5,8,128]{2,1,0:T(8,128)S(1)}, u32[]{:S(2)}, u32[]{:S(2)}) %collective-permute-start.4) | collective-permute-done | bytes 20512 | tf_op jit(solution)/shard_map/ppermute | solution.py:520
  15.7 0.2 shard_map.61
  15.9 0.7 %collective-permute-done.9.refs_1_ = f32[5,2,32,128]{3,2,1,0:T(8,128)S(1)} collective-permute-done((f32[5,2,32,128]{3,2,1,0:T(8,128)S(1)}, f32[5,2,32,128]{3,2,1,0:T(8,128)S(1)}, u32[]{:S(2)}, u32[]{:S(2)}) %collective-permute-start.9) | collective-permute-done | bytes 163872 | tf_op jit(solution)/shard_map/ppermute | solution.py:520
  16.6 0.1 shard_map.63
  16.7 1.5 %collective-permute-start.10 = (f32[5,2,32,128]{3,2,1,0:T(8,128)S(1)}, f32[5,2,32,128]{3,2,1,0:T(8,128)S(1)}, u32[]{:S(2)}, u32[]{:S(2)}) collective-permute-start(f32[5,2,32,128]{3,2,1,0:T(8,128)S(1)} %get-tuple-element.44), channel_id=1, source_target_pairs={{0,4},{2,6},{4,0},{6,2},{1,5},{3,7},{5,1},{7,3},{8,12},{10,14},{12... | collective-permute-start | bytes 491528 | tf_op jit(solution)/shard_map/ppermute | solution.py:520
  18.2 0.9 %collective-permute-start.6 = (f32[5,5,8,128]{3,2,1,0:T(8,128)S(1)}, f32[5,5,8,128]{3,2,1,0:T(8,128)S(1)}, u32[]{:S(2)}, u32[]{:S(2)}) collective-permute-start(f32[5,5,8,128]{3,2,1,0:T(8,128)S(1)} %get-tuple-element.37), channel_id=1, source_target_pairs={{0,16},{8,24},{16,0},{24,8},{1,17},{9,25},{17,1},{25,9},{2,18},{10... | collective-permute-start | bytes 307208 | tf_op jit(solution)/shard_map/ppermute | solution.py:520
  19.1 0.6 %collective-permute-start.7 = (f32[5,5,8,128]{3,2,1,0:T(8,128)S(1)}, f32[5,5,8,128]{3,2,1,0:T(8,128)S(1)}, u32[]{:S(2)}, u32[]{:S(2)}) collective-permute-start(f32[5,5,8,128]{3,2,1,0:T(8,128)S(1)} %get-tuple-element.39), channel_id=1, source_target_pairs={{0,8},{8,0},{16,24},{24,16},{1,9},{9,1},{17,25},{25,17},{2,10},{10... | collective-permute-start | bytes 307208 | tf_op jit(solution)/shard_map/ppermute | solution.py:520
  19.7 2.9 %collective-permute-start.8 = (f32[5,8,128]{2,1,0:T(8,128)S(1)}, f32[5,8,128]{2,1,0:T(8,128)S(1)}, u32[]{:S(2)}, u32[]{:S(2)}) collective-permute-start(f32[5,8,128]{2,1,0:T(8,128)S(1)} %get-tuple-element.40.after_ref), channel_id=1, source_target_pairs={{0,24},{8,16},{16,8},{24,0},{1,25},{9,17},{17,9},{25,1},{2,26},{10... | collective-permute-start | bytes 61448 | tf_op jit(solution)/shard_map/ppermute | solution.py:520
  22.6 0.4 %collective-permute-done.10.refs_1_ = f32[5,2,32,128]{3,2,1,0:T(8,128)S(1)} collective-permute-done((f32[5,2,32,128]{3,2,1,0:T(8,128)S(1)}, f32[5,2,32,128]{3,2,1,0:T(8,128)S(1)}, u32[]{:S(2)}, u32[]{:S(2)}) %collective-permute-start.10) | collective-permute-done | bytes 163872 | tf_op jit(solution)/shard_map/ppermute | solution.py:520
  23.0 1.1 %shard_map.64 = f32[2560,128]{1,0:T(8,128)S(1)} custom-call(f32[5,6,16,128]{3,2,1,0:T(8,128)S(1)} %get-tuple-element.27.rad_ref.refs_2_, f32[5,2,32,128]{3,2,1,0:T(8,128)S(1)} %get-tuple-element.43.refs_0_, f32[5,2,32,128]{3,2,1,0:T(8,128)S(1)} %collective-permute-done.10.refs_1_, f32[2560,128]{1,0:T(8,128)S(1)} %bitcast.12, ...), custom_call_target="tpu_custom_call" | custom-call | tf_op jit(solution)/shard_map/pallas_call | solution.py:14
  24.2 2.2 %collective-permute-done.8.refs_7_ = f32[5,8,128]{2,1,0:T(8,128)S(1)} collective-permute-done((f32[5,8,128]{2,1,0:T(8,128)S(1)}, f32[5,8,128]{2,1,0:T(8,128)S(1)}, u32[]{:S(2)}, u32[]{:S(2)}) %collective-permute-start.8) | collective-permute-done | bytes 20512 | tf_op jit(solution)/shard_map/ppermute | solution.py:520
  26.4 1.7 %shard_map.65 = f32[5,32,16,128]{3,2,1,0:T(8,128)} custom-call(f32[6,32,5,128]{3,2,1,0:T(8,128)S(1)} %copy-done.3, f32[5,16,8,128]{3,2,1,0:T(8,128)S(1)} %bitcast.14, f32[5,6,16,128]{3,2,1,0:T(8,128)S(1)} %get-tuple-element.27.rad_ref.refs_2_, f32[5,5,8,128]{3,2,1,0:T(8,128)S(1)} %get-tuple-element.36.refs_3_, ...), custom_call_target="tpu_custom_call" | custom-call | tf_op jit(solution)/shard_map/pallas_call | solution.py:604
  (21 shorter events, 0.0 us)
Async XLA Ops:
  0.0 1.3 %copy-start = (f32[5,32,16,128]{3,2,1,0:T(8,128)S(1)}, f32[5,32,16,128]{3,2,1,0:T(8,128)}, u32[]{:S(2)}) copy-start(f32[5,32,16,128]{3,2,1,0:T(8,128)} %res_ref.3) | copy-start | bytes 3932164
  1.3 3.5 %copy-start.6 = (f32[4,5,128]{2,0,1:T(4,128)S(1)}, f32[4,5,128]{2,0,1:T(4,128)}, u32[]{:S(2)}) copy-start(f32[4,5,128]{2,0,1:T(4,128)} %param.8) | copy-start | bytes 30724
  1.3 3.5 %copy-start.7 = (f32[2,5,64]{2,0,1:T(2,128)S(1)}, f32[2,5,64]{2,0,1:T(2,128)}, u32[]{:S(2)}) copy-start(f32[2,5,64]{2,0,1:T(2,128)} %param.9) | copy-start | bytes 7684
  1.3 4.1 %copy-start.4 = (f32[5,5]{1,0:T(8,128)S(1)}, f32[5,5]{1,0:T(8,128)}, u32[]{:S(2)}) copy-start(f32[5,5]{1,0:T(8,128)} %vec_ref.1) | copy-start | bytes 304
  1.3 4.1 %copy-start.5 = (f32[5]{0:T(128)S(1)}, f32[5]{0:T(128)}, u32[]{:S(2)}) copy-start(f32[5]{0:T(128)} %param.7) | copy-start | bytes 64
  1.3 4.7 %copy-start.1 = (f32[5,32,16,128]{3,2,1,0:T(8,128)S(1)}, f32[5,32,16,128]{3,2,1,0:T(8,128)}, u32[]{:S(2)}) copy-start(f32[5,32,16,128]{3,2,1,0:T(8,128)} %res_ref.3) | copy-start | bytes 3932164
  1.8 5.6 %collective-permute-start = (f32[5,16,128]{2,1,0:T(8,128)S(1)}, f32[5,16,128]{2,1,0:T(8,128)S(1)}, u32[]{:S(2)}, u32[]{:S(2)}) collective-permute-start(f32[5,16,128]{2,1,0:T(8,128)S(1)} %shard_map.58), channel_id=1, source_target_pairs={{0,1},{1,0},{2,3},{3,2},{4,5},{5,4},{6,7},{7,6},{8,9},{9,8},{10,11... | collective-permute-start | bytes 122888 | tf_op jit(solution)/shard_map/ppermute | solution.py:520
  6.0 1.6 %copy-start.2 = (f32[6,32,5,128]{3,2,1,0:T(8,128)}, f32[6,32,5,128]{3,2,1,0:T(8,128)S(1)}, u32[]{:S(2)}) copy-start(f32[6,32,5,128]{3,2,1,0:T(8,128)S(1)} %get-tuple-element.25.coef_ref.refs_0_) | copy-start | bytes 1474564
  7.6 8.1 %collective-permute-start.1 = (f32[5,4,8,128]{3,2,1,0:T(8,128)S(1)}, f32[5,4,8,128]{3,2,1,0:T(8,128)S(1)}, u32[]{:S(2)}, u32[]{:S(2)}) collective-permute-start(f32[5,4,8,128]{3,2,1,0:T(8,128)S(1)} %get-tuple-element.33.refs_2_), channel_id=1, source_target_pairs={{0,8},{8,0},{16,24},{24,16},{1,9},{9,1},{17,25},{25,17},{2,10},{10... | collective-permute-start | bytes 245768 | tf_op jit(solution)/shard_map/ppermute | solution.py:520
  9.2 6.5 %collective-permute-start.2 = (f32[5,4,8,128]{3,2,1,0:T(8,128)S(1)}, f32[5,4,8,128]{3,2,1,0:T(8,128)S(1)}, u32[]{:S(2)}, u32[]{:S(2)}) collective-permute-start(f32[5,4,8,128]{3,2,1,0:T(8,128)S(1)} %get-tuple-element.34.refs_4_), channel_id=1, source_target_pairs={{0,16},{8,24},{16,0},{24,8},{1,17},{9,25},{17,1},{25,9},{2,18},{10... | collective-permute-start | bytes 245768 | tf_op jit(solution)/shard_map/ppermute | solution.py:520
  11.8 3.4 %collective-permute-start.5 = (f32[5,8,128]{2,1,0:T(8,128)S(1)}, f32[5,8,128]{2,1,0:T(8,128)S(1)}, u32[]{:S(2)}, u32[]{:S(2)}) collective-permute-start(f32[5,8,128]{2,1,0:T(8,128)S(1)} %get-tuple-element.35.refs_6_), channel_id=1, source_target_pairs={{0,6},{2,4},{4,2},{6,0},{1,7},{3,5},{5,3},{7,1},{8,14},{10,12},{12... | collective-permute-start | bytes 61448 | tf_op jit(solution)/shard_map/ppermute | solution.py:520
  11.9 3.8 %collective-permute-start.4 = (f32[5,8,128]{2,1,0:T(8,128)S(1)}, f32[5,8,128]{2,1,0:T(8,128)S(1)}, u32[]{:S(2)}, u32[]{:S(2)}) collective-permute-start(f32[5,8,128]{2,1,0:T(8,128)S(1)} %get-tuple-element.35.refs_6_), channel_id=1, source_target_pairs={{0,4},{2,6},{4,0},{6,2},{1,5},{3,7},{5,1},{7,3},{8,12},{10,14},{12... | collective-permute-start | bytes 61448 | tf_op jit(solution)/shard_map/ppermute | solution.py:520
  13.3 2.4 %collective-permute-start.3 = (f32[5,8,128]{2,1,0:T(8,128)S(1)}, f32[5,8,128]{2,1,0:T(8,128)S(1)}, u32[]{:S(2)}, u32[]{:S(2)}) collective-permute-start(f32[5,8,128]{2,1,0:T(8,128)S(1)} %get-tuple-element.35.refs_6_), channel_id=1, source_target_pairs={{0,2},{2,0},{4,6},{6,4},{1,3},{3,1},{5,7},{7,5},{8,10},{10,8},{12,... | collective-permute-start | bytes 61448 | tf_op jit(solution)/shard_map/ppermute | solution.py:520
  15.2 1.4 %collective-permute-start.9 = (f32[5,2,32,128]{3,2,1,0:T(8,128)S(1)}, f32[5,2,32,128]{3,2,1,0:T(8,128)S(1)}, u32[]{:S(2)}, u32[]{:S(2)}) collective-permute-start(f32[5,2,32,128]{3,2,1,0:T(8,128)S(1)} %shard_map.62.refs_0_), channel_id=1, source_target_pairs={{0,2},{2,0},{4,6},{6,4},{1,3},{3,1},{5,7},{7,5},{8,10},{10,8},{12,... | collective-permute-start | bytes 491528 | tf_op jit(solution)/shard_map/ppermute | solution.py:520
  16.7 6.3 %collective-permute-start.10 = (f32[5,2,32,128]{3,2,1,0:T(8,128)S(1)}, f32[5,2,32,128]{3,2,1,0:T(8,128)S(1)}, u32[]{:S(2)}, u32[]{:S(2)}) collective-permute-start(f32[5,2,32,128]{3,2,1,0:T(8,128)S(1)} %get-tuple-element.44), channel_id=1, source_target_pairs={{0,4},{2,6},{4,0},{6,2},{1,5},{3,7},{5,1},{7,3},{8,12},{10,14},{12... | collective-permute-start | bytes 491528 | tf_op jit(solution)/shard_map/ppermute | solution.py:520
  18.2 8.2 %collective-permute-start.6 = (f32[5,5,8,128]{3,2,1,0:T(8,128)S(1)}, f32[5,5,8,128]{3,2,1,0:T(8,128)S(1)}, u32[]{:S(2)}, u32[]{:S(2)}) collective-permute-start(f32[5,5,8,128]{3,2,1,0:T(8,128)S(1)} %get-tuple-element.37), channel_id=1, source_target_pairs={{0,16},{8,24},{16,0},{24,8},{1,17},{9,25},{17,1},{25,9},{2,18},{10... | collective-permute-start | bytes 307208 | tf_op jit(solution)/shard_map/ppermute | solution.py:520
  19.1 7.3 %collective-permute-start.7 = (f32[5,5,8,128]{3,2,1,0:T(8,128)S(1)}, f32[5,5,8,128]{3,2,1,0:T(8,128)S(1)}, u32[]{:S(2)}, u32[]{:S(2)}) collective-permute-start(f32[5,5,8,128]{3,2,1,0:T(8,128)S(1)} %get-tuple-element.39), channel_id=1, source_target_pairs={{0,8},{8,0},{16,24},{24,16},{1,9},{9,1},{17,25},{25,17},{2,10},{10... | collective-permute-start | bytes 307208 | tf_op jit(solution)/shard_map/ppermute | solution.py:520
  19.7 6.7 %collective-permute-start.8 = (f32[5,8,128]{2,1,0:T(8,128)S(1)}, f32[5,8,128]{2,1,0:T(8,128)S(1)}, u32[]{:S(2)}, u32[]{:S(2)}) collective-permute-start(f32[5,8,128]{2,1,0:T(8,128)S(1)} %get-tuple-element.40.after_ref), channel_id=1, source_target_pairs={{0,24},{8,16},{16,8},{24,0},{1,25},{9,17},{17,9},{25,1},{2,26},{10... | collective-permute-start | bytes 61448 | tf_op jit(solution)/shard_map/ppermute | solution.py:520
  23.0 3.4 %copy-start.3 = (f32[6,32,5,128]{3,2,1,0:T(8,128)S(1)}, f32[6,32,5,128]{3,2,1,0:T(8,128)}, u32[]{:S(2)}) copy-start(f32[6,32,5,128]{3,2,1,0:T(8,128)} %copy-done.2) | copy-start | bytes 1474564

commit v5 on v4

--- a/solution.py
+++ b/solution.py
@@ -10,7 +10,7 @@
 params = pltpu.CompilerParams(vmem_limit_bytes=32 * 1024 * 1024)
 
 
-def call(body, outs, *operands, scratch=(), cost=0):
+def call(body, outs, *operands, scratch=(), cost=0, aliases={}):
     return pl.pallas_call(
         body,
         out_shape=[jax.ShapeDtypeStruct(shape, f32) for shape in outs],
@@ -18,6 +18,7 @@
         out_specs=[VMEM] * len(outs),
         scratch_shapes=[pltpu.VMEM(shape, f32) for shape in scratch],
         compiler_params=params,
+        input_output_aliases=aliases,
         cost_estimate=pl.CostEstimate(flops=cost, bytes_accessed=0, transcendentals=0),
     )(*operands)
 
@@ -151,7 +152,7 @@
 
 
 def patch_kernel(
-    mix_ref, rad_ref, halo_ref, state_ref, reply_ref, first_ref, second_ref, part_ref, end_ref, work_ref
+    mix_ref, rad_ref, halo_ref, state_ref, reply_ref, _, first_ref, second_ref, part_ref, end_ref, work_ref
 ):
     fields, _, rows, width = state_ref.shape
     lane = lanes_of((rows, width))
@@ -166,28 +167,56 @@
             second_ref[f, m] = tile[rows // 2 :]
             work_ref[pl.ds((f * 4 + m) * rows, rows)] = tile
     for f in range(fields):
-        end_ref[f, 0:4], end_ref[f, 4:8] = radial_ends(
-            rad_ref, f, lambda i: work_ref[pl.ds(f * 4 * rows + i, 4, stride=rows)]
+        ends = radial_ends(rad_ref, f, lambda i: work_ref[pl.ds(f * 4 * rows + i, 4, stride=rows)])
+        for k in range(2):
+            side = slice(4 * k, 4 * k + 4)
+            first_ref[f, 4, side] = second_ref[f, 4, side] = end_ref[f, side] = ends[k]
+
+
+def source_ends(rad_ref, src_ref, end_ref):
+    fields, _, cells, _ = end_ref.shape
+    rows = rad_ref.shape[2]
+    for f in range(fields):
+        end_ref[f, 0], end_ref[f, 1] = radial_ends(
+            rad_ref, f, lambda i: src_ref[pl.ds(f * cells * rows + i, cells, stride=rows)]
         )
 
 
-def source_kernel(rad_ref, src_ref, part_ref, end_ref, turn_ref):
-    fields, _, cells, width = end_ref.shape
-    rows = part_ref.shape[1]
+def halo_ends_kernel(rad_ref, part_ref, known_ref, *refs):
+    outs, turn_ref = refs[:-1], refs[-1]
+    fields, _, cells, width = known_ref.shape
     lane = lanes_of((cells, width))
     target = far_lane(width)
+    size = cells // len(outs)
     turn_ref[...] = jnp.zeros(turn_ref.shape, f32)
     for f in range(fields):
         ends = radial_ends(rad_ref, f, lambda i: part_ref[f, i : i + 1])
         turn_ref[2 * f : 2 * f + 1], turn_ref[2 * f + 1 : 2 * f + 2] = ends
     turned = jnp.transpose(turn_ref[...])[:cells]
     for f in range(fields):
-        ends = radial_ends(
-            rad_ref, f, lambda i: src_ref[pl.ds(f * cells * rows + i, cells, stride=rows)]
-        )
         for k in range(2):
             moved = pltpu.roll(turned, (target - (2 * f + k) + width) % width, 1)
-            end_ref[f, k] = ends[k] + jnp.where(lane == target, moved, 0.0)
+            value = known_ref[f, k] + jnp.where(lane == target, moved, 0.0)
+            for i, out_ref in enumerate(outs):
+                out_ref[f, k] = value[i * size : (i + 1) * size]
+
+
+def first_half():
+    return lax.axis_index("azim") < lax.axis_size("azim") // 2
+
+
+def early_kernel(coef_ref, rad_ref, src_ref, enter_ref, lone_ref, end_ref):
+    @pl.when(first_half())
+    def _():
+        azim_table(coef_ref, enter_ref, lone_ref)
+        source_ends(rad_ref, src_ref, end_ref)
+
+
+def late_kernel(coef_ref, rad_ref, src_ref, _, __, ___, enter_ref, lone_ref, end_ref):
+    @pl.when(jnp.logical_not(first_half()))
+    def _():
+        azim_table(coef_ref, enter_ref, lone_ref)
+        source_ends(rad_ref, src_ref, end_ref)
 
 
 def weighted(enter_ref, f, target, m, pieces):
@@ -199,36 +228,51 @@
 
 
 def spread_kernel(count, size, near, far, enter_ref, *refs):
-    arrays, sums = refs[: len(near)], refs[len(near) :]
-    fields = sums[0].shape[0]
+    arrays, sums = refs[: -len(far)], refs[-len(far) :]
+    parts = len(arrays) // len(near)
+    extent = arrays[0].shape[2]
     for s, out_ref in zip(far, sums):
         target = targets_of(count).index(s)
-        for f in range(fields):
-            pieces = [(size * n + k, ref[f, k]) for n, ref in zip(near, arrays) for k in range(size)]
-            for m in range(size):
-                out_ref[f, m] = weighted(enter_ref, f, target, m, pieces)
-
-
-def send_kernel(count, near, far, rads, enter_ref, rad_enter_ref, *refs):
+        for part in range(parts):
+            for f in range(out_ref.shape[0]):
+                pieces = [
+                    (size * n + k, ref[f, k]) for n, ref in zip(near, arrays[part::parts]) for k in range(size)
+                ]
+                for m in range(size):
+                    value = weighted(enter_ref, f, target, m, pieces)
+                    out_ref[f, m, part * extent : (part + 1) * extent] = value
+
+
+def send_kernel(count, near, far, enter_ref, *refs):
     firsts, refs = refs[: len(near)], refs[len(near) :]
     seconds, refs = refs[: len(far)], refs[len(far) :]
-    ends, outs = refs[:rads], refs[rads:]
-    fields = ends[0].shape[0]
-    spread_kernel(count, 4, near, far, enter_ref, *firsts, *outs[: len(far)])
-    spread_kernel(count, 4, far, near, enter_ref, *seconds, *outs[len(far) : -1])
-    for f in range(fields):
-        pieces = [(2 * s + k, ends[s][f, 4 * k : 4 * k + 4]) for s in range(rads) for k in range(2)]
-        for m in range(2):
-            own = weighted(rad_enter_ref, f, 0, m, pieces)
-            for out_ref in outs[:-1]:
-                out_ref[f, 4, 4 * m : 4 * m + 4] = own
-            outs[-1][f, 4 * m : 4 * m + 4] = own
+    spread_kernel(count, 4, near, far, enter_ref, *firsts, *refs[: len(far)])
+    spread_kernel(count, 4, far, near, enter_ref, *seconds, *refs[len(far) :])
+
+
+def pass_kernel(in_ref, out_ref):
+    out_ref[...] = in_ref[...]
+
+
+def entry_end_kernel(steps, enter_ref, *refs):
+    parts, out_ref = refs[:-1], refs[-1]
+    fields, _, width = out_ref.shape
+    upper_rows = lax.broadcasted_iota(jnp.int32, (8, width), 0) < 4
+    for f in range(fields):
+        total = None
+        for s, ref in zip(steps, parts):
+            for k in range(4):
+                here = ref.at[f, 4] if len(ref.shape) == 4 else ref.at[f]
+                value = jnp.where(upper_rows, here[k : k + 1], here[4 + k : 5 + k])
+                term = enter_ref[f, 4 * s + k] * value
+                total = term if total is None else total + term
+        out_ref[f] = total
 
 
 def radial_kernel(rad_ref, *refs):
     ends, (src_ref, part_ref, out_ref, all_ref) = refs[:-4], refs[-4:]
-    fields, _, cells, width = ends[0].shape
-    rows = part_ref.shape[1]
+    fields, rows, width = part_ref.shape
+    cells = src_ref.shape[0] // (fields * rows)
     lane = lanes_of((rows, width))
     target = far_lane(width)
     for f in range(fields):
@@ -249,31 +293,18 @@
             radial_sweeps(rad_ref, f, lambda i: all_ref[at(i)], ahead, back, store)
 
 
-def last_kernel(firsts, seconds, steps, coef_ref, enter_ref, rad_ref, *refs):
+def last_kernel(firsts, seconds, coef_ref, rad_enter_ref, rad_ref, *refs):
     parts, (src_ref, out_ref, z_ref, work_ref, held_ref, sems) = refs[:-6], refs[-6:]
     fields, cells, rows, width = src_ref.shape
     half = rows // 2
-    at = {s: i for i, s in reversed(list(enumerate(steps)))}
-    upper_rows = lax.broadcasted_iota(jnp.int32, (8, width), 0) < 4
+    ends = parts[firsts + seconds :]
     entry = []
     for f in range(fields):
         for m in range(4):
             base = (f * 4 + m) * rows
             work_ref[pl.ds(base, half)] = sum(ref[f, m] for ref in parts[:firsts])
             work_ref[pl.ds(base + half, half)] = sum(ref[f, m] for ref in parts[firsts : firsts + seconds])
-
-        def row(s, k):
-            ref = parts[at[s]]
-            if at[s] < firsts + seconds:
-                return ref[f, 4, k : k + 1]
-            return ref[f, k : k + 1]
-
-        sides = None
-        for s in range(len(at)):
-            for k in range(4):
-                value = jnp.where(upper_rows, row(s, k), row(s, 4 + k))
-                term = enter_ref[f, 4 * s + k] * value
-                sides = term if sides is None else sides + term
+        pieces = [(2 * s + k, ref[f, 4 * k : 4 * k + 4]) for s, ref in enumerate(ends) for k in range(2)]
 
         def store(i, value):
             work_ref[pl.ds(f * 4 * rows + i, 4, stride=rows)] = value
@@ -282,8 +313,7 @@
             rad_ref,
             f,
             lambda i: work_ref[pl.ds(f * 4 * rows + i, 4, stride=rows)],
-            sides[0:4],
-            sides[4:8],
+            *(weighted(rad_enter_ref, f, 0, m, pieces) for m in range(2)),
             store,
         )
         entry.append([work_ref[pl.ds((f * 4 + m) * rows, rows)] for m in range(4)])
@@ -348,7 +378,7 @@
     mix_ref[fields + 1] = over_lanes(1.0 - 2.0 * dis, width)
 
 
-def azim_table_kernel(coef_ref, enter_ref, lone_ref):
+def azim_table(coef_ref, enter_ref, lone_ref):
     _, blocks, cells, fields = coef_ref.shape
     width = enter_ref.shape[-1]
     own = lax.axis_index("azim")
@@ -535,15 +565,6 @@
         dissip.reshape(1, fields),
     )
     azim_blocks = azim_coef.reshape(4, fields, azim_count, cells).transpose(0, 2, 3, 1)
-    azim_enter, lone_enter = call(
-        azim_table_kernel,
-        [
-            (fields, len(targets_of(azim_count)), 4, 4 * azim_count, width),
-            (fields * 4 * azim_count * 8, width),
-        ],
-        azim_blocks,
-    )
-    lone_enter = lone_enter.reshape(fields, 4 * azim_count, 8, width)
     rad_blocks = radial_coef.reshape(2, fields, rad_count, rows).transpose(0, 3, 2, 1)
     own_rad, rad_enter = call(
         rad_table_kernel,
@@ -555,56 +576,76 @@
     src, states = call(
         first_kernel, [whole, (fields, 4, rows, width)], own_azim, mixing, residual, scratch=[whole]
     )
+    src = src.reshape(flat)
+    tables = [
+        (fields, len(targets_of(azim_count)), 4, 4 * azim_count, width),
+        (fields * 4 * azim_count * 8, width),
+        (fields, 2, cells, width),
+    ]
+    known = call(early_kernel, tables, azim_blocks, own_rad, src)
     half, small = (fields, 4, rows // 2, width), (fields, 8, width)
+    message = (fields, 5, rows // 2, width)
     one, two, part, end = call(
         patch_kernel,
-        [half, half, (fields, rows, width), small],
+        [message, message, (fields, rows, width), small],
         mixing,
         own_rad,
         halo,
         states,
         reply,
+        known[2],
         scratch=[(fields * 4 * rows, width)],
     )
-    low, high = low_high(azim_count)
-    ones = [from_partner(one, "azim", s) for s in low]
-    twos = [from_partner(two, "azim", s) for s in high]
-    smalls = [from_partner(end, "rad", s) for s in range(rad_count)]
-    src = src.reshape(flat)
-    ends = call(source_kernel, [(fields, 2, cells, width)], own_rad, src, part, scratch=[(width, width)])[0]
-
-    message = (fields, 5, rows // 2, width)
-    *sums, lone = call(
-        lambda *refs: send_kernel(azim_count, low, high, rad_count, *refs),
-        [message] * (len(low) + len(high)) + [small],
+    far, near = low_high(azim_count)
+    ones = [from_partner(one, "azim", s) for s in near]
+    twos = [from_partner(two, "azim", s) for s in far]
+    steps = near + far[1:] + [s for s in range(azim_count) if s not in near + far]
+    lone = [from_partner(end, "azim", s) for s in steps[len(near + far) - 1 :]]
+    lone = [call(pass_kernel, [small], value, cost=10**11)[0] for value in lone]
+    azim_enter, lone_enter, ends = call(
+        late_kernel, tables, azim_blocks, own_rad, src, *known, aliases={3: 0, 4: 1, 5: 2}
+    )
+    lone_enter = lone_enter.reshape(fields, 4 * azim_count, 8, width)
+    low, high = low_high(rad_count)
+    ends = call(
+        halo_ends_kernel, [(fields, 2, cells // 2, width)] * 2, own_rad, part, ends, scratch=[(width, width)]
+    )
+    ends = call(
+        lambda *refs: spread_kernel(rad_count, 2, low, high, *refs),
+        [(fields, 2, cells, width)] * len(high),
+        rad_enter,
+        *(from_partner(value, "rad", s) for s in low for value in ends),
+    )
+    ends = [from_partner(value, "rad", s) for s, value in zip(high, ends)]
+
+    sums = call(
+        lambda enter_ref, _, *refs: send_kernel(azim_count, near, far, enter_ref, *refs),
+        [half] * (len(near) + len(far)),
         azim_enter,
-        rad_enter,
+        lone[-1],
         *ones,
         *twos,
-        *smalls,
         cost=10**11,
     )
-    near, far = low_high(rad_count)
-    gathered = [from_partner(ends, "rad", s) for s in near]
-    entry = call(
-        lambda enter_ref, after_ref, *refs: spread_kernel(rad_count, 2, near, far, enter_ref, *refs),
-        [ends.shape] * len(far),
-        rad_enter,
-        lone,
-        *gathered,
-    )
-    entry = [from_partner(value, "rad", s) for s, value in zip(far, entry)]
-    src = call(radial_kernel, [flat], own_rad, *entry, src, part, scratch=[flat])[0]
-
-    rest = [s for s in range(azim_count) if s not in low + high]
-    parts = [from_partner(value, "azim", s) for s, value in zip(high + low, sums)]
-    parts += [from_partner(lone, "azim", s) for s in rest]
+    parts = [from_partner(value, "azim", s) for s, value in zip(far + near, sums)]
+    end = call(
+        lambda enter_ref, _, *refs: entry_end_kernel(steps, enter_ref, *refs),
+        [small],
+        lone_enter,
+        sums[0],
+        *ones,
+        *twos[1:],
+        *lone,
+    )[0]
+    entry_ends = [from_partner(end, "rad", s) for s in range(rad_count)]
+
+    src = call(radial_kernel, [flat], own_rad, *ends, src, part, scratch=[flat])[0]
 
     chunks = 4
     return pl.pallas_call(
-        lambda *refs: last_kernel(len(high), len(low), high + low + rest, *refs),
+        lambda *refs: last_kernel(len(far), len(near), *refs),
         out_shape=jax.ShapeDtypeStruct(whole, f32),
-        in_specs=[VMEM] * (len(parts) + 4),
+        in_specs=[VMEM] * (len(parts + entry_ends) + 4),
         out_specs=pl.BlockSpec(memory_space=pl.ANY),
         scratch_shapes=[
             pltpu.VMEM(whole, f32),
@@ -613,7 +654,7 @@
             pltpu.SemaphoreType.DMA((chunks,)),
         ],
         compiler_params=params,
-    )(own_azim, lone_enter, own_rad, *parts, src.reshape(whole))
+    )(own_azim, rad_enter, own_rad, *parts, *entry_ends, src.reshape(whole))
 
 
 def solution(mesh):

time: 28.2 us -> 27.1 us (0.961)
  starting transfers between devices: 15.2 us -> 13.7 us
    ppermute x11 -> x12, starting transfers between devices: 15.2 us -> 13.7 us  [from_partner(): lax.ppermute(values, axis, [(i, i ^ step) for i in range(lax.axis_size(ax...]
    ppermute x11 -> x12, waiting for transfers between devices: 3.77 us -> 4.03 us  [from_partner(): lax.ppermute(values, axis, [(i, i ^ step) for i in range(lax.axis_size(ax...]
    pallas_call x10 -> x13, Pallas kernels: 5.59 us -> 5.64 us  [call(): pl.pallas_call(body, out_shape=[jax.ShapeDtypeStruct(shape, f32) for shap...]
    unnamed x18 -> x26, local copies, waits for them, and re-layouts: 1.49 us -> 1.51 us
  transfers between devices with their start and end apart: 11 -> 12, of which waited for: 5 -> 7; matrix products, arithmetic and copies ran while one was open for 1% -> 1% of each run, Pallas kernels for 17% -> 19%
where the time goes in v5:
time: 27.1 us; the launch traced here: 26.9 us
  starting transfers between devices  13.7 us (51%)
  Pallas kernels  7.31 us (27%)
  waiting for transfers between devices  4.03 us (15%)
  local copies, waits for them, and re-layouts  1.73 us (6%)
    ppermute x12, starting transfers between devices, from_partner(): lax.ppermute(values, axis, [(i, i ^ step) for i in range(lax.axis_size(ax...  13.7 us
    pallas_call x13, Pallas kernels, call(): pl.pallas_call(body, out_shape=[jax.ShapeDtypeStruct(shape, f32) for shap...  5.64 us
    ppermute x12, waiting for transfers between devices, from_partner(): lax.ppermute(values, axis, [(i, i ^ step) for i in range(lax.axis_size(ax...  4.03 us
    pallas_call x1, Pallas kernels, local(): pl.pallas_call(lambda *refs: last_kernel(len(far), len(near), *refs), out...  1.67 us
    unnamed x26, local copies, waits for them, and re-layouts  1.51 us
  transfers between devices with their start and end apart: 12, of which 7 were waited for; matrix products, arithmetic and copies ran while one was open for 1% of the time, Pallas kernels for 19%

profile of v5, /device:TPU:0, one launch (start us, length us, event | category | flops | bytes accessed | tf_op | source)
XLA Modules:
  0.0 26.9 jit_solution(7141458513457782126)
XLA Ops:
  0.0 1.3 %copy-done.2 = f32[5,32,16,128]{3,2,1,0:T(8,128)S(1)} copy-done((f32[5,32,16,128]{3,2,1,0:T(8,128)S(1)}, f32[5,32,16,128]{3,2,1,0:T(8,128)}, u32[]{:S(2)}) %copy-start.2) | copy-done | bytes 1310744
  1.3 0.4 %shard_map.60 = f32[5,16,128]{2,1,0:T(8,128)S(1)} custom-call(f32[5,32,16,128]{3,2,1,0:T(8,128)S(1)} %copy-done.2), custom_call_target="tpu_custom_call" | custom-call | tf_op jit(solution)/shard_map/pallas_call | solution.py:14
  1.8 3.0 %collective-permute-start = (f32[5,16,128]{2,1,0:T(8,128)S(1)}, f32[5,16,128]{2,1,0:T(8,128)S(1)}, u32[]{:S(2)}, u32[]{:S(2)}) collective-permute-start(f32[5,16,128]{2,1,0:T(8,128)S(1)} %shard_map.60), channel_id=1, source_target_pairs={{0,1},{1,0},{2,3},{3,2},{4,5},{5,4},{6,7},{7,6},{8,9},{9,8},{10,11... | collective-permute-start | bytes 122888 | tf_op jit(solution)/shard_map/ppermute | solution.py:550
  4.8 0.1 copy.13
  5.0 0.1 reshape.19
  5.0 0.1 copy.12
  5.2 0.4 %shard_map.56 = (f32[5,6,16,128]{3,2,1,0:T(8,128)S(1)}, f32[5,3,2,8,128]{4,3,2,1,0:T(8,128)S(1)}) custom-call(f32[2,16,4,5]{3,2,1,0:T(4,128)S(1)} %bitcast.17), custom_call_target="tpu_custom_call" | custom-call | tf_op jit(solution)/shard_map/pallas_call | solution.py:14
  5.6 0.5 %shard_map.55 = (f32[6,32,5,128]{3,2,1,0:T(8,128)S(1)}, f32[4,5,128]{2,1,0:T(8,128)S(1)}, f32[7,5,128]{2,1,0:T(8,128)S(1)}) custom-call(f32[4,5,128]{2,1,0:T(8,128)S(1)} %copy.11.coef_ref, f32[5,5]{1,0:T(8,128)S(1)} %copy-done.8, f32[1,5]{1,0:T(1,128)S(1)} %bitcast.18), custom_call_target="tpu_custom_call" | custom-call | tf_op jit(solution)/shard_map/pallas_call | solution.py:14
  6.2 1.4 %shard_map.57 = (f32[5,32,16,128]{3,2,1,0:T(8,128)S(1)}, f32[5,4,16,128]{3,2,1,0:T(8,128)S(1)}) custom-call(f32[6,32,5,128]{3,2,1,0:T(8,128)S(1)} %get-tuple-element.30.coef_ref.refs_0_, f32[7,5,128]{2,1,0:T(8,128)S(1)} %get-tuple-element.33.mix_ref, f32[5,32,16,128]{3,2,1,0:T(8,128)S(1)} %copy-done.3), custom_call_target="tpu_custom_call" | custom-call | tf_op jit(solution)/shard_map/pallas_call | solution.py:14
  7.5 0.9 %shard_map.58 = (f32[5,3,4,16,128]{4,3,2,1,0:T(8,128)S(1)}, f32[640,128]{1,0:T(8,128)S(1)}, f32[5,2,32,128]{3,2,1,0:T(8,128)S(1)}) custom-call(f32[4,4,32,5]{3,2,1,0:T(8,128)S(1)} %bitcast.14, f32[5,6,16,128]{3,2,1,0:T(8,128)S(1)} %get-tuple-element.32.rad_ref.refs_2_, f32[2560,128]{1,0:T(8,128)S(1)} %bitcast.10), custom_call_target="tpu_custom_call" | custom-call | tf_op jit(solution)/shard_map/pallas_call | solution.py:14
  8.5 0.2 shard_map.61
  8.7 2.7 %collective-permute-start.1 = (f32[5,8,128]{2,1,0:T(8,128)S(1)}, f32[5,8,128]{2,1,0:T(8,128)S(1)}, u32[]{:S(2)}, u32[]{:S(2)}) collective-permute-start(f32[5,8,128]{2,1,0:T(8,128)S(1)} %get-tuple-element.41), channel_id=1, source_target_pairs={{0,24},{8,16},{16,8},{24,0},{1,25},{9,17},{17,9},{25,1},{2,26},{10... | collective-permute-start | bytes 61448 | tf_op jit(solution)/shard_map/ppermute | solution.py:550
  11.4 1.7 %collective-permute-start.2 = (f32[5,5,8,128]{3,2,1,0:T(8,128)S(1)}, f32[5,5,8,128]{3,2,1,0:T(8,128)S(1)}, u32[]{:S(2)}, u32[]{:S(2)}) collective-permute-start(f32[5,5,8,128]{3,2,1,0:T(8,128)S(1)} %get-tuple-element.42.refs_0_), channel_id=1, source_target_pairs={{0,16},{8,24},{16,0},{24,8},{1,17},{9,25},{17,1},{25,9},{2,18},{10... | collective-permute-start | bytes 307208 | tf_op jit(solution)/shard_map/ppermute | solution.py:550
  13.2 0.3 shard_map.65
  13.4 0.1 collective-permute-start.9
  13.5 0.5 %collective-permute-start.10 = (f32[5,2,16,128]{3,2,1,0:T(8,128)S(1)}, f32[5,2,16,128]{3,2,1,0:T(8,128)S(1)}, u32[]{:S(2)}, u32[]{:S(2)}) collective-permute-start(f32[5,2,16,128]{3,2,1,0:T(8,128)S(1)} %get-tuple-element.52.refs_2_), channel_id=1, source_target_pairs={{0,2},{2,0},{4,6},{6,4},{1,3},{3,1},{5,7},{7,5},{8,10},{10,8},{12,... | collective-permute-start | bytes 245768 | tf_op jit(solution)/shard_map/ppermute | solution.py:550
  14.0 0.6 %collective-permute-done.1.in_ref = f32[5,8,128]{2,1,0:T(8,128)S(1)} collective-permute-done((f32[5,8,128]{2,1,0:T(8,128)S(1)}, f32[5,8,128]{2,1,0:T(8,128)S(1)}, u32[]{:S(2)}, u32[]{:S(2)}) %collective-permute-start.1) | collective-permute-done | bytes 20512 | tf_op jit(solution)/shard_map/ppermute | solution.py:550
  14.6 0.1 collective-permute-done.9.refs_3_
  14.8 0.2 collective-permute-done.10.refs_4_
  14.9 0.1 shard_map.66
  15.0 1.6 %collective-permute-start.11 = (f32[5,2,32,128]{3,2,1,0:T(8,128)S(1)}, f32[5,2,32,128]{3,2,1,0:T(8,128)S(1)}, u32[]{:S(2)}, u32[]{:S(2)}) collective-permute-start(f32[5,2,32,128]{3,2,1,0:T(8,128)S(1)} %get-tuple-element.54), channel_id=1, source_target_pairs={{0,4},{2,6},{4,0},{6,2},{1,5},{3,7},{5,1},{7,3},{8,12},{10,14},{12... | collective-permute-start | bytes 491528 | tf_op jit(solution)/shard_map/ppermute | solution.py:550
  16.6 0.9 %collective-permute-done.3.refs_3_.refs_2_ = f32[5,5,8,128]{3,2,1,0:T(8,128)S(1)} collective-permute-done((f32[5,5,8,128]{3,2,1,0:T(8,128)S(1)}, f32[5,5,8,128]{3,2,1,0:T(8,128)S(1)}, u32[]{:S(2)}, u32[]{:S(2)}) %collective-permute-start.3) | collective-permute-done | bytes 102432 | tf_op jit(solution)/shard_map/ppermute | solution.py:550
  17.5 1.4 %collective-permute-done.2.refs_1_ = f32[5,5,8,128]{3,2,1,0:T(8,128)S(1)} collective-permute-done((f32[5,5,8,128]{3,2,1,0:T(8,128)S(1)}, f32[5,5,8,128]{3,2,1,0:T(8,128)S(1)}, u32[]{:S(2)}, u32[]{:S(2)}) %collective-permute-start.2) | collective-permute-done | bytes 102432 | tf_op jit(solution)/shard_map/ppermute | solution.py:550
  18.9 0.2 shard_map.63
  19.1 0.2 collective-permute-start.4
  19.3 2.0 %collective-permute-start.5 = (f32[5,4,8,128]{3,2,1,0:T(8,128)S(1)}, f32[5,4,8,128]{3,2,1,0:T(8,128)S(1)}, u32[]{:S(2)}, u32[]{:S(2)}) collective-permute-start(f32[5,4,8,128]{3,2,1,0:T(8,128)S(1)} %get-tuple-element.47), channel_id=1, source_target_pairs={{0,16},{8,24},{16,0},{24,8},{1,17},{9,25},{17,1},{25,9},{2,18},{10... | collective-permute-start | bytes 245768 | tf_op jit(solution)/shard_map/ppermute | solution.py:550
  21.4 1.6 %collective-permute-start.7 = (f32[5,8,128]{2,1,0:T(8,128)S(1)}, f32[5,8,128]{2,1,0:T(8,128)S(1)}, u32[]{:S(2)}, u32[]{:S(2)}) collective-permute-start(f32[5,8,128]{2,1,0:T(8,128)S(1)} %shard_map.64.refs_7_), channel_id=1, source_target_pairs={{0,4},{2,6},{4,0},{6,2},{1,5},{3,7},{5,1},{7,3},{8,12},{10,14},{12... | collective-permute-start | bytes 61448 | tf_op jit(solution)/shard_map/ppermute | solution.py:550
  23.0 0.3 %collective-permute-start.6 = (f32[5,8,128]{2,1,0:T(8,128)S(1)}, f32[5,8,128]{2,1,0:T(8,128)S(1)}, u32[]{:S(2)}, u32[]{:S(2)}) collective-permute-start(f32[5,8,128]{2,1,0:T(8,128)S(1)} %shard_map.64.refs_7_), channel_id=1, source_target_pairs={{0,2},{2,0},{4,6},{6,4},{1,3},{3,1},{5,7},{7,5},{8,10},{10,8},{12,... | collective-permute-start | bytes 61448 | tf_op jit(solution)/shard_map/ppermute | solution.py:550
  23.3 1.2 %shard_map.67 = f32[2560,128]{1,0:T(8,128)S(1)} custom-call(f32[5,6,16,128]{3,2,1,0:T(8,128)S(1)} %copy-done.1, f32[5,2,32,128]{3,2,1,0:T(8,128)S(1)} %get-tuple-element.53.refs_0_, f32[5,2,32,128]{3,2,1,0:T(8,128)S(1)} %collective-permute-done.11.refs_1_, f32[2560,128]{1,0:T(8,128)S(1)} %bitcast.12, f32[5,16,128]{2,1,0:T(8,128)S(1)} %copy-done.7), custom_call_target="tpu_custom_call" | custom-call | tf_op jit(solution)/shard_map/pallas_call | solution.py:14
  24.5 0.3 %collective-permute-done.8.refs_10_ = f32[5,8,128]{2,1,0:T(8,128)S(1)} collective-permute-done((f32[5,8,128]{2,1,0:T(8,128)S(1)}, f32[5,8,128]{2,1,0:T(8,128)S(1)}, u32[]{:S(2)}, u32[]{:S(2)}) %collective-permute-start.8) | collective-permute-done | bytes 20512 | tf_op jit(solution)/shard_map/ppermute | solution.py:550
  24.8 0.5 %collective-permute-done.7.refs_9_ = f32[5,8,128]{2,1,0:T(8,128)S(1)} collective-permute-done((f32[5,8,128]{2,1,0:T(8,128)S(1)}, f32[5,8,128]{2,1,0:T(8,128)S(1)}, u32[]{:S(2)}, u32[]{:S(2)}) %collective-permute-start.7) | collective-permute-done | bytes 20512 | tf_op jit(solution)/shard_map/ppermute | solution.py:550
  25.3 1.7 %shard_map.68 = f32[5,32,16,128]{3,2,1,0:T(8,128)} custom-call(f32[6,32,5,128]{3,2,1,0:T(8,128)S(1)} %copy-done.5, f32[5,3,2,8,128]{4,3,2,1,0:T(8,128)S(1)} %get-tuple-element.31.refs_0_.refs_1_, f32[5,6,16,128]{3,2,1,0:T(8,128)S(1)} %copy-done.1, f32[5,4,8,128]{3,2,1,0:T(8,128)S(1)} %get-tuple-element.44._.refs_3_, ...), custom_call_target="tpu_custom_call" | custom-call | tf_op jit(solution)/shard_map/pallas_call | solution.py:645
  (34 shorter events, 0.2 us)
Async XLA Ops:
  0.0 1.3 %copy-start.2 = (f32[5,32,16,128]{3,2,1,0:T(8,128)S(1)}, f32[5,32,16,128]{3,2,1,0:T(8,128)}, u32[]{:S(2)}) copy-start(f32[5,32,16,128]{3,2,1,0:T(8,128)} %res_ref.3) | copy-start | bytes 3932164
  1.3 3.5 %copy-start.10 = (f32[4,5,128]{2,0,1:T(4,128)S(1)}, f32[4,5,128]{2,0,1:T(4,128)}, u32[]{:S(2)}) copy-start(f32[4,5,128]{2,0,1:T(4,128)} %param.8) | copy-start | bytes 30724
  1.3 3.6 %copy-start.11 = (f32[2,5,64]{2,0,1:T(2,128)S(1)}, f32[2,5,64]{2,0,1:T(2,128)}, u32[]{:S(2)}) copy-start(f32[2,5,64]{2,0,1:T(2,128)} %param.9) | copy-start | bytes 7684
  1.3 4.3 %copy-start.8 = (f32[5,5]{1,0:T(8,128)S(1)}, f32[5,5]{1,0:T(8,128)}, u32[]{:S(2)}) copy-start(f32[5,5]{1,0:T(8,128)} %vec_ref.1) | copy-start | bytes 304
  1.3 4.3 %copy-start.9 = (f32[5]{0:T(128)S(1)}, f32[5]{0:T(128)}, u32[]{:S(2)}) copy-start(f32[5]{0:T(128)} %param.7) | copy-start | bytes 64
  1.3 4.8 %copy-start.3 = (f32[5,32,16,128]{3,2,1,0:T(8,128)S(1)}, f32[5,32,16,128]{3,2,1,0:T(8,128)}, u32[]{:S(2)}) copy-start(f32[5,32,16,128]{3,2,1,0:T(8,128)} %res_ref.3) | copy-start | bytes 3932164
  1.8 6.7 %collective-permute-start = (f32[5,16,128]{2,1,0:T(8,128)S(1)}, f32[5,16,128]{2,1,0:T(8,128)S(1)}, u32[]{:S(2)}, u32[]{:S(2)}) collective-permute-start(f32[5,16,128]{2,1,0:T(8,128)S(1)} %shard_map.60), channel_id=1, source_target_pairs={{0,1},{1,0},{2,3},{3,2},{4,5},{5,4},{6,7},{7,6},{8,9},{9,8},{10,11... | collective-permute-start | bytes 122888 | tf_op jit(solution)/shard_map/ppermute | solution.py:550
  5.6 7.6 %copy-start = (f32[5,6,16,128]{3,2,1,0:T(8,128)}, f32[5,6,16,128]{3,2,1,0:T(8,128)S(1)}, u32[]{:S(2)}) copy-start(f32[5,6,16,128]{3,2,1,0:T(8,128)S(1)} %get-tuple-element.32.rad_ref.refs_2_) | copy-start | bytes 737284
  6.1 1.4 %copy-start.4 = (f32[6,32,5,128]{3,2,1,0:T(8,128)}, f32[6,32,5,128]{3,2,1,0:T(8,128)S(1)}, u32[]{:S(2)}) copy-start(f32[6,32,5,128]{3,2,1,0:T(8,128)S(1)} %get-tuple-element.30.coef_ref.refs_0_) | copy-start | bytes 1474564
  8.7 4.5 %copy-start.6 = (f32[5,16,128]{2,1,0:T(8,128)}, f32[5,16,128]{2,1,0:T(8,128)S(1)}, u32[]{:S(2)}) copy-start(f32[5,16,128]{2,1,0:T(8,128)S(1)} %get-tuple-element.49.part_ref.refs_3_) | copy-start | bytes 122884
  8.7 5.9 %collective-permute-start.1 = (f32[5,8,128]{2,1,0:T(8,128)S(1)}, f32[5,8,128]{2,1,0:T(8,128)S(1)}, u32[]{:S(2)}, u32[]{:S(2)}) collective-permute-start(f32[5,8,128]{2,1,0:T(8,128)S(1)} %get-tuple-element.41), channel_id=1, source_target_pairs={{0,24},{8,16},{16,8},{24,0},{1,25},{9,17},{17,9},{25,1},{2,26},{10... | collective-permute-start | bytes 61448 | tf_op jit(solution)/shard_map/ppermute | solution.py:550
  11.4 6.0 %collective-permute-start.3 = (f32[5,5,8,128]{3,2,1,0:T(8,128)S(1)}, f32[5,5,8,128]{3,2,1,0:T(8,128)S(1)}, u32[]{:S(2)}, u32[]{:S(2)}) collective-permute-start(f32[5,5,8,128]{3,2,1,0:T(8,128)S(1)} %get-tuple-element.43.refs_2_), channel_id=1, source_target_pairs={{0,8},{8,0},{16,24},{24,16},{1,9},{9,1},{17,25},{25,17},{2,10},{10... | collective-permute-start | bytes 307208 | tf_op jit(solution)/shard_map/ppermute | solution.py:550
  11.4 7.5 %collective-permute-start.2 = (f32[5,5,8,128]{3,2,1,0:T(8,128)S(1)}, f32[5,5,8,128]{3,2,1,0:T(8,128)S(1)}, u32[]{:S(2)}, u32[]{:S(2)}) collective-permute-start(f32[5,5,8,128]{3,2,1,0:T(8,128)S(1)} %get-tuple-element.42.refs_0_), channel_id=1, source_target_pairs={{0,16},{8,24},{16,0},{24,8},{1,17},{9,25},{17,1},{25,9},{2,18},{10... | collective-permute-start | bytes 307208 | tf_op jit(solution)/shard_map/ppermute | solution.py:550
  13.4 1.3 %collective-permute-start.9 = (f32[5,2,16,128]{3,2,1,0:T(8,128)S(1)}, f32[5,2,16,128]{3,2,1,0:T(8,128)S(1)}, u32[]{:S(2)}, u32[]{:S(2)}) collective-permute-start(f32[5,2,16,128]{3,2,1,0:T(8,128)S(1)} %get-tuple-element.51.refs_1_), channel_id=1, source_target_pairs={{0,2},{2,0},{4,6},{6,4},{1,3},{3,1},{5,7},{7,5},{8,10},{10,8},{12,... | collective-permute-start | bytes 245768 | tf_op jit(solution)/shard_map/ppermute | solution.py:550
  13.5 1.4 %collective-permute-start.10 = (f32[5,2,16,128]{3,2,1,0:T(8,128)S(1)}, f32[5,2,16,128]{3,2,1,0:T(8,128)S(1)}, u32[]{:S(2)}, u32[]{:S(2)}) collective-permute-start(f32[5,2,16,128]{3,2,1,0:T(8,128)S(1)} %get-tuple-element.52.refs_2_), channel_id=1, source_target_pairs={{0,2},{2,0},{4,6},{6,4},{1,3},{3,1},{5,7},{7,5},{8,10},{10,8},{12,... | collective-permute-start | bytes 245768 | tf_op jit(solution)/shard_map/ppermute | solution.py:550
  15.0 7.9 %collective-permute-start.11 = (f32[5,2,32,128]{3,2,1,0:T(8,128)S(1)}, f32[5,2,32,128]{3,2,1,0:T(8,128)S(1)}, u32[]{:S(2)}, u32[]{:S(2)}) collective-permute-start(f32[5,2,32,128]{3,2,1,0:T(8,128)S(1)} %get-tuple-element.54), channel_id=1, source_target_pairs={{0,4},{2,6},{4,0},{6,2},{1,5},{3,7},{5,1},{7,3},{8,12},{10,14},{12... | collective-permute-start | bytes 491528 | tf_op jit(solution)/shard_map/ppermute | solution.py:550
  18.9 4.3 %copy-start.1 = (f32[5,6,16,128]{3,2,1,0:T(8,128)S(1)}, f32[5,6,16,128]{3,2,1,0:T(8,128)}, u32[]{:S(2)}) copy-start(f32[5,6,16,128]{3,2,1,0:T(8,128)} %copy-done) | copy-start | bytes 737284
  18.9 4.3 %copy-start.7 = (f32[5,16,128]{2,1,0:T(8,128)S(1)}, f32[5,16,128]{2,1,0:T(8,128)}, u32[]{:S(2)}) copy-start(f32[5,16,128]{2,1,0:T(8,128)} %copy-done.6) | copy-start | bytes 122884
  19.1 6.1 %collective-permute-start.4 = (f32[5,4,8,128]{3,2,1,0:T(8,128)S(1)}, f32[5,4,8,128]{3,2,1,0:T(8,128)S(1)}, u32[]{:S(2)}, u32[]{:S(2)}) collective-permute-start(f32[5,4,8,128]{3,2,1,0:T(8,128)S(1)} %get-tuple-element.45), channel_id=1, source_target_pairs={{0,8},{8,0},{16,24},{24,16},{1,9},{9,1},{17,25},{25,17},{2,10},{10... | collective-permute-start | bytes 245768 | tf_op jit(solution)/shard_map/ppermute | solution.py:550
  19.3 6.0 %collective-permute-start.5 = (f32[5,4,8,128]{3,2,1,0:T(8,128)S(1)}, f32[5,4,8,128]{3,2,1,0:T(8,128)S(1)}, u32[]{:S(2)}, u32[]{:S(2)}) collective-permute-start(f32[5,4,8,128]{3,2,1,0:T(8,128)S(1)} %get-tuple-element.47), channel_id=1, source_target_pairs={{0,16},{8,24},{16,0},{24,8},{1,17},{9,25},{17,1},{25,9},{2,18},{10... | collective-permute-start | bytes 245768 | tf_op jit(solution)/shard_map/ppermute | solution.py:550
  21.3 3.4 %collective-permute-start.8 = (f32[5,8,128]{2,1,0:T(8,128)S(1)}, f32[5,8,128]{2,1,0:T(8,128)S(1)}, u32[]{:S(2)}, u32[]{:S(2)}) collective-permute-start(f32[5,8,128]{2,1,0:T(8,128)S(1)} %shard_map.64.refs_7_), channel_id=1, source_target_pairs={{0,6},{2,4},{4,2},{6,0},{1,7},{3,5},{5,3},{7,1},{8,14},{10,12},{12... | collective-permute-start | bytes 61448 | tf_op jit(solution)/shard_map/ppermute | solution.py:550
  21.4 3.8 %collective-permute-start.7 = (f32[5,8,128]{2,1,0:T(8,128)S(1)}, f32[5,8,128]{2,1,0:T(8,128)S(1)}, u32[]{:S(2)}, u32[]{:S(2)}) collective-permute-start(f32[5,8,128]{2,1,0:T(8,128)S(1)} %shard_map.64.refs_7_), channel_id=1, source_target_pairs={{0,4},{2,6},{4,0},{6,2},{1,5},{3,7},{5,1},{7,3},{8,12},{10,14},{12... | collective-permute-start | bytes 61448 | tf_op jit(solution)/shard_map/ppermute | solution.py:550
  23.0 2.3 %collective-permute-start.6 = (f32[5,8,128]{2,1,0:T(8,128)S(1)}, f32[5,8,128]{2,1,0:T(8,128)S(1)}, u32[]{:S(2)}, u32[]{:S(2)}) collective-permute-start(f32[5,8,128]{2,1,0:T(8,128)S(1)} %shard_map.64.refs_7_), channel_id=1, source_target_pairs={{0,2},{2,0},{4,6},{6,4},{1,3},{3,1},{5,7},{7,5},{8,10},{10,8},{12,... | collective-permute-start | bytes 61448 | tf_op jit(solution)/shard_map/ppermute | solution.py:550
  23.2 2.0 %copy-start.5 = (f32[6,32,5,128]{3,2,1,0:T(8,128)S(1)}, f32[6,32,5,128]{3,2,1,0:T(8,128)}, u32[]{:S(2)}) copy-start(f32[6,32,5,128]{3,2,1,0:T(8,128)} %copy-done.4) | copy-start | bytes 1474564

commit v6 on v5

--- a/solution.py
+++ b/solution.py
@@ -596,12 +596,12 @@
         known[2],
         scratch=[(fields * 4 * rows, width)],
     )
-    far, near = low_high(azim_count)
+    near, far = low_high(azim_count)
     ones = [from_partner(one, "azim", s) for s in near]
     twos = [from_partner(two, "azim", s) for s in far]
     steps = near + far[1:] + [s for s in range(azim_count) if s not in near + far]
     lone = [from_partner(end, "azim", s) for s in steps[len(near + far) - 1 :]]
-    lone = [call(pass_kernel, [small], value, cost=10**11)[0] for value in lone]
+    lone = [call(pass_kernel, [small], value, cost=6 * 10**8)[0] for value in lone]
     azim_enter, lone_enter, ends = call(
         late_kernel, tables, azim_blocks, own_rad, src, *known, aliases={3: 0, 4: 1, 5: 2}
     )
@@ -619,10 +619,9 @@
     ends = [from_partner(value, "rad", s) for s, value in zip(high, ends)]
 
     sums = call(
-        lambda enter_ref, _, *refs: send_kernel(azim_count, near, far, enter_ref, *refs),
+        lambda *refs: send_kernel(azim_count, near, far, *refs),
         [half] * (len(near) + len(far)),
         azim_enter,
-        lone[-1],
         *ones,
         *twos,
         cost=10**11,

time: 27.1 us -> 25.6 us (0.945)
  waiting for transfers between devices: 4.03 us -> 0.79 us
  starting transfers between devices: 13.7 us -> 15.5 us
    ppermute x12, waiting for transfers between devices: 4.03 us -> 0.79 us  [from_partner(): lax.ppermute(values, axis, [(i, i ^ step) for i in range(lax.axis_size(ax...]
    ppermute x12, starting transfers between devices: 13.7 us -> 15.5 us  [from_partner(): lax.ppermute(values, axis, [(i, i ^ step) for i in range(lax.axis_size(ax...]
    unnamed x26 -> x14, local copies, waits for them, and re-layouts: 1.51 us -> 1.48 us
  transfers between devices with their start and end apart: 12 -> 12, of which waited for: 7 -> 2; matrix products, arithmetic and copies ran while one was open for 1% -> 1% of each run, Pallas kernels for 19% -> 20%
where the time goes in v6:
time: 25.6 us; the launch traced here: 25.4 us
  starting transfers between devices  15.5 us (61%)
  Pallas kernels  7.29 us (28%)
  local copies, waits for them, and re-layouts  1.7 us (7%)
  waiting for transfers between devices  0.79 us (3%)
    ppermute x12, starting transfers between devices, from_partner(): lax.ppermute(values, axis, [(i, i ^ step) for i in range(lax.axis_size(ax...  15.5 us
    pallas_call x13, Pallas kernels, call(): pl.pallas_call(body, out_shape=[jax.ShapeDtypeStruct(shape, f32) for shap...  5.64 us
    pallas_call x1, Pallas kernels, local(): pl.pallas_call(lambda *refs: last_kernel(len(far), len(near), *refs), out...  1.65 us
    unnamed x14, local copies, waits for them, and re-layouts  1.48 us
    ppermute x12, waiting for transfers between devices, from_partner(): lax.ppermute(values, axis, [(i, i ^ step) for i in range(lax.axis_size(ax...  0.79 us
  transfers between devices with their start and end apart: 12, of which 2 were waited for; matrix products, arithmetic and copies ran while one was open for 1% of the time, Pallas kernels for 20%

profile of v6, /device:TPU:0, one launch (start us, length us, event | category | flops | bytes accessed | tf_op | source)
XLA Modules:
  0.0 25.4 jit_solution(12757307316473975491)
XLA Ops:
  0.0 1.3 %copy-done = f32[5,32,16,128]{3,2,1,0:T(8,128)S(1)} copy-done((f32[5,32,16,128]{3,2,1,0:T(8,128)S(1)}, f32[5,32,16,128]{3,2,1,0:T(8,128)}, u32[]{:S(2)}) %copy-start) | copy-done | bytes 1310744
  1.3 0.4 %shard_map.60 = f32[5,16,128]{2,1,0:T(8,128)S(1)} custom-call(f32[5,32,16,128]{3,2,1,0:T(8,128)S(1)} %copy-done), custom_call_target="tpu_custom_call" | custom-call | tf_op jit(solution)/shard_map/pallas_call | solution.py:14
  1.8 3.0 %collective-permute-start = (f32[5,16,128]{2,1,0:T(8,128)S(1)}, f32[5,16,128]{2,1,0:T(8,128)S(1)}, u32[]{:S(2)}, u32[]{:S(2)}) collective-permute-start(f32[5,16,128]{2,1,0:T(8,128)S(1)} %shard_map.60), channel_id=1, source_target_pairs={{0,1},{1,0},{2,3},{3,2},{4,5},{5,4},{6,7},{7,6},{8,9},{9,8},{10,11... | collective-permute-start | bytes 122888 | tf_op jit(solution)/shard_map/ppermute | solution.py:550
  4.8 0.1 copy.13
  5.0 0.1 reshape.19
  5.0 0.1 copy.12
  5.2 0.4 %shard_map.56 = (f32[5,6,16,128]{3,2,1,0:T(8,128)S(1)}, f32[5,3,2,8,128]{4,3,2,1,0:T(8,128)S(1)}) custom-call(f32[2,16,4,5]{3,2,1,0:T(4,128)S(1)} %bitcast.17), custom_call_target="tpu_custom_call" | custom-call | tf_op jit(solution)/shard_map/pallas_call | solution.py:14
  5.6 0.5 %shard_map.55 = (f32[6,32,5,128]{3,2,1,0:T(8,128)S(1)}, f32[4,5,128]{2,1,0:T(8,128)S(1)}, f32[7,5,128]{2,1,0:T(8,128)S(1)}) custom-call(f32[4,5,128]{2,1,0:T(8,128)S(1)} %copy.11.coef_ref, f32[5,5]{1,0:T(8,128)S(1)} %copy-done.2, f32[1,5]{1,0:T(1,128)S(1)} %bitcast.18), custom_call_target="tpu_custom_call" | custom-call | tf_op jit(solution)/shard_map/pallas_call | solution.py:14
  6.1 1.4 %shard_map.57 = (f32[5,32,16,128]{3,2,1,0:T(8,128)S(1)}, f32[5,4,16,128]{3,2,1,0:T(8,128)S(1)}) custom-call(f32[6,32,5,128]{3,2,1,0:T(8,128)S(1)} %get-tuple-element.30.coef_ref.refs_0_, f32[7,5,128]{2,1,0:T(8,128)S(1)} %get-tuple-element.33.mix_ref, f32[5,32,16,128]{3,2,1,0:T(8,128)S(1)} %copy-done.1), custom_call_target="tpu_custom_call" | custom-call | tf_op jit(solution)/shard_map/pallas_call | solution.py:14
  7.5 0.9 %shard_map.58 = (f32[5,3,4,16,128]{4,3,2,1,0:T(8,128)S(1)}, f32[640,128]{1,0:T(8,128)S(1)}, f32[5,2,32,128]{3,2,1,0:T(8,128)S(1)}) custom-call(f32[4,4,32,5]{3,2,1,0:T(8,128)S(1)} %bitcast.14, f32[5,6,16,128]{3,2,1,0:T(8,128)S(1)} %get-tuple-element.32.rad_ref.refs_2_, f32[2560,128]{1,0:T(8,128)S(1)} %bitcast.10), custom_call_target="tpu_custom_call" | custom-call | tf_op jit(solution)/shard_map/pallas_call | solution.py:14
  8.4 0.0 collective-permute-done.halo_ref
  8.5 0.2 shard_map.61
  8.7 1.7 %collective-permute-start.2 = (f32[5,5,8,128]{3,2,1,0:T(8,128)S(1)}, f32[5,5,8,128]{3,2,1,0:T(8,128)S(1)}, u32[]{:S(2)}, u32[]{:S(2)}) collective-permute-start(f32[5,5,8,128]{3,2,1,0:T(8,128)S(1)} %get-tuple-element.42.refs_3_), channel_id=1, source_target_pairs={{0,16},{8,24},{16,0},{24,8},{1,17},{9,25},{17,1},{25,9},{2,18},{10... | collective-permute-start | bytes 307208 | tf_op jit(solution)/shard_map/ppermute | solution.py:550
  10.4 1.6 %collective-permute-start.1 = (f32[5,5,8,128]{3,2,1,0:T(8,128)S(1)}, f32[5,5,8,128]{3,2,1,0:T(8,128)S(1)}, u32[]{:S(2)}, u32[]{:S(2)}) collective-permute-start(f32[5,5,8,128]{3,2,1,0:T(8,128)S(1)} %get-tuple-element.41.refs_1_.refs_0_), channel_id=1, source_target_pairs={{0,8},{8,0},{16,24},{24,16},{1,9},{9,1},{17,25},{25,17},{2,10},{10... | collective-permute-start | bytes 307208 | tf_op jit(solution)/shard_map/ppermute | solution.py:550
  12.0 0.3 %shard_map.65 = (f32[5,2,16,128]{3,2,1,0:T(8,128)S(1)}, f32[5,2,16,128]{3,2,1,0:T(8,128)S(1)}) custom-call(f32[5,6,16,128]{3,2,1,0:T(8,128)S(1)} %get-tuple-element.32.rad_ref.refs_2_, f32[5,16,128]{2,1,0:T(8,128)S(1)} %get-tuple-element.49.part_ref.refs_3_, f32[5,2,32,128]{3,2,1,0:T(8,128)S(1)} %get-tuple-element.50.known_ref), custom_call_target="tpu_custom_call" | custom-call | tf_op jit(solution)/shard_map/pallas_call | solution.py:14
  12.2 0.1 collective-permute-start.9
  12.3 0.5 %collective-permute-start.10 = (f32[5,2,16,128]{3,2,1,0:T(8,128)S(1)}, f32[5,2,16,128]{3,2,1,0:T(8,128)S(1)}, u32[]{:S(2)}, u32[]{:S(2)}) collective-permute-start(f32[5,2,16,128]{3,2,1,0:T(8,128)S(1)} %get-tuple-element.52.refs_2_), channel_id=1, source_target_pairs={{0,2},{2,0},{4,6},{6,4},{1,3},{3,1},{5,7},{7,5},{8,10},{10,8},{12,... | collective-permute-start | bytes 245768 | tf_op jit(solution)/shard_map/ppermute | solution.py:550
  12.8 2.1 %collective-permute-start.5 = (f32[5,8,128]{2,1,0:T(8,128)S(1)}, f32[5,8,128]{2,1,0:T(8,128)S(1)}, u32[]{:S(2)}, u32[]{:S(2)}) collective-permute-start(f32[5,8,128]{2,1,0:T(8,128)S(1)} %get-tuple-element.48), channel_id=1, source_target_pairs={{0,24},{8,16},{16,8},{24,0},{1,25},{9,17},{17,9},{25,1},{2,26},{10... | collective-permute-start | bytes 61448 | tf_op jit(solution)/shard_map/ppermute | solution.py:550
  14.9 0.0 collective-permute-done.9.refs_3_
  14.9 0.1 shard_map.66
  15.0 1.6 %collective-permute-start.11 = (f32[5,2,32,128]{3,2,1,0:T(8,128)S(1)}, f32[5,2,32,128]{3,2,1,0:T(8,128)S(1)}, u32[]{:S(2)}, u32[]{:S(2)}) collective-permute-start(f32[5,2,32,128]{3,2,1,0:T(8,128)S(1)} %get-tuple-element.54), channel_id=1, source_target_pairs={{0,4},{2,6},{4,0},{6,2},{1,5},{3,7},{5,1},{7,3},{8,12},{10,14},{12... | collective-permute-start | bytes 491528 | tf_op jit(solution)/shard_map/ppermute | solution.py:550
  16.5 0.2 shard_map.62
  16.7 1.3 %collective-permute-start.3 = (f32[5,4,8,128]{3,2,1,0:T(8,128)S(1)}, f32[5,4,8,128]{3,2,1,0:T(8,128)S(1)}, u32[]{:S(2)}, u32[]{:S(2)}) collective-permute-start(f32[5,4,8,128]{3,2,1,0:T(8,128)S(1)} %get-tuple-element.44), channel_id=1, source_target_pairs={{0,16},{8,24},{16,0},{24,8},{1,17},{9,25},{17,1},{25,9},{2,18},{10... | collective-permute-start | bytes 245768 | tf_op jit(solution)/shard_map/ppermute | solution.py:550
  18.0 1.8 %collective-permute-start.4 = (f32[5,4,8,128]{3,2,1,0:T(8,128)S(1)}, f32[5,4,8,128]{3,2,1,0:T(8,128)S(1)}, u32[]{:S(2)}, u32[]{:S(2)}) collective-permute-start(f32[5,4,8,128]{3,2,1,0:T(8,128)S(1)} %get-tuple-element.46), channel_id=1, source_target_pairs={{0,8},{8,0},{16,24},{24,16},{1,9},{9,1},{17,25},{25,17},{2,10},{10... | collective-permute-start | bytes 245768 | tf_op jit(solution)/shard_map/ppermute | solution.py:550
  19.8 0.1 shard_map.64.refs_7_
  19.8 0.1 collective-permute-start.8
  19.9 1.6 %collective-permute-start.7 = (f32[5,8,128]{2,1,0:T(8,128)S(1)}, f32[5,8,128]{2,1,0:T(8,128)S(1)}, u32[]{:S(2)}, u32[]{:S(2)}) collective-permute-start(f32[5,8,128]{2,1,0:T(8,128)S(1)} %shard_map.64.refs_7_), channel_id=1, source_target_pairs={{0,4},{2,6},{4,0},{6,2},{1,5},{3,7},{5,1},{7,3},{8,12},{10,14},{12... | collective-permute-start | bytes 61448 | tf_op jit(solution)/shard_map/ppermute | solution.py:550
  21.5 0.3 %collective-permute-start.6 = (f32[5,8,128]{2,1,0:T(8,128)S(1)}, f32[5,8,128]{2,1,0:T(8,128)S(1)}, u32[]{:S(2)}, u32[]{:S(2)}) collective-permute-start(f32[5,8,128]{2,1,0:T(8,128)S(1)} %shard_map.64.refs_7_), channel_id=1, source_target_pairs={{0,2},{2,0},{4,6},{6,4},{1,3},{3,1},{5,7},{7,5},{8,10},{10,8},{12,... | collective-permute-start | bytes 61448 | tf_op jit(solution)/shard_map/ppermute | solution.py:550
  21.8 1.2 %shard_map.67 = f32[2560,128]{1,0:T(8,128)S(1)} custom-call(f32[5,6,16,128]{3,2,1,0:T(8,128)S(1)} %get-tuple-element.32.rad_ref.refs_2_, f32[5,2,32,128]{3,2,1,0:T(8,128)S(1)} %get-tuple-element.53.refs_0_, f32[5,2,32,128]{3,2,1,0:T(8,128)S(1)} %collective-permute-done.11.refs_1_, f32[2560,128]{1,0:T(8,128)S(1)} %bitcast.12, ...), custom_call_target="tpu_custom_call" | custom-call | tf_op jit(solution)/shard_map/pallas_call | solution.py:14
  23.0 0.3 %collective-permute-done.8.refs_10_ = f32[5,8,128]{2,1,0:T(8,128)S(1)} collective-permute-done((f32[5,8,128]{2,1,0:T(8,128)S(1)}, f32[5,8,128]{2,1,0:T(8,128)S(1)}, u32[]{:S(2)}, u32[]{:S(2)}) %collective-permute-start.8) | collective-permute-done | bytes 20512 | tf_op jit(solution)/shard_map/ppermute | solution.py:550
  23.3 0.5 %collective-permute-done.7.refs_9_ = f32[5,8,128]{2,1,0:T(8,128)S(1)} collective-permute-done((f32[5,8,128]{2,1,0:T(8,128)S(1)}, f32[5,8,128]{2,1,0:T(8,128)S(1)}, u32[]{:S(2)}, u32[]{:S(2)}) %collective-permute-start.7) | collective-permute-done | bytes 20512 | tf_op jit(solution)/shard_map/ppermute | solution.py:550
  23.8 1.6 %shard_map.68 = f32[5,32,16,128]{3,2,1,0:T(8,128)} custom-call(f32[6,32,5,128]{3,2,1,0:T(8,128)S(1)} %get-tuple-element.30.coef_ref.refs_0_, f32[5,3,2,8,128]{4,3,2,1,0:T(8,128)S(1)} %get-tuple-element.31.refs_0_.refs_1_, f32[5,6,16,128]{3,2,1,0:T(8,128)S(1)} %get-tuple-element.32.rad_ref.refs_2_, f32[5,4,8,128]{3,2,1,0:T(8,128)S(1)} %get-tuple-element.43._.refs_3_, ...), custom_call_target="tpu_custom_call" | custom-call | tf_op jit(solution)/shard_map/pallas_call | solution.py:644
  (22 shorter events, 0.0 us)
Async XLA Ops:
  0.0 1.3 %copy-start = (f32[5,32,16,128]{3,2,1,0:T(8,128)S(1)}, f32[5,32,16,128]{3,2,1,0:T(8,128)}, u32[]{:S(2)}) copy-start(f32[5,32,16,128]{3,2,1,0:T(8,128)} %res_ref.3) | copy-start | bytes 3932164
  1.3 3.5 %copy-start.4 = (f32[4,5,128]{2,0,1:T(4,128)S(1)}, f32[4,5,128]{2,0,1:T(4,128)}, u32[]{:S(2)}) copy-start(f32[4,5,128]{2,0,1:T(4,128)} %param.8) | copy-start | bytes 30724
  1.3 3.6 %copy-start.5 = (f32[2,5,64]{2,0,1:T(2,128)S(1)}, f32[2,5,64]{2,0,1:T(2,128)}, u32[]{:S(2)}) copy-start(f32[2,5,64]{2,0,1:T(2,128)} %param.9) | copy-start | bytes 7684
  1.3 4.3 %copy-start.2 = (f32[5,5]{1,0:T(8,128)S(1)}, f32[5,5]{1,0:T(8,128)}, u32[]{:S(2)}) copy-start(f32[5,5]{1,0:T(8,128)} %vec_ref.1) | copy-start | bytes 304
  1.3 4.3 %copy-start.3 = (f32[5]{0:T(128)S(1)}, f32[5]{0:T(128)}, u32[]{:S(2)}) copy-start(f32[5]{0:T(128)} %param.7) | copy-start | bytes 64
  1.3 4.8 %copy-start.1 = (f32[5,32,16,128]{3,2,1,0:T(8,128)S(1)}, f32[5,32,16,128]{3,2,1,0:T(8,128)}, u32[]{:S(2)}) copy-start(f32[5,32,16,128]{3,2,1,0:T(8,128)} %res_ref.3) | copy-start | bytes 3932164
  1.8 6.7 %collective-permute-start = (f32[5,16,128]{2,1,0:T(8,128)S(1)}, f32[5,16,128]{2,1,0:T(8,128)S(1)}, u32[]{:S(2)}, u32[]{:S(2)}) collective-permute-start(f32[5,16,128]{2,1,0:T(8,128)S(1)} %shard_map.60), channel_id=1, source_target_pairs={{0,1},{1,0},{2,3},{3,2},{4,5},{5,4},{6,7},{7,6},{8,9},{9,8},{10,11... | collective-permute-start | bytes 122888 | tf_op jit(solution)/shard_map/ppermute | solution.py:550
  8.7 7.9 %collective-permute-start.2 = (f32[5,5,8,128]{3,2,1,0:T(8,128)S(1)}, f32[5,5,8,128]{3,2,1,0:T(8,128)S(1)}, u32[]{:S(2)}, u32[]{:S(2)}) collective-permute-start(f32[5,5,8,128]{3,2,1,0:T(8,128)S(1)} %get-tuple-element.42.refs_3_), channel_id=1, source_target_pairs={{0,16},{8,24},{16,0},{24,8},{1,17},{9,25},{17,1},{25,9},{2,18},{10... | collective-permute-start | bytes 307208 | tf_op jit(solution)/shard_map/ppermute | solution.py:550
  10.4 6.2 %collective-permute-start.1 = (f32[5,5,8,128]{3,2,1,0:T(8,128)S(1)}, f32[5,5,8,128]{3,2,1,0:T(8,128)S(1)}, u32[]{:S(2)}, u32[]{:S(2)}) collective-permute-start(f32[5,5,8,128]{3,2,1,0:T(8,128)S(1)} %get-tuple-element.41.refs_1_.refs_0_), channel_id=1, source_target_pairs={{0,8},{8,0},{16,24},{24,16},{1,9},{9,1},{17,25},{25,17},{2,10},{10... | collective-permute-start | bytes 307208 | tf_op jit(solution)/shard_map/ppermute | solution.py:550
  12.2 2.7 %collective-permute-start.9 = (f32[5,2,16,128]{3,2,1,0:T(8,128)S(1)}, f32[5,2,16,128]{3,2,1,0:T(8,128)S(1)}, u32[]{:S(2)}, u32[]{:S(2)}) collective-permute-start(f32[5,2,16,128]{3,2,1,0:T(8,128)S(1)} %get-tuple-element.51.refs_1_), channel_id=1, source_target_pairs={{0,2},{2,0},{4,6},{6,4},{1,3},{3,1},{5,7},{7,5},{8,10},{10,8},{12,... | collective-permute-start | bytes 245768 | tf_op jit(solution)/shard_map/ppermute | solution.py:550
  12.3 2.6 %collective-permute-start.10 = (f32[5,2,16,128]{3,2,1,0:T(8,128)S(1)}, f32[5,2,16,128]{3,2,1,0:T(8,128)S(1)}, u32[]{:S(2)}, u32[]{:S(2)}) collective-permute-start(f32[5,2,16,128]{3,2,1,0:T(8,128)S(1)} %get-tuple-element.52.refs_2_), channel_id=1, source_target_pairs={{0,2},{2,0},{4,6},{6,4},{1,3},{3,1},{5,7},{7,5},{8,10},{10,8},{12,... | collective-permute-start | bytes 245768 | tf_op jit(solution)/shard_map/ppermute | solution.py:550
  12.8 7.0 %collective-permute-start.5 = (f32[5,8,128]{2,1,0:T(8,128)S(1)}, f32[5,8,128]{2,1,0:T(8,128)S(1)}, u32[]{:S(2)}, u32[]{:S(2)}) collective-permute-start(f32[5,8,128]{2,1,0:T(8,128)S(1)} %get-tuple-element.48), channel_id=1, source_target_pairs={{0,24},{8,16},{16,8},{24,0},{1,25},{9,17},{17,9},{25,1},{2,26},{10... | collective-permute-start | bytes 61448 | tf_op jit(solution)/shard_map/ppermute | solution.py:550
  15.0 6.5 %collective-permute-start.11 = (f32[5,2,32,128]{3,2,1,0:T(8,128)S(1)}, f32[5,2,32,128]{3,2,1,0:T(8,128)S(1)}, u32[]{:S(2)}, u32[]{:S(2)}) collective-permute-start(f32[5,2,32,128]{3,2,1,0:T(8,128)S(1)} %get-tuple-element.54), channel_id=1, source_target_pairs={{0,4},{2,6},{4,0},{6,2},{1,5},{3,7},{5,1},{7,3},{8,12},{10,14},{12... | collective-permute-start | bytes 491528 | tf_op jit(solution)/shard_map/ppermute | solution.py:550
  16.7 7.0 %collective-permute-start.3 = (f32[5,4,8,128]{3,2,1,0:T(8,128)S(1)}, f32[5,4,8,128]{3,2,1,0:T(8,128)S(1)}, u32[]{:S(2)}, u32[]{:S(2)}) collective-permute-start(f32[5,4,8,128]{3,2,1,0:T(8,128)S(1)} %get-tuple-element.44), channel_id=1, source_target_pairs={{0,16},{8,24},{16,0},{24,8},{1,17},{9,25},{17,1},{25,9},{2,18},{10... | collective-permute-start | bytes 245768 | tf_op jit(solution)/shard_map/ppermute | solution.py:550
  18.0 5.8 %collective-permute-start.4 = (f32[5,4,8,128]{3,2,1,0:T(8,128)S(1)}, f32[5,4,8,128]{3,2,1,0:T(8,128)S(1)}, u32[]{:S(2)}, u32[]{:S(2)}) collective-permute-start(f32[5,4,8,128]{3,2,1,0:T(8,128)S(1)} %get-tuple-element.46), channel_id=1, source_target_pairs={{0,8},{8,0},{16,24},{24,16},{1,9},{9,1},{17,25},{25,17},{2,10},{10... | collective-permute-start | bytes 245768 | tf_op jit(solution)/shard_map/ppermute | solution.py:550
  19.8 3.4 %collective-permute-start.8 = (f32[5,8,128]{2,1,0:T(8,128)S(1)}, f32[5,8,128]{2,1,0:T(8,128)S(1)}, u32[]{:S(2)}, u32[]{:S(2)}) collective-permute-start(f32[5,8,128]{2,1,0:T(8,128)S(1)} %shard_map.64.refs_7_), channel_id=1, source_target_pairs={{0,6},{2,4},{4,2},{6,0},{1,7},{3,5},{5,3},{7,1},{8,14},{10,12},{12... | collective-permute-start | bytes 61448 | tf_op jit(solution)/shard_map/ppermute | solution.py:550
  19.9 3.8 %collective-permute-start.7 = (f32[5,8,128]{2,1,0:T(8,128)S(1)}, f32[5,8,128]{2,1,0:T(8,128)S(1)}, u32[]{:S(2)}, u32[]{:S(2)}) collective-permute-start(f32[5,8,128]{2,1,0:T(8,128)S(1)} %shard_map.64.refs_7_), channel_id=1, source_target_pairs={{0,4},{2,6},{4,0},{6,2},{1,5},{3,7},{5,1},{7,3},{8,12},{10,14},{12... | collective-permute-start | bytes 61448 | tf_op jit(solution)/shard_map/ppermute | solution.py:550
  21.5 2.3 %collective-permute-start.6 = (f32[5,8,128]{2,1,0:T(8,128)S(1)}, f32[5,8,128]{2,1,0:T(8,128)S(1)}, u32[]{:S(2)}, u32[]{:S(2)}) collective-permute-start(f32[5,8,128]{2,1,0:T(8,128)S(1)} %shard_map.64.refs_7_), channel_id=1, source_target_pairs={{0,2},{2,0},{4,6},{6,4},{1,3},{3,1},{5,7},{7,5},{8,10},{10,8},{12,... | collective-permute-start | bytes 61448 | tf_op jit(solution)/shard_map/ppermute | solution.py:550

commit v7 on v6

--- a/solution.py
+++ b/solution.py
@@ -202,20 +202,33 @@
 
 
 def first_half():
-    return lax.axis_index("azim") < lax.axis_size("azim") // 2
-
-
-def early_kernel(coef_ref, rad_ref, src_ref, enter_ref, lone_ref, end_ref):
+    return lax.axis_index("azim") < lax.axis_size("azim") // 4
+
+
+def azim_blocks(coef_ref, turn_ref, block_ref):
+    kinds, blocks, cells, width = block_ref.shape
+    fields = coef_ref.shape[1]
+    turn_ref[...] = jnp.zeros(turn_ref.shape, f32)
+    for kind in range(kinds):
+        turn_ref[8 * kind : 8 * kind + fields] = coef_ref[kind]
+    turned = jnp.transpose(turn_ref[...])
+    for kind in range(kinds):
+        block_ref[kind] = pltpu.roll(turned, (width - 8 * kind) % width, 1).reshape(blocks, cells, width)
+
+
+def early_kernel(coef_ref, rad_ref, src_ref, enter_ref, lone_ref, end_ref, turn_ref, block_ref):
     @pl.when(first_half())
     def _():
-        azim_table(coef_ref, enter_ref, lone_ref)
+        azim_blocks(coef_ref, turn_ref, block_ref)
+        azim_table(block_ref, enter_ref, lone_ref)
         source_ends(rad_ref, src_ref, end_ref)
 
 
-def late_kernel(coef_ref, rad_ref, src_ref, _, __, ___, enter_ref, lone_ref, end_ref):
+def late_kernel(coef_ref, rad_ref, src_ref, _, __, ___, enter_ref, lone_ref, end_ref, turn_ref, block_ref):
     @pl.when(jnp.logical_not(first_half()))
     def _():
-        azim_table(coef_ref, enter_ref, lone_ref)
+        azim_blocks(coef_ref, turn_ref, block_ref)
+        azim_table(block_ref, enter_ref, lone_ref)
         source_ends(rad_ref, src_ref, end_ref)
 
 
@@ -373,14 +386,14 @@
         mix_ref[f] = over_lanes(vec_ref[:, f : f + 1], width)
     square = (fields, fields)
     diagonal = lanes_of(square) == lax.broadcasted_iota(jnp.int32, square, 0)
-    dis = jnp.sum(jnp.where(diagonal, dis_ref[...], 0.0), axis=1, keepdims=True)
+    dis = jnp.sum(jnp.where(diagonal, dis_ref[...].reshape(1, fields), 0.0), axis=1, keepdims=True)
     mix_ref[fields] = over_lanes(dis, width)
     mix_ref[fields + 1] = over_lanes(1.0 - 2.0 * dis, width)
 
 
 def azim_table(coef_ref, enter_ref, lone_ref):
-    _, blocks, cells, fields = coef_ref.shape
-    width = enter_ref.shape[-1]
+    _, blocks, cells, width = coef_ref.shape
+    fields = enter_ref.shape[0]
     own = lax.axis_index("azim")
     unit = lax.broadcasted_iota(jnp.int32, (blocks, 8, fields), 1)
 
@@ -390,13 +403,13 @@
     one, two = ones(0), ones(1)
     held = []
     for j in range(cells):
-        z = coef_ref[0, :, j : j + 1] * one + coef_ref[1, :, j : j + 1] * two
+        z = coef_ref[0, :, j : j + 1, :fields] * one + coef_ref[1, :, j : j + 1, :fields] * two
         held.append(z)
         one, two = z, one
     lower = (one, two)
     one, two = ones(2), ones(3)
     for j in reversed(range(cells)):
-        c, e = coef_ref[2, :, j : j + 1], coef_ref[3, :, j : j + 1]
+        c, e = coef_ref[2, :, j : j + 1, :fields], coef_ref[3, :, j : j + 1, :fields]
         v = weight(c, e) * held[j] + c * one + e * two
         one, two = v, one
     upper = (one, two)
@@ -562,15 +575,14 @@
         [(6, cells, fields, width), (4, fields, width), (fields + 2, fields, width)],
         azim_coef,
         left_vec,
-        dissip.reshape(1, fields),
-    )
-    azim_blocks = azim_coef.reshape(4, fields, azim_count, cells).transpose(0, 2, 3, 1)
+        dissip,
+    )
     rad_blocks = radial_coef.reshape(2, fields, rad_count, rows).transpose(0, 3, 2, 1)
     own_rad, rad_enter = call(
         rad_table_kernel,
         [(fields, 6, rows, width), (fields, len(targets_of(rad_count)), 2, 2 * rad_count, width)],
         rad_blocks,
-        scratch=[(6 * rows * -(-rad_count // 8) * 8, fields)],
+        scratch=[((6 * rows + 1) * -(-rad_count // 8) * 8, fields)],
     )
 
     src, states = call(
@@ -582,7 +594,8 @@
         (fields * 4 * azim_count * 8, width),
         (fields, 2, cells, width),
     ]
-    known = call(early_kernel, tables, azim_blocks, own_rad, src)
+    turning = [(width, azim_count * cells), (4, azim_count, cells, width)]
+    known = call(early_kernel, tables, azim_coef, own_rad, src, scratch=turning)
     half, small = (fields, 4, rows // 2, width), (fields, 8, width)
     message = (fields, 5, rows // 2, width)
     one, two, part, end = call(
@@ -603,7 +616,7 @@
     lone = [from_partner(end, "azim", s) for s in steps[len(near + far) - 1 :]]
     lone = [call(pass_kernel, [small], value, cost=6 * 10**8)[0] for value in lone]
     azim_enter, lone_enter, ends = call(
-        late_kernel, tables, azim_blocks, own_rad, src, *known, aliases={3: 0, 4: 1, 5: 2}
+        late_kernel, tables, azim_coef, own_rad, src, *known, scratch=turning, aliases={3: 0, 4: 1, 5: 2}
     )
     lone_enter = lone_enter.reshape(fields, 4 * azim_count, 8, width)
     low, high = low_high(rad_count)

time: 25.6 us -> 25.4 us (level)
    unnamed x14 -> x13, local copies, waits for them, and re-layouts: 1.48 us -> 1.34 us
  transfers between devices with their start and end apart: 12 -> 12, of which waited for: 2 -> 2; matrix products, arithmetic and copies ran while one was open for 1% -> 1% of each run, Pallas kernels for 20% -> 21%
where the time goes in v7:
time: 25.4 us; the launch traced here: 25.3 us
  starting transfers between devices  15.3 us (60%)
  Pallas kernels  7.47 us (29%)
  local copies, waits for them, and re-layouts  1.56 us (6%)
  waiting for transfers between devices  0.79 us (3%)
    ppermute x12, starting transfers between devices, from_partner(): lax.ppermute(values, axis, [(i, i ^ step) for i in range(lax.axis_size(ax...  15.3 us
    pallas_call x13, Pallas kernels, call(): pl.pallas_call(body, out_shape=[jax.ShapeDtypeStruct(shape, f32) for shap...  5.82 us
    pallas_call x1, Pallas kernels, local(): pl.pallas_call(lambda *refs: last_kernel(len(far), len(near), *refs), out...  1.65 us
    unnamed x13, local copies, waits for them, and re-layouts  1.34 us
    ppermute x12, waiting for transfers between devices, from_partner(): lax.ppermute(values, axis, [(i, i ^ step) for i in range(lax.axis_size(ax...  0.79 us
  transfers between devices with their start and end apart: 12, of which 2 were waited for; matrix products, arithmetic and copies ran while one was open for 1% of the time, Pallas kernels for 21%

profile of v7, /device:TPU:0, one launch (start us, length us, event | category | flops | bytes accessed | tf_op | source)
XLA Modules:
  0.0 25.3 jit_solution(6440861444573319222)
XLA Ops:
  0.0 1.3 %copy-done = f32[5,32,16,128]{3,2,1,0:T(8,128)S(1)} copy-done((f32[5,32,16,128]{3,2,1,0:T(8,128)S(1)}, f32[5,32,16,128]{3,2,1,0:T(8,128)}, u32[]{:S(2)}) %copy-start) | copy-done | bytes 1310744
  1.3 0.4 %shard_map.60 = f32[5,16,128]{2,1,0:T(8,128)S(1)} custom-call(f32[5,32,16,128]{3,2,1,0:T(8,128)S(1)} %copy-done), custom_call_target="tpu_custom_call" | custom-call | tf_op jit(solution)/shard_map/pallas_call | solution.py:14
  1.8 3.0 %collective-permute-start = (f32[5,16,128]{2,1,0:T(8,128)S(1)}, f32[5,16,128]{2,1,0:T(8,128)S(1)}, u32[]{:S(2)}, u32[]{:S(2)}) collective-permute-start(f32[5,16,128]{2,1,0:T(8,128)S(1)} %shard_map.60), channel_id=1, source_target_pairs={{0,1},{1,0},{2,3},{3,2},{4,5},{5,4},{6,7},{7,6},{8,9},{9,8},{10,11... | collective-permute-start | bytes 122888 | tf_op jit(solution)/shard_map/ppermute | solution.py:563
  4.8 0.1 reshape.12
  4.9 0.1 copy.13
  5.0 0.4 %shard_map.56 = (f32[5,6,16,128]{3,2,1,0:T(8,128)S(1)}, f32[5,3,2,8,128]{4,3,2,1,0:T(8,128)S(1)}) custom-call(f32[2,16,4,5]{3,2,1,0:T(4,128)S(1)} %bitcast.11), custom_call_target="tpu_custom_call" | custom-call | tf_op jit(solution)/shard_map/pallas_call | solution.py:14
  5.4 0.5 %shard_map.55 = (f32[6,32,5,128]{3,2,1,0:T(8,128)S(1)}, f32[4,5,128]{2,1,0:T(8,128)S(1)}, f32[7,5,128]{2,1,0:T(8,128)S(1)}) custom-call(f32[4,5,128]{2,1,0:T(8,128)S(1)} %copy.12.coef_ref, f32[5,5]{1,0:T(8,128)S(1)} %copy-done.2, f32[5]{0:T(128)S(1)} %copy-done.3), custom_call_target="tpu_custom_call" | custom-call | tf_op jit(solution)/shard_map/pallas_call | solution.py:14
  6.0 1.4 %shard_map.57 = (f32[5,32,16,128]{3,2,1,0:T(8,128)S(1)}, f32[5,4,16,128]{3,2,1,0:T(8,128)S(1)}) custom-call(f32[6,32,5,128]{3,2,1,0:T(8,128)S(1)} %get-tuple-element.30.coef_ref.refs_0_, f32[7,5,128]{2,1,0:T(8,128)S(1)} %get-tuple-element.33.mix_ref, f32[5,32,16,128]{3,2,1,0:T(8,128)S(1)} %copy-done.1), custom_call_target="tpu_custom_call" | custom-call | tf_op jit(solution)/shard_map/pallas_call | solution.py:14
  7.3 1.1 %shard_map.58 = (f32[5,3,4,16,128]{4,3,2,1,0:T(8,128)S(1)}, f32[640,128]{1,0:T(8,128)S(1)}, f32[5,2,32,128]{3,2,1,0:T(8,128)S(1)}) custom-call(f32[4,5,128]{2,1,0:T(8,128)S(1)} %copy.12.coef_ref, f32[5,6,16,128]{3,2,1,0:T(8,128)S(1)} %get-tuple-element.32.rad_ref.refs_2_, f32[2560,128]{1,0:T(8,128)S(1)} %bitcast.6), custom_call_target="tpu_custom_call" | custom-call | tf_op jit(solution)/shard_map/pallas_call | solution.py:14
  8.5 0.0 collective-permute-done.halo_ref
  8.5 0.2 shard_map.61
  8.7 1.5 %collective-permute-start.2 = (f32[5,5,8,128]{3,2,1,0:T(8,128)S(1)}, f32[5,5,8,128]{3,2,1,0:T(8,128)S(1)}, u32[]{:S(2)}, u32[]{:S(2)}) collective-permute-start(f32[5,5,8,128]{3,2,1,0:T(8,128)S(1)} %get-tuple-element.42.refs_3_), channel_id=1, source_target_pairs={{0,16},{8,24},{16,0},{24,8},{1,17},{9,25},{17,1},{25,9},{2,18},{10... | collective-permute-start | bytes 307208 | tf_op jit(solution)/shard_map/ppermute | solution.py:563
  10.2 1.6 %collective-permute-start.1 = (f32[5,5,8,128]{3,2,1,0:T(8,128)S(1)}, f32[5,5,8,128]{3,2,1,0:T(8,128)S(1)}, u32[]{:S(2)}, u32[]{:S(2)}) collective-permute-start(f32[5,5,8,128]{3,2,1,0:T(8,128)S(1)} %get-tuple-element.41.refs_1_.refs_0_), channel_id=1, source_target_pairs={{0,8},{8,0},{16,24},{24,16},{1,9},{9,1},{17,25},{25,17},{2,10},{10... | collective-permute-start | bytes 307208 | tf_op jit(solution)/shard_map/ppermute | solution.py:563
  11.8 0.3 %shard_map.65 = (f32[5,2,16,128]{3,2,1,0:T(8,128)S(1)}, f32[5,2,16,128]{3,2,1,0:T(8,128)S(1)}) custom-call(f32[5,6,16,128]{3,2,1,0:T(8,128)S(1)} %get-tuple-element.32.rad_ref.refs_2_, f32[5,16,128]{2,1,0:T(8,128)S(1)} %get-tuple-element.49.part_ref.refs_3_, f32[5,2,32,128]{3,2,1,0:T(8,128)S(1)} %get-tuple-element.50.known_ref), custom_call_target="tpu_custom_call" | custom-call | tf_op jit(solution)/shard_map/pallas_call | solution.py:14
  12.1 0.1 collective-permute-start.9
  12.2 0.5 %collective-permute-start.10 = (f32[5,2,16,128]{3,2,1,0:T(8,128)S(1)}, f32[5,2,16,128]{3,2,1,0:T(8,128)S(1)}, u32[]{:S(2)}, u32[]{:S(2)}) collective-permute-start(f32[5,2,16,128]{3,2,1,0:T(8,128)S(1)} %get-tuple-element.52.refs_2_), channel_id=1, source_target_pairs={{0,2},{2,0},{4,6},{6,4},{1,3},{3,1},{5,7},{7,5},{8,10},{10,8},{12,... | collective-permute-start | bytes 245768 | tf_op jit(solution)/shard_map/ppermute | solution.py:563
  12.7 2.4 %collective-permute-start.5 = (f32[5,8,128]{2,1,0:T(8,128)S(1)}, f32[5,8,128]{2,1,0:T(8,128)S(1)}, u32[]{:S(2)}, u32[]{:S(2)}) collective-permute-start(f32[5,8,128]{2,1,0:T(8,128)S(1)} %get-tuple-element.48), channel_id=1, source_target_pairs={{0,24},{8,16},{16,8},{24,0},{1,25},{9,17},{17,9},{25,1},{2,26},{10... | collective-permute-start | bytes 61448 | tf_op jit(solution)/shard_map/ppermute | solution.py:563
  15.1 0.0 collective-permute-done.10.refs_4_
  15.1 0.1 shard_map.66
  15.2 1.6 %collective-permute-start.11 = (f32[5,2,32,128]{3,2,1,0:T(8,128)S(1)}, f32[5,2,32,128]{3,2,1,0:T(8,128)S(1)}, u32[]{:S(2)}, u32[]{:S(2)}) collective-permute-start(f32[5,2,32,128]{3,2,1,0:T(8,128)S(1)} %get-tuple-element.54), channel_id=1, source_target_pairs={{0,4},{2,6},{4,0},{6,2},{1,5},{3,7},{5,1},{7,3},{8,12},{10,14},{12... | collective-permute-start | bytes 491528 | tf_op jit(solution)/shard_map/ppermute | solution.py:563
  16.8 0.0 collective-permute-done.2.refs_4_.refs_2_
  16.8 0.2 shard_map.62
  16.9 0.6 %collective-permute-start.3 = (f32[5,4,8,128]{3,2,1,0:T(8,128)S(1)}, f32[5,4,8,128]{3,2,1,0:T(8,128)S(1)}, u32[]{:S(2)}, u32[]{:S(2)}) collective-permute-start(f32[5,4,8,128]{3,2,1,0:T(8,128)S(1)} %get-tuple-element.44), channel_id=1, source_target_pairs={{0,16},{8,24},{16,0},{24,8},{1,17},{9,25},{17,1},{25,9},{2,18},{10... | collective-permute-start | bytes 245768 | tf_op jit(solution)/shard_map/ppermute | solution.py:563
  17.6 2.0 %collective-permute-start.4 = (f32[5,4,8,128]{3,2,1,0:T(8,128)S(1)}, f32[5,4,8,128]{3,2,1,0:T(8,128)S(1)}, u32[]{:S(2)}, u32[]{:S(2)}) collective-permute-start(f32[5,4,8,128]{3,2,1,0:T(8,128)S(1)} %get-tuple-element.46), channel_id=1, source_target_pairs={{0,8},{8,0},{16,24},{24,16},{1,9},{9,1},{17,25},{25,17},{2,10},{10... | collective-permute-start | bytes 245768 | tf_op jit(solution)/shard_map/ppermute | solution.py:563
  19.6 0.1 shard_map.64.refs_7_
  19.7 0.1 collective-permute-start.8
  19.8 1.6 %collective-permute-start.7 = (f32[5,8,128]{2,1,0:T(8,128)S(1)}, f32[5,8,128]{2,1,0:T(8,128)S(1)}, u32[]{:S(2)}, u32[]{:S(2)}) collective-permute-start(f32[5,8,128]{2,1,0:T(8,128)S(1)} %shard_map.64.refs_7_), channel_id=1, source_target_pairs={{0,4},{2,6},{4,0},{6,2},{1,5},{3,7},{5,1},{7,3},{8,12},{10,14},{12... | collective-permute-start | bytes 61448 | tf_op jit(solution)/shard_map/ppermute | solution.py:563
  21.3 0.3 %collective-permute-start.6 = (f32[5,8,128]{2,1,0:T(8,128)S(1)}, f32[5,8,128]{2,1,0:T(8,128)S(1)}, u32[]{:S(2)}, u32[]{:S(2)}) collective-permute-start(f32[5,8,128]{2,1,0:T(8,128)S(1)} %shard_map.64.refs_7_), channel_id=1, source_target_pairs={{0,2},{2,0},{4,6},{6,4},{1,3},{3,1},{5,7},{7,5},{8,10},{10,8},{12,... | collective-permute-start | bytes 61448 | tf_op jit(solution)/shard_map/ppermute | solution.py:563
  21.6 1.2 %shard_map.67 = f32[2560,128]{1,0:T(8,128)S(1)} custom-call(f32[5,6,16,128]{3,2,1,0:T(8,128)S(1)} %get-tuple-element.32.rad_ref.refs_2_, f32[5,2,32,128]{3,2,1,0:T(8,128)S(1)} %get-tuple-element.53.refs_0_, f32[5,2,32,128]{3,2,1,0:T(8,128)S(1)} %collective-permute-done.11.refs_1_, f32[2560,128]{1,0:T(8,128)S(1)} %bitcast.8, ...), custom_call_target="tpu_custom_call" | custom-call | tf_op jit(solution)/shard_map/pallas_call | solution.py:14
  22.8 0.3 %collective-permute-done.8.refs_10_ = f32[5,8,128]{2,1,0:T(8,128)S(1)} collective-permute-done((f32[5,8,128]{2,1,0:T(8,128)S(1)}, f32[5,8,128]{2,1,0:T(8,128)S(1)}, u32[]{:S(2)}, u32[]{:S(2)}) %collective-permute-start.8) | collective-permute-done | bytes 20512 | tf_op jit(solution)/shard_map/ppermute | solution.py:563
  23.1 0.5 %collective-permute-done.7.refs_9_ = f32[5,8,128]{2,1,0:T(8,128)S(1)} collective-permute-done((f32[5,8,128]{2,1,0:T(8,128)S(1)}, f32[5,8,128]{2,1,0:T(8,128)S(1)}, u32[]{:S(2)}, u32[]{:S(2)}) %collective-permute-start.7) | collective-permute-done | bytes 20512 | tf_op jit(solution)/shard_map/ppermute | solution.py:563
  23.6 1.6 %shard_map.68 = f32[5,32,16,128]{3,2,1,0:T(8,128)} custom-call(f32[6,32,5,128]{3,2,1,0:T(8,128)S(1)} %get-tuple-element.30.coef_ref.refs_0_, f32[5,3,2,8,128]{4,3,2,1,0:T(8,128)S(1)} %get-tuple-element.31.refs_0_.refs_1_, f32[5,6,16,128]{3,2,1,0:T(8,128)S(1)} %get-tuple-element.32.rad_ref.refs_2_, f32[5,4,8,128]{3,2,1,0:T(8,128)S(1)} %get-tuple-element.43._.refs_3_, ...), custom_call_target="tpu_custom_call" | custom-call | tf_op jit(solution)/shard_map/pallas_call | solution.py:657
  (21 shorter events, 0.0 us)
Async XLA Ops:
  0.0 1.3 %copy-start = (f32[5,32,16,128]{3,2,1,0:T(8,128)S(1)}, f32[5,32,16,128]{3,2,1,0:T(8,128)}, u32[]{:S(2)}) copy-start(f32[5,32,16,128]{3,2,1,0:T(8,128)} %res_ref.3) | copy-start | bytes 3932164
  1.3 3.5 %copy-start.4 = (f32[4,5,128]{2,0,1:T(4,128)S(1)}, f32[4,5,128]{2,0,1:T(4,128)}, u32[]{:S(2)}) copy-start(f32[4,5,128]{2,0,1:T(4,128)} %param.8) | copy-start | bytes 30724
  1.3 3.5 %copy-start.5 = (f32[2,5,64]{2,0,1:T(2,128)S(1)}, f32[2,5,64]{2,0,1:T(2,128)}, u32[]{:S(2)}) copy-start(f32[2,5,64]{2,0,1:T(2,128)} %param.9) | copy-start | bytes 7684
  1.3 4.1 %copy-start.2 = (f32[5,5]{1,0:T(8,128)S(1)}, f32[5,5]{1,0:T(8,128)}, u32[]{:S(2)}) copy-start(f32[5,5]{1,0:T(8,128)} %vec_ref.1) | copy-start | bytes 304
  1.3 4.1 %copy-start.3 = (f32[5]{0:T(128)S(1)}, f32[5]{0:T(128)}, u32[]{:S(2)}) copy-start(f32[5]{0:T(128)} %dis_ref.1) | copy-start | bytes 64
  1.3 4.6 %copy-start.1 = (f32[5,32,16,128]{3,2,1,0:T(8,128)S(1)}, f32[5,32,16,128]{3,2,1,0:T(8,128)}, u32[]{:S(2)}) copy-start(f32[5,32,16,128]{3,2,1,0:T(8,128)} %res_ref.3) | copy-start | bytes 3932164
  1.8 6.7 %collective-permute-start = (f32[5,16,128]{2,1,0:T(8,128)S(1)}, f32[5,16,128]{2,1,0:T(8,128)S(1)}, u32[]{:S(2)}, u32[]{:S(2)}) collective-permute-start(f32[5,16,128]{2,1,0:T(8,128)S(1)} %shard_map.60), channel_id=1, source_target_pairs={{0,1},{1,0},{2,3},{3,2},{4,5},{5,4},{6,7},{7,6},{8,9},{9,8},{10,11... | collective-permute-start | bytes 122888 | tf_op jit(solution)/shard_map/ppermute | solution.py:563
  8.7 8.1 %collective-permute-start.2 = (f32[5,5,8,128]{3,2,1,0:T(8,128)S(1)}, f32[5,5,8,128]{3,2,1,0:T(8,128)S(1)}, u32[]{:S(2)}, u32[]{:S(2)}) collective-permute-start(f32[5,5,8,128]{3,2,1,0:T(8,128)S(1)} %get-tuple-element.42.refs_3_), channel_id=1, source_target_pairs={{0,16},{8,24},{16,0},{24,8},{1,17},{9,25},{17,1},{25,9},{2,18},{10... | collective-permute-start | bytes 307208 | tf_op jit(solution)/shard_map/ppermute | solution.py:563
  10.2 6.5 %collective-permute-start.1 = (f32[5,5,8,128]{3,2,1,0:T(8,128)S(1)}, f32[5,5,8,128]{3,2,1,0:T(8,128)S(1)}, u32[]{:S(2)}, u32[]{:S(2)}) collective-permute-start(f32[5,5,8,128]{3,2,1,0:T(8,128)S(1)} %get-tuple-element.41.refs_1_.refs_0_), channel_id=1, source_target_pairs={{0,8},{8,0},{16,24},{24,16},{1,9},{9,1},{17,25},{25,17},{2,10},{10... | collective-permute-start | bytes 307208 | tf_op jit(solution)/shard_map/ppermute | solution.py:563
  12.1 3.0 %collective-permute-start.9 = (f32[5,2,16,128]{3,2,1,0:T(8,128)S(1)}, f32[5,2,16,128]{3,2,1,0:T(8,128)S(1)}, u32[]{:S(2)}, u32[]{:S(2)}) collective-permute-start(f32[5,2,16,128]{3,2,1,0:T(8,128)S(1)} %get-tuple-element.51.refs_1_), channel_id=1, source_target_pairs={{0,2},{2,0},{4,6},{6,4},{1,3},{3,1},{5,7},{7,5},{8,10},{10,8},{12,... | collective-permute-start | bytes 245768 | tf_op jit(solution)/shard_map/ppermute | solution.py:563
  12.2 3.0 %collective-permute-start.10 = (f32[5,2,16,128]{3,2,1,0:T(8,128)S(1)}, f32[5,2,16,128]{3,2,1,0:T(8,128)S(1)}, u32[]{:S(2)}, u32[]{:S(2)}) collective-permute-start(f32[5,2,16,128]{3,2,1,0:T(8,128)S(1)} %get-tuple-element.52.refs_2_), channel_id=1, source_target_pairs={{0,2},{2,0},{4,6},{6,4},{1,3},{3,1},{5,7},{7,5},{8,10},{10,8},{12,... | collective-permute-start | bytes 245768 | tf_op jit(solution)/shard_map/ppermute | solution.py:563
  12.7 7.0 %collective-permute-start.5 = (f32[5,8,128]{2,1,0:T(8,128)S(1)}, f32[5,8,128]{2,1,0:T(8,128)S(1)}, u32[]{:S(2)}, u32[]{:S(2)}) collective-permute-start(f32[5,8,128]{2,1,0:T(8,128)S(1)} %get-tuple-element.48), channel_id=1, source_target_pairs={{0,24},{8,16},{16,8},{24,0},{1,25},{9,17},{17,9},{25,1},{2,26},{10... | collective-permute-start | bytes 61448 | tf_op jit(solution)/shard_map/ppermute | solution.py:563
  15.2 6.1 %collective-permute-start.11 = (f32[5,2,32,128]{3,2,1,0:T(8,128)S(1)}, f32[5,2,32,128]{3,2,1,0:T(8,128)S(1)}, u32[]{:S(2)}, u32[]{:S(2)}) collective-permute-start(f32[5,2,32,128]{3,2,1,0:T(8,128)S(1)} %get-tuple-element.54), channel_id=1, source_target_pairs={{0,4},{2,6},{4,0},{6,2},{1,5},{3,7},{5,1},{7,3},{8,12},{10,14},{12... | collective-permute-start | bytes 491528 | tf_op jit(solution)/shard_map/ppermute | solution.py:563
  16.9 6.7 %collective-permute-start.3 = (f32[5,4,8,128]{3,2,1,0:T(8,128)S(1)}, f32[5,4,8,128]{3,2,1,0:T(8,128)S(1)}, u32[]{:S(2)}, u32[]{:S(2)}) collective-permute-start(f32[5,4,8,128]{3,2,1,0:T(8,128)S(1)} %get-tuple-element.44), channel_id=1, source_target_pairs={{0,16},{8,24},{16,0},{24,8},{1,17},{9,25},{17,1},{25,9},{2,18},{10... | collective-permute-start | bytes 245768 | tf_op jit(solution)/shard_map/ppermute | solution.py:563
  17.6 6.0 %collective-permute-start.4 = (f32[5,4,8,128]{3,2,1,0:T(8,128)S(1)}, f32[5,4,8,128]{3,2,1,0:T(8,128)S(1)}, u32[]{:S(2)}, u32[]{:S(2)}) collective-permute-start(f32[5,4,8,128]{3,2,1,0:T(8,128)S(1)} %get-tuple-element.46), channel_id=1, source_target_pairs={{0,8},{8,0},{16,24},{24,16},{1,9},{9,1},{17,25},{25,17},{2,10},{10... | collective-permute-start | bytes 245768 | tf_op jit(solution)/shard_map/ppermute | solution.py:563
  19.7 3.4 %collective-permute-start.8 = (f32[5,8,128]{2,1,0:T(8,128)S(1)}, f32[5,8,128]{2,1,0:T(8,128)S(1)}, u32[]{:S(2)}, u32[]{:S(2)}) collective-permute-start(f32[5,8,128]{2,1,0:T(8,128)S(1)} %shard_map.64.refs_7_), channel_id=1, source_target_pairs={{0,6},{2,4},{4,2},{6,0},{1,7},{3,5},{5,3},{7,1},{8,14},{10,12},{12... | collective-permute-start | bytes 61448 | tf_op jit(solution)/shard_map/ppermute | solution.py:563
  19.8 3.8 %collective-permute-start.7 = (f32[5,8,128]{2,1,0:T(8,128)S(1)}, f32[5,8,128]{2,1,0:T(8,128)S(1)}, u32[]{:S(2)}, u32[]{:S(2)}) collective-permute-start(f32[5,8,128]{2,1,0:T(8,128)S(1)} %shard_map.64.refs_7_), channel_id=1, source_target_pairs={{0,4},{2,6},{4,0},{6,2},{1,5},{3,7},{5,1},{7,3},{8,12},{10,14},{12... | collective-permute-start | bytes 61448 | tf_op jit(solution)/shard_map/ppermute | solution.py:563
  21.3 2.3 %collective-permute-start.6 = (f32[5,8,128]{2,1,0:T(8,128)S(1)}, f32[5,8,128]{2,1,0:T(8,128)S(1)}, u32[]{:S(2)}, u32[]{:S(2)}) collective-permute-start(f32[5,8,128]{2,1,0:T(8,128)S(1)} %shard_map.64.refs_7_), channel_id=1, source_target_pairs={{0,2},{2,0},{4,6},{6,4},{1,3},{3,1},{5,7},{7,5},{8,10},{10,8},{12,... | collective-permute-start | bytes 61448 | tf_op jit(solution)/shard_map/ppermute | solution.py:563

commit v8 on v7

--- a/solution.py
+++ b/solution.py
@@ -72,7 +72,7 @@
             out.append((z, one))
         return tuple(out)
 
-    return lax.fori_loop(0, cells, step, start, unroll=8)
+    return lax.fori_loop(0, cells, step, start, unroll=cells)
 
 
 def upper_sweep(coef_ref, cells, z_ref, start, store=None, first=0, count=None):

time: 25.4 us -> 25.3 us (level)
  transfers between devices with their start and end apart: 12 -> 12, of which waited for: 2 -> 2; matrix products, arithmetic and copies ran while one was open for 1% -> 1% of each run, Pallas kernels for 21% -> 20%
where the time goes in v8:
time: 25.3 us; the launch traced here: 25.1 us
  starting transfers between devices  15.3 us (60%)
  Pallas kernels  7.32 us (29%)
  local copies, waits for them, and re-layouts  1.56 us (6%)
  waiting for transfers between devices  0.79 us (3%)
    ppermute x12, starting transfers between devices, from_partner(): lax.ppermute(values, axis, [(i, i ^ step) for i in range(lax.axis_size(ax...  15.3 us
    pallas_call x13, Pallas kernels, call(): pl.pallas_call(body, out_shape=[jax.ShapeDtypeStruct(shape, f32) for shap...  5.72 us
    pallas_call x1, Pallas kernels, local(): pl.pallas_call(lambda *refs: last_kernel(len(far), len(near), *refs), out...  1.6 us
    unnamed x13, local copies, waits for them, and re-layouts  1.34 us
    ppermute x12, waiting for transfers between devices, from_partner(): lax.ppermute(values, axis, [(i, i ^ step) for i in range(lax.axis_size(ax...  0.79 us
  transfers between devices with their start and end apart: 12, of which 2 were waited for; matrix products, arithmetic and copies ran while one was open for 1% of the time, Pallas kernels for 20%

profile of v8, /device:TPU:0, one launch (start us, length us, event | category | flops | bytes accessed | tf_op | source)
XLA Modules:
  0.0 25.1 jit_solution(4124381110765187263)
XLA Ops:
  0.0 1.3 %copy-done = f32[5,32,16,128]{3,2,1,0:T(8,128)S(1)} copy-done((f32[5,32,16,128]{3,2,1,0:T(8,128)S(1)}, f32[5,32,16,128]{3,2,1,0:T(8,128)}, u32[]{:S(2)}) %copy-start) | copy-done | bytes 1310744
  1.3 0.4 %shard_map.60 = f32[5,16,128]{2,1,0:T(8,128)S(1)} custom-call(f32[5,32,16,128]{3,2,1,0:T(8,128)S(1)} %copy-done), custom_call_target="tpu_custom_call" | custom-call | tf_op jit(solution)/shard_map/pallas_call | solution.py:14
  1.8 3.0 %collective-permute-start = (f32[5,16,128]{2,1,0:T(8,128)S(1)}, f32[5,16,128]{2,1,0:T(8,128)S(1)}, u32[]{:S(2)}, u32[]{:S(2)}) collective-permute-start(f32[5,16,128]{2,1,0:T(8,128)S(1)} %shard_map.60), channel_id=1, source_target_pairs={{0,1},{1,0},{2,3},{3,2},{4,5},{5,4},{6,7},{7,6},{8,9},{9,8},{10,11... | collective-permute-start | bytes 122888 | tf_op jit(solution)/shard_map/ppermute | solution.py:563
  4.8 0.1 reshape.12
  4.9 0.1 copy.13
  5.0 0.4 %shard_map.56 = (f32[5,6,16,128]{3,2,1,0:T(8,128)S(1)}, f32[5,3,2,8,128]{4,3,2,1,0:T(8,128)S(1)}) custom-call(f32[2,16,4,5]{3,2,1,0:T(4,128)S(1)} %bitcast.11), custom_call_target="tpu_custom_call" | custom-call | tf_op jit(solution)/shard_map/pallas_call | solution.py:14
  5.4 0.5 %shard_map.55 = (f32[6,32,5,128]{3,2,1,0:T(8,128)S(1)}, f32[4,5,128]{2,1,0:T(8,128)S(1)}, f32[7,5,128]{2,1,0:T(8,128)S(1)}) custom-call(f32[4,5,128]{2,1,0:T(8,128)S(1)} %copy.12.coef_ref, f32[5,5]{1,0:T(8,128)S(1)} %copy-done.2, f32[5]{0:T(128)S(1)} %copy-done.3), custom_call_target="tpu_custom_call" | custom-call | tf_op jit(solution)/shard_map/pallas_call | solution.py:14
  6.0 1.3 %shard_map.57 = (f32[5,32,16,128]{3,2,1,0:T(8,128)S(1)}, f32[5,4,16,128]{3,2,1,0:T(8,128)S(1)}) custom-call(f32[6,32,5,128]{3,2,1,0:T(8,128)S(1)} %get-tuple-element.30.coef_ref.refs_0_, f32[7,5,128]{2,1,0:T(8,128)S(1)} %get-tuple-element.33.mix_ref, f32[5,32,16,128]{3,2,1,0:T(8,128)S(1)} %copy-done.1), custom_call_target="tpu_custom_call" | custom-call | tf_op jit(solution)/shard_map/pallas_call | solution.py:14
  7.2 1.1 %shard_map.58 = (f32[5,3,4,16,128]{4,3,2,1,0:T(8,128)S(1)}, f32[640,128]{1,0:T(8,128)S(1)}, f32[5,2,32,128]{3,2,1,0:T(8,128)S(1)}) custom-call(f32[4,5,128]{2,1,0:T(8,128)S(1)} %copy.12.coef_ref, f32[5,6,16,128]{3,2,1,0:T(8,128)S(1)} %get-tuple-element.32.rad_ref.refs_2_, f32[2560,128]{1,0:T(8,128)S(1)} %bitcast.6), custom_call_target="tpu_custom_call" | custom-call | tf_op jit(solution)/shard_map/pallas_call | solution.py:14
  8.4 0.0 collective-permute-done.halo_ref
  8.4 0.2 shard_map.61
  8.6 1.5 %collective-permute-start.2 = (f32[5,5,8,128]{3,2,1,0:T(8,128)S(1)}, f32[5,5,8,128]{3,2,1,0:T(8,128)S(1)}, u32[]{:S(2)}, u32[]{:S(2)}) collective-permute-start(f32[5,5,8,128]{3,2,1,0:T(8,128)S(1)} %get-tuple-element.42.refs_3_), channel_id=1, source_target_pairs={{0,16},{8,24},{16,0},{24,8},{1,17},{9,25},{17,1},{25,9},{2,18},{10... | collective-permute-start | bytes 307208 | tf_op jit(solution)/shard_map/ppermute | solution.py:563
  10.1 1.6 %collective-permute-start.1 = (f32[5,5,8,128]{3,2,1,0:T(8,128)S(1)}, f32[5,5,8,128]{3,2,1,0:T(8,128)S(1)}, u32[]{:S(2)}, u32[]{:S(2)}) collective-permute-start(f32[5,5,8,128]{3,2,1,0:T(8,128)S(1)} %get-tuple-element.41.refs_1_.refs_0_), channel_id=1, source_target_pairs={{0,8},{8,0},{16,24},{24,16},{1,9},{9,1},{17,25},{25,17},{2,10},{10... | collective-permute-start | bytes 307208 | tf_op jit(solution)/shard_map/ppermute | solution.py:563
  11.7 0.3 %shard_map.65 = (f32[5,2,16,128]{3,2,1,0:T(8,128)S(1)}, f32[5,2,16,128]{3,2,1,0:T(8,128)S(1)}) custom-call(f32[5,6,16,128]{3,2,1,0:T(8,128)S(1)} %get-tuple-element.32.rad_ref.refs_2_, f32[5,16,128]{2,1,0:T(8,128)S(1)} %get-tuple-element.49.part_ref.refs_3_, f32[5,2,32,128]{3,2,1,0:T(8,128)S(1)} %get-tuple-element.50.known_ref), custom_call_target="tpu_custom_call" | custom-call | tf_op jit(solution)/shard_map/pallas_call | solution.py:14
  12.0 0.1 collective-permute-start.9
  12.1 0.5 %collective-permute-start.10 = (f32[5,2,16,128]{3,2,1,0:T(8,128)S(1)}, f32[5,2,16,128]{3,2,1,0:T(8,128)S(1)}, u32[]{:S(2)}, u32[]{:S(2)}) collective-permute-start(f32[5,2,16,128]{3,2,1,0:T(8,128)S(1)} %get-tuple-element.52.refs_2_), channel_id=1, source_target_pairs={{0,2},{2,0},{4,6},{6,4},{1,3},{3,1},{5,7},{7,5},{8,10},{10,8},{12,... | collective-permute-start | bytes 245768 | tf_op jit(solution)/shard_map/ppermute | solution.py:563
  12.5 2.4 %collective-permute-start.5 = (f32[5,8,128]{2,1,0:T(8,128)S(1)}, f32[5,8,128]{2,1,0:T(8,128)S(1)}, u32[]{:S(2)}, u32[]{:S(2)}) collective-permute-start(f32[5,8,128]{2,1,0:T(8,128)S(1)} %get-tuple-element.48), channel_id=1, source_target_pairs={{0,24},{8,16},{16,8},{24,0},{1,25},{9,17},{17,9},{25,1},{2,26},{10... | collective-permute-start | bytes 61448 | tf_op jit(solution)/shard_map/ppermute | solution.py:563
  15.0 0.1 shard_map.66
  15.1 1.6 %collective-permute-start.11 = (f32[5,2,32,128]{3,2,1,0:T(8,128)S(1)}, f32[5,2,32,128]{3,2,1,0:T(8,128)S(1)}, u32[]{:S(2)}, u32[]{:S(2)}) collective-permute-start(f32[5,2,32,128]{3,2,1,0:T(8,128)S(1)} %get-tuple-element.54), channel_id=1, source_target_pairs={{0,4},{2,6},{4,0},{6,2},{1,5},{3,7},{5,1},{7,3},{8,12},{10,14},{12... | collective-permute-start | bytes 491528 | tf_op jit(solution)/shard_map/ppermute | solution.py:563
  16.7 0.0 collective-permute-done.2.refs_4_.refs_2_
  16.7 0.0 collective-permute-done.1.refs_2_.refs_1_
  16.7 0.2 shard_map.62
  16.8 0.6 %collective-permute-start.3 = (f32[5,4,8,128]{3,2,1,0:T(8,128)S(1)}, f32[5,4,8,128]{3,2,1,0:T(8,128)S(1)}, u32[]{:S(2)}, u32[]{:S(2)}) collective-permute-start(f32[5,4,8,128]{3,2,1,0:T(8,128)S(1)} %get-tuple-element.44), channel_id=1, source_target_pairs={{0,16},{8,24},{16,0},{24,8},{1,17},{9,25},{17,1},{25,9},{2,18},{10... | collective-permute-start | bytes 245768 | tf_op jit(solution)/shard_map/ppermute | solution.py:563
  17.5 2.0 %collective-permute-start.4 = (f32[5,4,8,128]{3,2,1,0:T(8,128)S(1)}, f32[5,4,8,128]{3,2,1,0:T(8,128)S(1)}, u32[]{:S(2)}, u32[]{:S(2)}) collective-permute-start(f32[5,4,8,128]{3,2,1,0:T(8,128)S(1)} %get-tuple-element.46), channel_id=1, source_target_pairs={{0,8},{8,0},{16,24},{24,16},{1,9},{9,1},{17,25},{25,17},{2,10},{10... | collective-permute-start | bytes 245768 | tf_op jit(solution)/shard_map/ppermute | solution.py:563
  19.5 0.1 shard_map.64.refs_7_
  19.6 0.1 collective-permute-start.8
  19.6 1.6 %collective-permute-start.7 = (f32[5,8,128]{2,1,0:T(8,128)S(1)}, f32[5,8,128]{2,1,0:T(8,128)S(1)}, u32[]{:S(2)}, u32[]{:S(2)}) collective-permute-start(f32[5,8,128]{2,1,0:T(8,128)S(1)} %shard_map.64.refs_7_), channel_id=1, source_target_pairs={{0,4},{2,6},{4,0},{6,2},{1,5},{3,7},{5,1},{7,3},{8,12},{10,14},{12... | collective-permute-start | bytes 61448 | tf_op jit(solution)/shard_map/ppermute | solution.py:563
  21.2 0.3 %collective-permute-start.6 = (f32[5,8,128]{2,1,0:T(8,128)S(1)}, f32[5,8,128]{2,1,0:T(8,128)S(1)}, u32[]{:S(2)}, u32[]{:S(2)}) collective-permute-start(f32[5,8,128]{2,1,0:T(8,128)S(1)} %shard_map.64.refs_7_), channel_id=1, source_target_pairs={{0,2},{2,0},{4,6},{6,4},{1,3},{3,1},{5,7},{7,5},{8,10},{10,8},{12,... | collective-permute-start | bytes 61448 | tf_op jit(solution)/shard_map/ppermute | solution.py:563
  21.5 1.2 %shard_map.67 = f32[2560,128]{1,0:T(8,128)S(1)} custom-call(f32[5,6,16,128]{3,2,1,0:T(8,128)S(1)} %get-tuple-element.32.rad_ref.refs_2_, f32[5,2,32,128]{3,2,1,0:T(8,128)S(1)} %get-tuple-element.53.refs_0_, f32[5,2,32,128]{3,2,1,0:T(8,128)S(1)} %collective-permute-done.11.refs_1_, f32[2560,128]{1,0:T(8,128)S(1)} %bitcast.8, ...), custom_call_target="tpu_custom_call" | custom-call | tf_op jit(solution)/shard_map/pallas_call | solution.py:14
  22.7 0.3 %collective-permute-done.8.refs_10_ = f32[5,8,128]{2,1,0:T(8,128)S(1)} collective-permute-done((f32[5,8,128]{2,1,0:T(8,128)S(1)}, f32[5,8,128]{2,1,0:T(8,128)S(1)}, u32[]{:S(2)}, u32[]{:S(2)}) %collective-permute-start.8) | collective-permute-done | bytes 20512 | tf_op jit(solution)/shard_map/ppermute | solution.py:563
  23.0 0.5 %collective-permute-done.7.refs_9_ = f32[5,8,128]{2,1,0:T(8,128)S(1)} collective-permute-done((f32[5,8,128]{2,1,0:T(8,128)S(1)}, f32[5,8,128]{2,1,0:T(8,128)S(1)}, u32[]{:S(2)}, u32[]{:S(2)}) %collective-permute-start.7) | collective-permute-done | bytes 20512 | tf_op jit(solution)/shard_map/ppermute | solution.py:563
  23.5 1.6 %shard_map.68 = f32[5,32,16,128]{3,2,1,0:T(8,128)} custom-call(f32[6,32,5,128]{3,2,1,0:T(8,128)S(1)} %get-tuple-element.30.coef_ref.refs_0_, f32[5,3,2,8,128]{4,3,2,1,0:T(8,128)S(1)} %get-tuple-element.31.refs_0_.refs_1_, f32[5,6,16,128]{3,2,1,0:T(8,128)S(1)} %get-tuple-element.32.rad_ref.refs_2_, f32[5,4,8,128]{3,2,1,0:T(8,128)S(1)} %get-tuple-element.43._.refs_3_, ...), custom_call_target="tpu_custom_call" | custom-call | tf_op jit(solution)/shard_map/pallas_call | solution.py:657
  (21 shorter events, 0.0 us)
Async XLA Ops:
  0.0 1.3 %copy-start = (f32[5,32,16,128]{3,2,1,0:T(8,128)S(1)}, f32[5,32,16,128]{3,2,1,0:T(8,128)}, u32[]{:S(2)}) copy-start(f32[5,32,16,128]{3,2,1,0:T(8,128)} %res_ref.3) | copy-start | bytes 3932164
  1.3 3.5 %copy-start.4 = (f32[4,5,128]{2,0,1:T(4,128)S(1)}, f32[4,5,128]{2,0,1:T(4,128)}, u32[]{:S(2)}) copy-start(f32[4,5,128]{2,0,1:T(4,128)} %param.8) | copy-start | bytes 30724
  1.3 3.5 %copy-start.5 = (f32[2,5,64]{2,0,1:T(2,128)S(1)}, f32[2,5,64]{2,0,1:T(2,128)}, u32[]{:S(2)}) copy-start(f32[2,5,64]{2,0,1:T(2,128)} %param.9) | copy-start | bytes 7684
  1.3 4.1 %copy-start.2 = (f32[5,5]{1,0:T(8,128)S(1)}, f32[5,5]{1,0:T(8,128)}, u32[]{:S(2)}) copy-start(f32[5,5]{1,0:T(8,128)} %vec_ref.1) | copy-start | bytes 304
  1.3 4.1 %copy-start.3 = (f32[5]{0:T(128)S(1)}, f32[5]{0:T(128)}, u32[]{:S(2)}) copy-start(f32[5]{0:T(128)} %dis_ref.1) | copy-start | bytes 64
  1.3 4.6 %copy-start.1 = (f32[5,32,16,128]{3,2,1,0:T(8,128)S(1)}, f32[5,32,16,128]{3,2,1,0:T(8,128)}, u32[]{:S(2)}) copy-start(f32[5,32,16,128]{3,2,1,0:T(8,128)} %res_ref.3) | copy-start | bytes 3932164
  1.8 6.6 %collective-permute-start = (f32[5,16,128]{2,1,0:T(8,128)S(1)}, f32[5,16,128]{2,1,0:T(8,128)S(1)}, u32[]{:S(2)}, u32[]{:S(2)}) collective-permute-start(f32[5,16,128]{2,1,0:T(8,128)S(1)} %shard_map.60), channel_id=1, source_target_pairs={{0,1},{1,0},{2,3},{3,2},{4,5},{5,4},{6,7},{7,6},{8,9},{9,8},{10,11... | collective-permute-start | bytes 122888 | tf_op jit(solution)/shard_map/ppermute | solution.py:563
  8.6 8.1 %collective-permute-start.2 = (f32[5,5,8,128]{3,2,1,0:T(8,128)S(1)}, f32[5,5,8,128]{3,2,1,0:T(8,128)S(1)}, u32[]{:S(2)}, u32[]{:S(2)}) collective-permute-start(f32[5,5,8,128]{3,2,1,0:T(8,128)S(1)} %get-tuple-element.42.refs_3_), channel_id=1, source_target_pairs={{0,16},{8,24},{16,0},{24,8},{1,17},{9,25},{17,1},{25,9},{2,18},{10... | collective-permute-start | bytes 307208 | tf_op jit(solution)/shard_map/ppermute | solution.py:563
  10.1 6.5 %collective-permute-start.1 = (f32[5,5,8,128]{3,2,1,0:T(8,128)S(1)}, f32[5,5,8,128]{3,2,1,0:T(8,128)S(1)}, u32[]{:S(2)}, u32[]{:S(2)}) collective-permute-start(f32[5,5,8,128]{3,2,1,0:T(8,128)S(1)} %get-tuple-element.41.refs_1_.refs_0_), channel_id=1, source_target_pairs={{0,8},{8,0},{16,24},{24,16},{1,9},{9,1},{17,25},{25,17},{2,10},{10... | collective-permute-start | bytes 307208 | tf_op jit(solution)/shard_map/ppermute | solution.py:563
  12.0 3.0 %collective-permute-start.9 = (f32[5,2,16,128]{3,2,1,0:T(8,128)S(1)}, f32[5,2,16,128]{3,2,1,0:T(8,128)S(1)}, u32[]{:S(2)}, u32[]{:S(2)}) collective-permute-start(f32[5,2,16,128]{3,2,1,0:T(8,128)S(1)} %get-tuple-element.51.refs_1_), channel_id=1, source_target_pairs={{0,2},{2,0},{4,6},{6,4},{1,3},{3,1},{5,7},{7,5},{8,10},{10,8},{12,... | collective-permute-start | bytes 245768 | tf_op jit(solution)/shard_map/ppermute | solution.py:563
  12.1 3.0 %collective-permute-start.10 = (f32[5,2,16,128]{3,2,1,0:T(8,128)S(1)}, f32[5,2,16,128]{3,2,1,0:T(8,128)S(1)}, u32[]{:S(2)}, u32[]{:S(2)}) collective-permute-start(f32[5,2,16,128]{3,2,1,0:T(8,128)S(1)} %get-tuple-element.52.refs_2_), channel_id=1, source_target_pairs={{0,2},{2,0},{4,6},{6,4},{1,3},{3,1},{5,7},{7,5},{8,10},{10,8},{12,... | collective-permute-start | bytes 245768 | tf_op jit(solution)/shard_map/ppermute | solution.py:563
  12.5 7.0 %collective-permute-start.5 = (f32[5,8,128]{2,1,0:T(8,128)S(1)}, f32[5,8,128]{2,1,0:T(8,128)S(1)}, u32[]{:S(2)}, u32[]{:S(2)}) collective-permute-start(f32[5,8,128]{2,1,0:T(8,128)S(1)} %get-tuple-element.48), channel_id=1, source_target_pairs={{0,24},{8,16},{16,8},{24,0},{1,25},{9,17},{17,9},{25,1},{2,26},{10... | collective-permute-start | bytes 61448 | tf_op jit(solution)/shard_map/ppermute | solution.py:563
  15.1 6.1 %collective-permute-start.11 = (f32[5,2,32,128]{3,2,1,0:T(8,128)S(1)}, f32[5,2,32,128]{3,2,1,0:T(8,128)S(1)}, u32[]{:S(2)}, u32[]{:S(2)}) collective-permute-start(f32[5,2,32,128]{3,2,1,0:T(8,128)S(1)} %get-tuple-element.54), channel_id=1, source_target_pairs={{0,4},{2,6},{4,0},{6,2},{1,5},{3,7},{5,1},{7,3},{8,12},{10,14},{12... | collective-permute-start | bytes 491528 | tf_op jit(solution)/shard_map/ppermute | solution.py:563
  16.8 6.7 %collective-permute-start.3 = (f32[5,4,8,128]{3,2,1,0:T(8,128)S(1)}, f32[5,4,8,128]{3,2,1,0:T(8,128)S(1)}, u32[]{:S(2)}, u32[]{:S(2)}) collective-permute-start(f32[5,4,8,128]{3,2,1,0:T(8,128)S(1)} %get-tuple-element.44), channel_id=1, source_target_pairs={{0,16},{8,24},{16,0},{24,8},{1,17},{9,25},{17,1},{25,9},{2,18},{10... | collective-permute-start | bytes 245768 | tf_op jit(solution)/shard_map/ppermute | solution.py:563
  17.5 6.0 %collective-permute-start.4 = (f32[5,4,8,128]{3,2,1,0:T(8,128)S(1)}, f32[5,4,8,128]{3,2,1,0:T(8,128)S(1)}, u32[]{:S(2)}, u32[]{:S(2)}) collective-permute-start(f32[5,4,8,128]{3,2,1,0:T(8,128)S(1)} %get-tuple-element.46), channel_id=1, source_target_pairs={{0,8},{8,0},{16,24},{24,16},{1,9},{9,1},{17,25},{25,17},{2,10},{10... | collective-permute-start | bytes 245768 | tf_op jit(solution)/shard_map/ppermute | solution.py:563
  19.6 3.4 %collective-permute-start.8 = (f32[5,8,128]{2,1,0:T(8,128)S(1)}, f32[5,8,128]{2,1,0:T(8,128)S(1)}, u32[]{:S(2)}, u32[]{:S(2)}) collective-permute-start(f32[5,8,128]{2,1,0:T(8,128)S(1)} %shard_map.64.refs_7_), channel_id=1, source_target_pairs={{0,6},{2,4},{4,2},{6,0},{1,7},{3,5},{5,3},{7,1},{8,14},{10,12},{12... | collective-permute-start | bytes 61448 | tf_op jit(solution)/shard_map/ppermute | solution.py:563
  19.6 3.8 %collective-permute-start.7 = (f32[5,8,128]{2,1,0:T(8,128)S(1)}, f32[5,8,128]{2,1,0:T(8,128)S(1)}, u32[]{:S(2)}, u32[]{:S(2)}) collective-permute-start(f32[5,8,128]{2,1,0:T(8,128)S(1)} %shard_map.64.refs_7_), channel_id=1, source_target_pairs={{0,4},{2,6},{4,0},{6,2},{1,5},{3,7},{5,1},{7,3},{8,12},{10,14},{12... | collective-permute-start | bytes 61448 | tf_op jit(solution)/shard_map/ppermute | solution.py:563
  21.2 2.3 %collective-permute-start.6 = (f32[5,8,128]{2,1,0:T(8,128)S(1)}, f32[5,8,128]{2,1,0:T(8,128)S(1)}, u32[]{:S(2)}, u32[]{:S(2)}) collective-permute-start(f32[5,8,128]{2,1,0:T(8,128)S(1)} %shard_map.64.refs_7_), channel_id=1, source_target_pairs={{0,2},{2,0},{4,6},{6,4},{1,3},{3,1},{5,7},{7,5},{8,10},{10,8},{12,... | collective-permute-start | bytes 61448 | tf_op jit(solution)/shard_map/ppermute | solution.py:563
